TPU v7x, 32 devices: a whole 2x2x4 slice. The times are simulated.
32 devices in a mesh: section: 2 (over core), shard: 4 (over y, x), dp: 4 (over z).
Axes of the slice: x: 2, y: 2, z: 4, core: 2. Of those that a mesh axis runs over, the one named last changes fastest.
Arguments:
- ends_in: bfloat16 [2, 2048, 2048], P('section', ('shard', 'dp')), may hold values from -6 to 6
- in_weight: bfloat16 [2, 2048, 19456], P('section', 'shard'), may hold values from -0.125 to 0.125
- out_weight: bfloat16 [2, 2048, 10240], P('section', 'shard')
- norm_gain: float32 [2, 2, 2048], P('section'), may hold values from 0.5 to 1.5
- seq_len: int32 [32], P(('shard', 'dp')), may hold values from 1 to 64, as said below
Outputs:
- ends_out: bfloat16 [2, 2048, 2048], P('section', ('shard', 'dp'))
- in_grad: float32 [2, 2048, 19456], P('section', ('shard', 'dp'))
- out_grad: float32 [2, 2048, 10240], P('section', ('shard', 'dp'))
- gain_grad: float32 [2, 2, 2048], P('section', None, ('shard', 'dp'))
Inputs may be any that keep to these rules, and one draw needn't show every extreme that they name: `seq_len`: each value is the live length of one slot of 64 positions; lengths differ from slot to slot and from device to device, and some slot is full in every draw.
All inputs are finite; a program needn't handle non-finite values.
Results may differ from a plain program's by a relative error of at most 0.02.
Values may be sent and summed in bfloat16 or wider, within the bound.
A program may use at most 960 MiB of HBM per device.

v0:
```python
import jax
import jax.numpy as jnp
from jax import lax
from jax.sharding import PartitionSpec as P

HEADS = 32
KV_HEADS = 8
HEAD_DIM = 64
FF = 8192


EPSILON = 1e-05
CONTRACT_ROWS = (((0,), (0,)), ((), ()))
CONTRACT_LAST = (((1,), (1,)), ((), ()))


def from_behind(value, axis, by):
    peers = lax.axis_size(axis)
    pairs = [(i, i + by) for i in range(peers) if 0 <= i + by < peers]
    return lax.ppermute(value, axis, pairs)


def rope_tables(length_rows):
    half_dim = HEAD_DIM // 2
    inverse = 500000.0 ** (-(jnp.arange(half_dim, dtype=jnp.float32) * 2.0 / HEAD_DIM))
    angles = jnp.arange(length_rows, dtype=jnp.float32)[:, None] * inverse[None, :]
    return (jnp.cos(angles)[:, None, :], jnp.sin(angles)[:, None, :])


def rotate(values, cosine, sine):
    half_dim = HEAD_DIM // 2
    first_half = values[..., :half_dim]
    second_half = values[..., half_dim:]
    return jnp.concatenate(
        [first_half * cosine - second_half * sine, second_half * cosine + first_half * sine], -1
    )


def unrotate(grads, cosine, sine):
    half_dim = HEAD_DIM // 2
    first_half = grads[..., :half_dim]
    second_half = grads[..., half_dim:]
    return jnp.concatenate(
        [first_half * cosine + second_half * sine, second_half * cosine - first_half * sine], -1
    )


def rms_scale(values):
    return lax.rsqrt(jnp.mean(values * values, -1, keepdims=True) + EPSILON)


def rms_back(values, scale, gain_row, grad_norm):
    grad_hat = grad_norm * gain_row
    grad_gain = jnp.sum(grad_norm * values * scale, 0)
    inner = jnp.mean(grad_hat * values, -1, keepdims=True)
    return (scale * grad_hat - values * scale * scale * scale * inner, grad_gain)


def allowed_keys(length_rows, seq_length):
    places = jnp.arange(length_rows)
    return (places[:, None] >= places[None, :]) & (places[None, :] < seq_length)


def score_block(queries, keys_rot, allowed):
    grouped = queries.reshape(queries.shape[0], KV_HEADS, HEADS // KV_HEADS, HEAD_DIM)
    scores = jnp.einsum(
        "qkgd,pkd->kgqp", grouped, keys_rot, preferred_element_type=jnp.float32
    ) * HEAD_DIM ** (-0.5)
    return (jnp.where(allowed[None, None], scores, -1e30), grouped)


def split_weights(full_in, full_out):
    q_width = HEADS * HEAD_DIM
    qkv_width = q_width + 2 * KV_HEADS * HEAD_DIM
    w_in = full_in[0]
    w_out = full_out[0]
    return (w_in[:, :qkv_width], w_in[:, qkv_width:], w_out[:, :q_width], w_out[:, q_width:])


def forward_layer(block_in, seq_length, weight_parts, gain_pair, cosine, sine):
    w_qkv, w_gate_up, w_attn, w_down = weight_parts
    q_width = HEADS * HEAD_DIM
    kv_width = KV_HEADS * HEAD_DIM
    length_rows = block_in.shape[0]
    values = block_in.astype(jnp.float32)
    scale_one = rms_scale(values)
    normed = (values * scale_one * gain_pair[0]).astype(jnp.bfloat16)
    projected = jnp.dot(normed, w_qkv, preferred_element_type=jnp.float32)
    queries = rotate(
        projected[:, :q_width].reshape(length_rows, HEADS, HEAD_DIM), cosine, sine
    ).astype(jnp.bfloat16)
    keys_rot = rotate(
        projected[:, q_width : q_width + kv_width].reshape(length_rows, KV_HEADS, HEAD_DIM),
        cosine,
        sine,
    ).astype(jnp.bfloat16)
    values_kv = (
        projected[:, q_width + kv_width :]
        .reshape(length_rows, KV_HEADS, HEAD_DIM)
        .astype(jnp.bfloat16)
    )
    allowed = allowed_keys(length_rows, seq_length)
    scores, grouped = score_block(queries, keys_rot, allowed)
    row_top = jnp.max(scores, -1, keepdims=True)
    exp_terms = jnp.exp(scores - row_top)
    row_total = jnp.sum(exp_terms, -1, keepdims=True)
    log_total = row_top + jnp.log(row_total)
    weights_low = (exp_terms / row_total).astype(jnp.bfloat16)
    context = jnp.einsum(
        "kgqp,pkd->qkgd", weights_low, values_kv, preferred_element_type=jnp.float32
    )
    context = context.reshape(length_rows, q_width).astype(jnp.bfloat16)
    middle = values + lax.dot_general(
        context, w_attn, CONTRACT_LAST, preferred_element_type=jnp.float32
    )
    scale_two = rms_scale(middle)
    normed_two = (middle * scale_two * gain_pair[1]).astype(jnp.bfloat16)
    gate_up = jnp.dot(normed_two, w_gate_up, preferred_element_type=jnp.float32)
    gate_act = gate_up[:, :FF]
    upward = gate_up[:, FF:]
    hidden = (jax.nn.silu(gate_act) * upward).astype(jnp.bfloat16)
    output = middle + lax.dot_general(
        hidden, w_down, CONTRACT_LAST, preferred_element_type=jnp.float32
    )
    kept_state = (
        values,
        scale_one,
        normed,
        queries,
        keys_rot,
        values_kv,
        log_total,
        context,
        middle,
        scale_two,
        normed_two,
        gate_act,
        upward,
        hidden,
    )
    return (output, kept_state)


def backward_layer(kept_state, grad_out, seq_length, weight_parts, gain_pair, cosine, sine):
    (
        values,
        scale_one,
        normed,
        queries,
        keys_rot,
        values_kv,
        log_total,
        context,
        middle,
        scale_two,
        normed_two,
        gate_act,
        upward,
        hidden,
    ) = kept_state
    w_qkv, w_gate_up, w_attn, w_down = weight_parts
    q_width = HEADS * HEAD_DIM
    kv_width = KV_HEADS * HEAD_DIM
    length_rows = values.shape[0]
    grad_mlp = grad_out.astype(jnp.bfloat16)
    grad_hidden = jnp.dot(grad_mlp, w_down, preferred_element_type=jnp.float32)
    sigmoid_gate = jax.nn.sigmoid(gate_act)
    grad_gate = grad_hidden * upward * sigmoid_gate * (1.0 + gate_act * (1.0 - sigmoid_gate))
    grad_up = grad_hidden * gate_act * sigmoid_gate
    grad_gate_up = jnp.concatenate([grad_gate, grad_up], 1).astype(jnp.bfloat16)
    grad_norm_two = lax.dot_general(
        grad_gate_up, w_gate_up, CONTRACT_LAST, preferred_element_type=jnp.float32
    )
    grad_mid, gain_two = rms_back(middle, scale_two, gain_pair[1], grad_norm_two)
    grad_mid = grad_out + grad_mid
    grad_attn = grad_mid.astype(jnp.bfloat16)
    grad_context = jnp.dot(grad_attn, w_attn, preferred_element_type=jnp.float32).astype(
        jnp.bfloat16
    )
    grad_context = grad_context.reshape(length_rows, KV_HEADS, HEADS // KV_HEADS, HEAD_DIM)
    allowed = allowed_keys(length_rows, seq_length)
    scores, grouped = score_block(queries, keys_rot, allowed)
    probs_full = jnp.exp(scores - log_total)
    grad_values = jnp.einsum(
        "kgqp,qkgd->pkd",
        probs_full.astype(jnp.bfloat16),
        grad_context,
        preferred_element_type=jnp.float32,
    )
    grad_probs = jnp.einsum(
        "qkgd,pkd->kgqp", grad_context, values_kv, preferred_element_type=jnp.float32
    )
    grad_scores = (
        probs_full * (grad_probs - jnp.sum(grad_probs * probs_full, -1, keepdims=True))
    ).astype(jnp.bfloat16)
    grad_queries = jnp.einsum(
        "kgqp,pkd->qkgd", grad_scores, keys_rot, preferred_element_type=jnp.float32
    ) * HEAD_DIM ** (-0.5)
    grad_keys = jnp.einsum(
        "kgqp,qkgd->pkd", grad_scores, grouped, preferred_element_type=jnp.float32
    ) * HEAD_DIM ** (-0.5)
    grad_queries = unrotate(
        grad_queries.reshape(length_rows, HEADS, HEAD_DIM), cosine, sine
    ).reshape(length_rows, q_width)
    grad_keys = unrotate(grad_keys, cosine, sine).reshape(length_rows, kv_width)
    grad_proj = jnp.concatenate(
        [grad_queries, grad_keys, grad_values.reshape(length_rows, kv_width)], 1
    ).astype(jnp.bfloat16)
    grad_norm_one = lax.dot_general(
        grad_proj, w_qkv, CONTRACT_LAST, preferred_element_type=jnp.float32
    )
    grad_input, gain_one = rms_back(values, scale_one, gain_pair[0], grad_norm_one)
    grad_input = grad_mid + grad_input
    pieces = (
        normed,
        grad_proj,
        normed_two,
        grad_gate_up,
        context,
        grad_attn,
        hidden,
        grad_mlp,
        jnp.stack([gain_one, gain_two]),
    )
    return (grad_input, pieces)


def choose(flag, when_first, otherwise):
    return jax.tree.map(
        lambda one_side, other_side: jnp.where(flag, one_side, other_side), when_first, otherwise
    )


def local(ends_in, in_weight, out_weight, norm_gain, seq_len):
    own_rows = ends_in[0]
    micro_count = seq_len.shape[0]
    slot_rows = own_rows.shape[0] // micro_count
    width = own_rows.shape[1]
    is_first = lax.axis_index("section") == 0
    gain_pair = norm_gain[0]
    cosine, sine = rope_tables(slot_rows)
    positions = jnp.arange(slot_rows)
    full_in, full_out = (
        lax.all_gather(in_weight, "shard", axis=1, tiled=True),
        lax.all_gather(out_weight, "shard", axis=1, tiled=True),
    )
    weight_parts = split_weights(full_in, full_out)
    steps_total = micro_count + 1
    received = jnp.zeros((slot_rows, width), jnp.bfloat16)
    saved_states = []
    outputs = []
    for step_index in range(steps_total):
        own_index = min(step_index, micro_count - 1)
        late_index = max(step_index - 1, 0)
        seq_length = jnp.where(is_first, seq_len[own_index], seq_len[late_index])
        block_in = jnp.where(
            is_first, own_rows[own_index * slot_rows : (own_index + 1) * slot_rows], received
        )
        output, kept_state = forward_layer(
            block_in, seq_length, weight_parts, gain_pair, cosine, sine
        )
        saved_states.append(kept_state)
        outputs.append(output)
        if step_index + 1 < steps_total:
            received = from_behind(output.astype(jnp.bfloat16), "section", 1)
    received = jnp.zeros((slot_rows, width), jnp.bfloat16)
    results = []
    for step_index in range(steps_total):
        own_index = min(step_index, micro_count - 1)
        late_index = max(step_index - 1, 0)
        seq_length = jnp.where(is_first, seq_len[late_index], seq_len[own_index])
        kept_state = choose(
            is_first, saved_states[late_index], saved_states[min(step_index + 1, micro_count)]
        )
        valid = (positions < seq_len[own_index]).astype(jnp.float32)[:, None]
        target = (
            own_rows[own_index * slot_rows : (own_index + 1) * slot_rows].astype(jnp.float32)
            * valid
        )
        grad_out = jnp.where(is_first, received.astype(jnp.float32), target)
        grad_input, pieces = backward_layer(
            kept_state, grad_out, seq_length, weight_parts, gain_pair, cosine, sine
        )
        results.append((grad_input, pieces))
        if step_index + 1 < steps_total:
            received = from_behind(grad_input.astype(jnp.bfloat16), "section", -1)
    per_micro = [
        choose(is_first, results[index_mb + 1], results[index_mb])
        for index_mb in range(micro_count)
    ]
    grad_first = jnp.concatenate([entry[0] for entry in per_micro], 0)
    final_rows = jnp.concatenate([outputs[index_mb + 1] for index_mb in range(micro_count)], 0)
    ends_local = jnp.where(is_first, grad_first, final_rows).astype(jnp.bfloat16)[None]

    def stacked(position):
        return jnp.concatenate([entry[1][position] for entry in per_micro], 0)

    normed_all = stacked(0)
    grad_proj_all = stacked(1)
    normed_two_all = stacked(2)
    grad_gate_up_all = stacked(3)
    context_all = stacked(4)
    grad_attn_all = stacked(5)
    hidden_all = stacked(6)
    grad_mlp_all = stacked(7)
    gain_terms = sum((entry[1][8] for entry in per_micro))

    def product_rows(rows_side, cols_side):
        return lax.dot_general(
            rows_side, cols_side, CONTRACT_ROWS, preferred_element_type=jnp.float32
        )

    group_rows = lax.psum_scatter(
        jnp.concatenate(
            [
                product_rows(normed_all, grad_proj_all),
                product_rows(normed_two_all, grad_gate_up_all),
                product_rows(grad_attn_all, context_all),
                product_rows(grad_mlp_all, hidden_all),
            ],
            1,
        ).astype(jnp.bfloat16),
        "shard",
        scatter_dimension=0,
        tiled=True,
    )
    device_rows = lax.psum_scatter(group_rows, "dp", scatter_dimension=0, tiled=True).astype(
        jnp.float32
    )
    gain_rows = lax.psum_scatter(gain_terms, ("shard", "dp"), scatter_dimension=1, tiled=True)
    in_cols = in_weight.shape[2]
    return (
        ends_local,
        device_rows[:, :in_cols][None],
        device_rows[:, in_cols:][None],
        gain_rows[None],
    )


def solution(mesh):
    in_specs = (
        P("section", ("shard", "dp"), None),
        P("section", "shard", None),
        P("section", "shard", None),
        P("section", None, None),
        P(("shard", "dp")),
    )
    out_specs = (
        P("section", ("shard", "dp"), None),
        P("section", ("shard", "dp"), None),
        P("section", ("shard", "dp"), None),
        P("section", None, ("shard", "dp")),
    )
    return jax.shard_map(local, mesh=mesh, in_specs=in_specs, out_specs=out_specs, check_vma=False)
```

profile of v0, /device:TPU:20, one launch (start us, length us, event | category | flops | bytes accessed | tf_op | source)
XLA Modules:
  0.0 3231.9 jit_solution(13781771068034692494)
XLA Ops:
  17.5 675.1 %all-gather.3.cloned.1.call-done = bf16[1,2048,19456]{2,1,0:T(8,128)(2,1)} async-done(((bf16[1,512,19456]{2,1,0:T(8,128)(2,1)}), bf16[1,2048,19456]{2,1,0:T(8,128)(2,1)}) %all-gather.3.cloned.1.call-update) | async-done | bytes 79691792 | tf_op jit(solution)/shard_map/all_gather | solution.py:244
  692.6 5.9 fusion.34
  702.9 359.1 %all-gather.5.cloned.1.call-done = bf16[1,2048,10240]{2,1,0:T(8,128)(2,1)} async-done(((bf16[1,512,10240]{2,1,0:T(8,128)(2,1)}), bf16[1,2048,10240]{2,1,0:T(8,128)(2,1)}) %all-gather.5.cloned.1.call-update) | async-done | bytes 41943056 | tf_op jit(solution)/shard_map/all_gather | solution.py:245
  1062.0 6.3 multiply_reduce_fusion.17
  1068.4 25.6 fusion.10
  1094.1 16.4 fusion.72
  1114.3 5.9 fusion.32
  1125.4 6.4 multiply_reduce_fusion.16
  1133.2 25.5 fusion.8
  1158.7 17.5 multiply_convert_fusion.7
  1176.2 29.8 multiply_reduce_fusion.5
  1207.5 5.8 fusion.75
  1213.3 2.0 copy.261
  1215.3 2.0 fusion.111
  1220.6 16.2 fusion.63
  1236.8 2.8 collective-permute-start.2
  1242.7 2.8 copy.253
  1245.5 2.5 add_convert_fusion.3
  1253.5 8.8 fusion.124
  1263.0 5.9 fusion.28
  1278.7 6.4 multiply_reduce_fusion.13
  1288.8 25.5 fusion.4
  1315.9 5.1 select_select_fusion.1
  1326.9 20.4 multiply_convert_fusion.4
  1347.3 29.8 multiply_reduce_fusion.7
  1377.1 2.4 broadcast_select_fusion.13
  1380.3 5.7 fusion.78
  1387.9 2.0 fusion.112
  1403.3 9.3 multiply_reduce_fusion.8
  1416.2 2.7 collective-permute-done.3
  1418.9 18.0 multiply_convert_fusion.2
  1436.9 4.5 broadcast_select_fusion.1
  1441.4 29.4 multiply_reduce_fusion.3
  1470.9 2.3 broadcast_select_fusion.12
  1474.0 5.0 fusion.81
  1488.7 7.0 convolution_convert_fusion.3
  1495.8 6.4 convolution_convert_fusion.2
  1502.2 13.9 convolution_convert_fusion.1
  1516.1 26.8 convolution_convert_fusion
  1542.9 79.3 %pad_maximum_fusion = bf16[2048,29696]{1,0:T(8,128)(2,1)} fusion(bf16[2048,8192]{1,0:T(8,128)(2,1)} %convolution_convert_fusion.1, bf16[2048,2048]{1,0:T(8,128)(2,1)} %convolution_convert_fusion.3, bf16[2048,16384]{1,0:T(8,128)(2,1)} %convolution_convert_fusion, bf16[2048,3072]{1,0:T(8,128)(2,1)} %convolution_convert_fusion.2), kind=kLoop, calls=%fused_computation | loop fusion | flops 486539264 | bytes 243269632 | tf_op jit(solution)/shard_map/concatenate | solution.py:314
  1623.4 7.1 multiply_reduce_fusion.4
  1632.0 987.8 %reduce-scatter.12.cloned.1.call-done = bf16[512,29696]{1,0:T(8,128)(2,1)} async-done(((bf16[2048,29696]{1,0:T(8,128)(2,1)}), bf16[512,29696]{1,0:T(8,128)(2,1)}) %reduce-scatter.12.cloned.1.call-update) | async-done | bytes 30408720
  2621.2 15.6 fusion.69
  2638.9 57.1 %reduce-scatter.10.cloned.1.call-done = f32[128,2]{1,0:T(8,128)} async-done(((f32[2048,2]{1,0:T(8,128)}), f32[128,2]{1,0:T(8,128)}) %reduce-scatter.10.cloned.1.call-update) | async-done | bytes 1040
  2697.5 503.5 %reduce-scatter.14.cloned.1.call-done = bf16[128,29696]{1,0:T(8,128)(2,1)} async-done(((bf16[512,29696]{1,0:T(8,128)(2,1)}), bf16[128,29696]{1,0:T(8,128)(2,1)}) %reduce-scatter.14.cloned.1.call-update) | async-done | bytes 7602192
  3201.0 10.0 convert_element_type.267
  3210.9 5.3 slice_bitcast_fusion.1
  3216.3 8.7 slice_bitcast_fusion
  (415 shorter events, 93.7 us)
Async XLA Ops:
  7.2 685.5 %all-gather.3.cloned.1.call-start = ((), (), s32[]{:S(2)}) async-start(), calls=%async_computation.3 | async-start | bytes 99614720 | tf_op jit(solution)/shard_map/all_gather | solution.py:244
  7.9 9.5 copy-start.88
  7.9 1054.1 %all-gather.5.cloned.1.call-start = ((), (), s32[]{:S(2)}) async-start(), calls=%async_computation.4 | async-start | bytes 52428800 | tf_op jit(solution)/shard_map/all_gather | solution.py:245
  8.7 2611.1 %reduce-scatter.12.cloned.1.call-start = ((), (), s32[]{:S(2)}) async-start(), calls=%async_computation.6 | async-start | bytes 152043520
  15.8 1097.8 %copy-start.100 = (f32[64]{0:T(128)}, f32[64]{0:T(128)S(1)}, u32[]{:S(2)}) copy-start(f32[64]{0:T(128)S(1)} %fusion.127) | copy-start | bytes 772
  15.9 682.7 %copy-start.125 = (f32[64]{0:T(128)}, f32[64]{0:T(128)S(1)}, u32[]{:S(2)}) copy-start(f32[64]{0:T(128)S(1)} %add_rsqrt_fusion.5) | copy-start | bytes 772
  16.0 684.9 %copy-start.86 = (pred[64,64]{0,1:T(8,128)(4,1)}, pred[64,64]{0,1:T(8,128)(4,1)S(1)}, u32[]{:S(2)}) copy-start(pred[64,64]{0,1:T(8,128)(4,1)S(1)} %fusion.189) | copy-start | bytes 12292
  17.5 1395.2 %copy-start.80 = (f32[1,1,2048]{2,1,0:T(1,128)}, f32[1,1,2048]{2,1,0:T(1,128)S(1)}, u32[]{:S(2)}) copy-start(f32[1,1,2048]{2,1,0:T(1,128)S(1)} %get-tuple-element.94) | copy-start | bytes 24580
  1068.4 25.7 copy-start.19
  1068.4 25.7 copy-start.114
  1068.4 25.6 copy-start.104
  1094.0 18.5 copy-start.70
  1110.5 3.0 collective-permute-start
  1113.7 299.0 %copy-start.8 = (bf16[64,2048]{1,0:T(8,128)(2,1)}, bf16[64,2048]{1,0:T(8,128)(2,1)S(1)}, u32[]{:S(2)}) copy-start(bf16[64,2048]{1,0:T(8,128)(2,1)S(1)} %get-tuple-element.34) | copy-start | bytes 786436
  1131.8 44.4 %copy-start.16 = (f32[64,2048]{1,0:T(8,128)}, f32[64,2048]{1,0:T(8,128)S(1)}, u32[]{:S(2)}) copy-start(f32[64,2048]{1,0:T(8,128)S(1)} %get-tuple-element.116) | copy-start | bytes 1572868
  1133.2 25.5 copy-start.106
  1158.7 17.5 copy-start.113
  1236.8 16.7 collective-permute-start.2
  1251.1 11.2 copy-start.72
  1251.5 10.9 copy-start.74
  1253.5 8.9 copy-start.47
  1253.5 8.9 copy-start.101
  1253.5 8.9 copy-start.103
  1314.4 10.7 collective-permute-start.1
  1326.9 20.4 copy-start.112
  1347.3 29.8 copy-start.98
  1394.1 9.1 copy-start.75
  1403.2 9.4 copy-start.49
  1403.2 9.4 copy-start.6
  1403.2 9.4 copy-start.61
  1403.2 9.4 copy-start.121
  1403.2 9.4 copy-start.123
  1403.3 9.4 copy-start.124
  1403.3 9.4 copy-start.126
  1403.3 12.2 copy-start.25
  1403.3 12.2 copy-start.35
  1403.3 12.2 copy-start.85
  1403.3 12.2 copy-start.89
  1414.2 4.7 collective-permute-start.3
  1418.9 18.0 copy-start.71
  1502.2 13.9 copy-start.2
  1502.2 13.9 copy-start.42
  1502.2 13.9 copy-start.43
  1622.3 1073.7 %reduce-scatter.10.cloned.1.call-start = ((), (), s32[]{:S(2)}) async-start(), calls=%async_computation.5 | async-start | bytes 1114112
  1631.9 1569.1 %reduce-scatter.14.cloned.1.call-start = ((), (), s32[]{:S(2)}) async-start(), calls=%async_computation.7 | async-start | bytes 38010880
  2621.2 15.6 copy-start.22
  2621.2 15.6 copy-start.64
  2621.2 15.9 copy-start.65
  (89 other events, 385.4 us)
Sparse Core Ops, SparseCore 0:
  9.9 682.6 all-gather.2
  694.5 367.4 all-gather.4
  1622.4 997.3 reduce-scatter.11
  2622.6 73.3 reduce-scatter.9
  2698.2 502.7 reduce-scatter.13
where the time goes:
time: 3240 us; the launch traced here: 3230 us
  waiting for transfers between devices  2590 us (80%)
  matrix products  421 us (13%)
  other arithmetic  138 us (4%)
  local copies, waits for them, and re-layouts  60.1 us (2%)
    unnamed x8, waiting for transfers between devices  1550 us
    all_gather x1, waiting for transfers between devices, local(): lax.all_gather(in_weight, 'shard', axis=1, tiled=True)  675 us
    all_gather x1, waiting for transfers between devices, local(): lax.all_gather(out_weight, 'shard', axis=1, tiled=True)  359 us
    dot_general x3, matrix products, backward_layer(): lax.dot_general(grad_gate_up, w_gate_up, CONTRACT_LAST, preferred_element...  89 us
    concatenate x1, other arithmetic, local(): jnp.concatenate([product_rows(normed_all, grad_proj_all), product_rows(no...  79.3 us
    dot_general x3, matrix products, forward_layer(): gate_up = jnp.dot(normed_two, w_gate_up, preferred_element_type=jnp.float32)  76.7 us
  transfers between devices with their start and end apart: 9, of which 6 were waited for; matrix products, arithmetic and copies ran while one was open for 2% of the time, Pallas kernels for 0%

commit v1 on v0

v1 whole, which is shorter than its diff:
```python
import functools

import jax
import jax.numpy as jnp
from jax import lax
from jax.experimental import pallas as pl
from jax.experimental.pallas import tpu as pltpu
from jax.sharding import PartitionSpec as P

HEADS = 32
KV_HEADS = 8
GROUP = HEADS // KV_HEADS
HEAD_DIM = 64
FF = 8192
EPSILON = 1e-05
BF16 = jnp.bfloat16
F32 = jnp.float32
CORES = 2
LINE = KV_HEADS // CORES
Q_SLAB = GROUP * HEAD_DIM
QKV_SLAB = Q_SLAB + 2 * HEAD_DIM
FF_SLAB = FF // KV_HEADS
Q_COLS = HEADS * HEAD_DIM
KV_COLS = KV_HEADS * HEAD_DIM


def line_place():
    core = lax.axis_index("section")
    depth = lax.axis_index("dp")
    return core, depth, lax.rem(depth, LINE)


def greet(core, depth, place):
    barrier = pltpu.get_barrier_semaphore()
    pl.semaphore_signal(barrier, inc=1, device_id={"section": 1 - core})

    @pl.when(place < LINE - 1)
    def _():
        pl.semaphore_signal(barrier, inc=1, device_id={"dp": depth + 1})

    @pl.when(place > 0)
    def _():
        pl.semaphore_signal(barrier, inc=1, device_id={"dp": depth - 1})

    both = jnp.where((place > 0) & (place < LINE - 1), 3, 2)
    pl.semaphore_wait(barrier, both)


def gather_body(x_ref, o_ref, up_send, dn_send, sib_send, z_recv, sib_recv):
    core, depth, place = line_place()
    greet(core, depth, place)
    own = place * CORES + core
    o_ref[own] = x_ref[...]

    def up(where):
        index = where * CORES + core
        return pltpu.make_async_remote_copy(
            o_ref.at[index], o_ref.at[index], up_send.at[where], z_recv.at[where],
            device_id={"dp": depth + 1},
        )

    def down(where):
        index = where * CORES + core
        return pltpu.make_async_remote_copy(
            o_ref.at[index], o_ref.at[index], dn_send.at[where], z_recv.at[where],
            device_id={"dp": depth - 1},
        )

    def across(where):
        index = where * CORES + core
        return pltpu.make_async_remote_copy(
            o_ref.at[index], o_ref.at[index], sib_send.at[where], sib_recv.at[where],
            device_id={"section": 1 - core},
        )

    def arrived(where, other):
        index = where * CORES + other
        sem = z_recv if other is core else sib_recv
        return pltpu.make_async_remote_copy(
            o_ref.at[index], o_ref.at[index], up_send.at[where], sem.at[where],
            device_id={"section": 1 - core},
        )

    @pl.when(place < LINE - 1)
    def _():
        up(place).start()

    @pl.when(place > 0)
    def _():
        down(place).start()

    across(place).start()
    for step in range(1, LINE):
        @pl.when(place >= step)
        def _():
            arrived(place - step, core).wait_recv()

            @pl.when(place < LINE - 1)
            def _():
                up(place - step).start()

            across(place - step).start()

        @pl.when(place + step < LINE)
        def _():
            arrived(place + step, core).wait_recv()

            @pl.when(place > 0)
            def _():
                down(place + step).start()

            across(place + step).start()

    for where in range(LINE):
        arrived(where, 1 - core).wait_recv()
        across(where).wait_send()

        @pl.when((where <= place) & (place < LINE - 1))
        def _():
            up(where).wait_send()

        @pl.when((where >= place) & (place > 0))
        def _():
            down(where).wait_send()


def gather_line(block):
    rows, width = block.shape
    blocks = LINE * CORES
    sems = pltpu.SemaphoreType.DMA((LINE,))
    out = pl.pallas_call(
        gather_body,
        out_shape=jax.ShapeDtypeStruct((blocks, rows, width), block.dtype),
        in_specs=[pl.BlockSpec(memory_space=pltpu.VMEM)],
        out_specs=pl.BlockSpec(memory_space=pltpu.VMEM),
        scratch_shapes=[sems] * 5,
        compiler_params=pltpu.CompilerParams(
            collective_id=0, has_side_effects=True, vmem_limit_bytes=16 * 2**20
        ),
        name="gather_line",
        cost_estimate=pl.CostEstimate(flops=0, bytes_accessed=60_000_000, transcendentals=0),
    )(block)
    return out.reshape(blocks * rows, width)


def scatter_body(p_ref, o_ref, sib_buf, rx_up, rx_dn, tx_up, tx_dn,
                 sib_send, sib_recv, up_send, up_recv, dn_send, dn_recv):
    core, depth, place = line_place()
    greet(core, depth, place)

    def across(where):
        return pltpu.make_async_remote_copy(
            p_ref.at[where * CORES + 1 - core], sib_buf.at[where],
            sib_send.at[where], sib_recv.at[where], device_id={"section": 1 - core},
        )

    def up(where):
        return pltpu.make_async_remote_copy(
            tx_up.at[where], rx_up.at[where], up_send.at[where], up_recv.at[where],
            device_id={"dp": depth + 1},
        )

    def down(where):
        return pltpu.make_async_remote_copy(
            tx_dn.at[where], rx_dn.at[where], dn_send.at[where], dn_recv.at[where],
            device_id={"dp": depth - 1},
        )

    def summed(where):
        return p_ref[where * CORES + core].astype(F32) + sib_buf[where].astype(F32)

    for step in range(LINE - 1, 0, -1):
        @pl.when(place + step < LINE)
        def _():
            across(place + step).start()

        @pl.when(place >= step)
        def _():
            across(place - step).start()

    across(place).start()
    for step in range(LINE - 1, 0, -1):
        @pl.when(place + step < LINE)
        def _():
            where = place + step
            across(where).wait_recv()

            @pl.when(place > 0)
            def _():
                up(where).wait_recv()
                tx_up[where] = (summed(where) + rx_up[where].astype(F32)).astype(BF16)

            @pl.when(place == 0)
            def _():
                tx_up[where] = summed(where).astype(BF16)

            up(where).start()

        @pl.when(place >= step)
        def _():
            where = place - step
            across(where).wait_recv()

            @pl.when(place < LINE - 1)
            def _():
                down(where).wait_recv()
                tx_dn[where] = (summed(where) + rx_dn[where].astype(F32)).astype(BF16)

            @pl.when(place == LINE - 1)
            def _():
                tx_dn[where] = summed(where).astype(BF16)

            down(where).start()

    across(place).wait_recv()
    o_ref[...] = summed(place)

    @pl.when(place > 0)
    def _():
        up(place).wait_recv()
        o_ref[...] += rx_up[place].astype(F32)

    @pl.when(place < LINE - 1)
    def _():
        down(place).wait_recv()
        o_ref[...] += rx_dn[place].astype(F32)

    for where in range(LINE):
        across(where).wait_send()

        @pl.when(where > place)
        def _():
            up(where).wait_send()

        @pl.when(where < place)
        def _():
            down(where).wait_send()


def scatter_line(partial):
    blocks = LINE * CORES
    rows = partial.shape[0] // blocks
    width = partial.shape[1]
    sems = pltpu.SemaphoreType.DMA((LINE,))
    buffer = pltpu.VMEM((LINE, rows, width), BF16)
    return pl.pallas_call(
        scatter_body,
        out_shape=jax.ShapeDtypeStruct((rows, width), F32),
        in_specs=[pl.BlockSpec(memory_space=pltpu.VMEM)],
        out_specs=pl.BlockSpec(memory_space=pltpu.VMEM),
        scratch_shapes=[buffer] * 5 + [sems] * 6,
        compiler_params=pltpu.CompilerParams(
            collective_id=1, has_side_effects=True, vmem_limit_bytes=24 * 2**20
        ),
        name="scatter_line",
        cost_estimate=pl.CostEstimate(flops=0, bytes_accessed=60_000_000, transcendentals=0),
    )(partial.reshape(blocks, rows, width))


def swap_cores(value):
    return lax.ppermute(value, "section", [(0, 1), (1, 0)])


def hop(value, bit):
    peers = lax.axis_size("shard")
    return lax.ppermute(value, "shard", [(i, i ^ bit) for i in range(peers)])


def gather_rows(block):
    half = block.shape[0] // 2
    one = hop(block, 1)
    two = hop(block, 2)
    top = hop(two[:half], 1)
    bottom = hop(one[half:], 2)
    return jnp.concatenate([block, one, two, top, bottom], 0)


def reduce_rows(term):
    far = term(3)
    half = far.shape[0] // 2
    via_one = hop(far[:half], 1).astype(F32)
    via_two = hop(far[half:], 2).astype(F32)
    first = term(1).astype(F32)
    one = hop(jnp.concatenate([first[:half], first[half:] + via_two], 0).astype(BF16), 1)
    second = term(2).astype(F32)
    two = hop(jnp.concatenate([second[:half] + via_one, second[half:]], 0).astype(BF16), 2)
    return (term(0).astype(F32) + one.astype(F32) + two.astype(F32)).astype(BF16)


def relative(values, shard):
    blocks = jnp.split(values, 4, -1)
    odd = (shard & 1) == 1
    high = (shard & 2) == 2
    blocks = [jnp.where(odd, blocks[i ^ 1], blocks[i]) for i in range(4)]
    blocks = [jnp.where(high, blocks[i ^ 2], blocks[i]) for i in range(4)]
    return jnp.concatenate(blocks, -1)


def rope_tables(rows):
    half_dim = HEAD_DIM // 2
    inverse = 500000.0 ** (-(jnp.arange(half_dim, dtype=F32) * 2.0 / HEAD_DIM))
    angles = jnp.arange(rows, dtype=F32)[:, None] * inverse[None, :]
    return (jnp.cos(angles)[None, :, None, :], jnp.sin(angles)[None, :, None, :])


def rotate(values, cosine, sine):
    a, b = jnp.split(values, 2, -1)
    return jnp.concatenate([a * cosine - b * sine, b * cosine + a * sine], -1)


def unrotate(grads, cosine, sine):
    a, b = jnp.split(grads, 2, -1)
    return jnp.concatenate([a * cosine + b * sine, b * cosine - a * sine], -1)


def rms_scale(values):
    return lax.rsqrt(jnp.mean(values * values, -1, keepdims=True) + EPSILON)


def rms_back(values, scale, gain_row, grad_norm):
    grad_hat = grad_norm * gain_row
    grad_gain = jnp.sum(grad_norm * values * scale, 0)
    inner = jnp.mean(grad_hat * values, -1, keepdims=True)
    return (scale * grad_hat - values * scale * scale * scale * inner, grad_gain)


def mm(a, b):
    return jnp.dot(a, b, preferred_element_type=F32)


def mm_last(a, b):
    return lax.dot_general(a, b, (((1,), (1,)), ((), ())), preferred_element_type=F32)


def mm_rows(a, b):
    return lax.dot_general(a, b, (((0,), (0,)), ((), ())), preferred_element_type=F32)


def masked_scores(queries, keys, lengths):
    rows = queries.shape[1]
    places = jnp.arange(rows)
    allowed = (places[:, None] >= places[None, :])[None] & (
        places[None, None, :] < lengths[:, None, None]
    )
    scores = jnp.einsum("sqgd,spd->sgqp", queries, keys, preferred_element_type=F32)
    return jnp.where(allowed[:, None], scores * HEAD_DIM**-0.5, -1e30)


def forward_layer(x, weights, gains, lengths, tables):
    w_qkv, w_attn, w_gu, w_down = weights
    slots = lengths.shape[0]
    rows = x.shape[0]
    scale_one = rms_scale(x)
    normed = gather_line((x * scale_one * gains[0]).astype(BF16))
    projected = mm(normed, w_qkv)
    queries = rotate(projected[:, :Q_SLAB].reshape(slots, rows, GROUP, HEAD_DIM), *tables).astype(BF16)
    keys = rotate(
        projected[:, Q_SLAB:Q_SLAB + HEAD_DIM].reshape(slots, rows, 1, HEAD_DIM), *tables
    ).astype(BF16)[:, :, 0]
    values = projected[:, Q_SLAB + HEAD_DIM:].reshape(slots, rows, HEAD_DIM).astype(BF16)
    scores = masked_scores(queries, keys, lengths)
    top = jnp.max(scores, -1, keepdims=True)
    terms = jnp.exp(scores - top)
    total = jnp.sum(terms, -1, keepdims=True)
    log_total = top + jnp.log(total)
    probs = (terms / total).astype(BF16)
    context = jnp.einsum("sgqp,spd->sqgd", probs, values, preferred_element_type=F32)
    context = context.reshape(slots * rows, Q_SLAB).astype(BF16)
    middle = x + scatter_line(mm_last(context, w_attn).astype(BF16))
    scale_two = rms_scale(middle)
    normed_two = gather_line((middle * scale_two * gains[1]).astype(BF16))
    gate_up = mm(normed_two, w_gu)
    gate, up = gate_up[:, :FF_SLAB], gate_up[:, FF_SLAB:]
    hidden = (jax.nn.silu(gate) * up).astype(BF16)
    output = middle + scatter_line(mm_last(hidden, w_down).astype(BF16))
    return output, (x, scale_one, normed, queries, keys, values, log_total, context,
                    middle, scale_two, normed_two, gate, up, hidden)


def backward_layer(kept, grad_out, weights, gains, lengths, tables):
    (x, scale_one, normed, queries, keys, values, log_total, context,
     middle, scale_two, normed_two, gate, up, hidden) = kept
    w_qkv, w_attn, w_gu, w_down = weights
    slots = lengths.shape[0]
    rows = x.shape[0]
    grad_mlp = gather_line(grad_out.astype(BF16))
    grad_hidden = mm(grad_mlp, w_down)
    sig = jax.nn.sigmoid(gate)
    grad_gate = grad_hidden * up * sig * (1.0 + gate * (1.0 - sig))
    grad_up = grad_hidden * gate * sig
    grad_gu = jnp.concatenate([grad_gate, grad_up], 1).astype(BF16)
    grad_normed = scatter_line(mm_last(grad_gu, w_gu).astype(BF16))
    back, gain_two = rms_back(middle, scale_two, gains[1], grad_normed)
    grad_mid = grad_out + back
    grad_attn = gather_line(grad_mid.astype(BF16))
    grad_context = mm(grad_attn, w_attn).astype(BF16).reshape(slots, rows, GROUP, HEAD_DIM)
    probs = jnp.exp(masked_scores(queries, keys, lengths) - log_total)
    grad_values = jnp.einsum("sgqp,sqgd->spd", probs.astype(BF16), grad_context, preferred_element_type=F32)
    grad_probs = jnp.einsum("sqgd,spd->sgqp", grad_context, values, preferred_element_type=F32)
    inner = jnp.sum(grad_probs * probs, -1, keepdims=True)
    grad_scores = (probs * (grad_probs - inner)).astype(BF16)
    grad_queries = jnp.einsum("sgqp,spd->sqgd", grad_scores, keys, preferred_element_type=F32)
    grad_keys = jnp.einsum("sgqp,sqgd->spd", grad_scores, queries, preferred_element_type=F32)
    grad_queries = unrotate(grad_queries * HEAD_DIM**-0.5, *tables)
    grad_keys = unrotate(grad_keys[:, :, None] * HEAD_DIM**-0.5, *tables)
    grad_proj = jnp.concatenate(
        [
            grad_queries.reshape(slots * rows, Q_SLAB),
            grad_keys.reshape(slots * rows, HEAD_DIM),
            grad_values.reshape(slots * rows, HEAD_DIM),
        ],
        1,
    ).astype(BF16)
    grad_normed = scatter_line(mm_last(grad_proj, w_qkv).astype(BF16))
    back, gain_one = rms_back(x, scale_one, gains[0], grad_normed)
    mlp = ((normed_two, grad_gu), (grad_mlp, hidden))
    attn = ((normed, grad_proj), (grad_attn, context))
    return grad_mid + back, mlp, attn, jnp.stack([gain_one, gain_two])


def slab(weight, start, size):
    return lax.dynamic_slice_in_dim(weight, start, size, 1)


def attn_slab(w_in, w_out, head):
    return jnp.concatenate(
        [
            slab(w_in, head * Q_SLAB, Q_SLAB),
            slab(w_in, Q_COLS + head * HEAD_DIM, HEAD_DIM),
            slab(w_in, Q_COLS + KV_COLS + head * HEAD_DIM, HEAD_DIM),
            slab(w_out, head * Q_SLAB, Q_SLAB),
        ],
        1,
    )


def mlp_slab(w_in, w_out, head):
    base = Q_COLS + 2 * KV_COLS
    return jnp.concatenate(
        [
            slab(w_in, base + head * FF_SLAB, FF_SLAB),
            slab(w_in, base + FF + head * FF_SLAB, FF_SLAB),
            slab(w_out, Q_COLS + head * FF_SLAB, FF_SLAB),
        ],
        1,
    )


def line_pairs(shift):
    peers = lax.axis_size("dp")
    return [(i, i // LINE * LINE + (i % LINE + shift) % LINE) for i in range(peers)]


def line_exchange(blocks, place):
    got = [lax.dynamic_index_in_dim(blocks, place, 0, False)]
    for shift in range(1, LINE):
        to = lax.rem(place + shift, LINE)
        got.append(lax.ppermute(lax.dynamic_index_in_dim(blocks, to, 0, False), "dp", line_pairs(shift)))
    return got


def local(ends_in, in_weight, out_weight, norm_gain, seq_len):
    core = lax.axis_index("section")
    shard = lax.axis_index("shard")
    depth = lax.axis_index("dp")
    place = lax.rem(depth, LINE)
    first = core == 0
    replicas = lax.axis_size("dp") // LINE
    w_in, w_out = in_weight[0], out_weight[0]
    head = place * CORES + core
    sibling = place * CORES + 1 - core
    rows = ends_in.shape[1] // CORES

    def by_layer(mine, others):
        return jnp.where(first, mine, others), jnp.where(first, others, mine)

    attn = by_layer(attn_slab(w_in, w_out, head), swap_cores(attn_slab(w_in, w_out, sibling)))
    mlp = by_layer(mlp_slab(w_in, w_out, head), swap_cores(mlp_slab(w_in, w_out, sibling)))

    def layer_weights(index):
        a = gather_rows(attn[index])
        m = gather_rows(mlp[index])
        return (a[:, :QKV_SLAB], a[:, QKV_SLAB:], m[:, :2 * FF_SLAB], m[:, 2 * FF_SLAB:])

    weights = [layer_weights(0), layer_weights(1)]
    own_gain = relative(norm_gain[0], shard)
    gains = by_layer(own_gain, swap_cores(own_gain))
    ends = relative(ends_in[0], shard)
    mine, others = ends[:rows], ends[rows:]
    crossed = swap_cores(jnp.where(first, others, mine))
    x = jnp.where(first, mine, crossed).astype(F32)
    cot = jnp.where(first, crossed, others).astype(F32)
    line_groups = [
        [r * LINE + p for p in range(LINE)] for r in range(replicas)
    ]
    lengths = lax.all_gather(seq_len, "dp", tiled=True, axis_index_groups=line_groups if replicas > 1 else None)
    own_length = jnp.where(first, seq_len[0], seq_len[1])
    valid = (jnp.arange(rows) < own_length).astype(F32)[:, None]
    tables = rope_tables(rows)

    y0, kept0 = forward_layer(x, weights[0], gains[0], lengths, tables)
    y1, kept1 = forward_layer(y0.astype(BF16).astype(F32), weights[1], gains[1], lengths, tables)
    dx1, mlp1, attn1, gain1 = backward_layer(kept1, cot * valid, weights[1], gains[1], lengths, tables)
    dx0, mlp0, attn0, gain0 = backward_layer(
        kept0, dx1.astype(BF16).astype(F32), weights[0], gains[0], lengths, tables
    )

    def reduced(pairs):
        (in_rows, in_cols), (out_rows, out_cols) = pairs

        def term(k):
            part = slice(k * in_rows.shape[1] // 4, (k + 1) * in_rows.shape[1] // 4)
            return jnp.concatenate(
                [mm_rows(in_rows[:, part], in_cols), mm_rows(out_rows[:, part], out_cols)], 1
            ).astype(BF16)

        total = reduce_rows(term)
        if replicas > 1:
            groups = [[r * LINE + p for r in range(replicas)] for p in range(LINE)]
            total = lax.psum_scatter(total, "dp", scatter_dimension=0, tiled=True, axis_index_groups=groups)
        blocks = total.reshape(LINE, total.shape[0] // LINE, total.shape[1])
        got = line_exchange(blocks, place)
        order = [lax.rem(place - shift + LINE, LINE) for shift in range(LINE)]
        return got

    grads = []
    for pairs in ((mlp1, attn1), (mlp0, attn0)):
        grads.append([jnp.stack(reduced(part)) for part in pairs])
    (m1, a1), (m0, a0) = grads

    def place_order(pieces):
        index = jnp.array([0], jnp.int32)
        index = jnp.remainder(place - jnp.arange(LINE), LINE)
        return jnp.take(pieces, index, axis=0)

    def to_layer_core(zero, one):
        zero, one = place_order(zero), place_order(one)
        mine = jnp.where(first, zero, one)
        others = swap_cores(jnp.where(first, one, zero))
        both = jnp.stack([jnp.where(first, mine, others), jnp.where(first, others, mine)], 1)
        return both.reshape(KV_HEADS, both.shape[2], both.shape[3]).astype(F32)

    grad_attn = to_layer_core(a0, a1)
    grad_mlp = to_layer_core(m0, m1)

    def columns(values, lo, hi):
        part = values[:, :, lo:hi].transpose(1, 0, 2)
        return part.reshape(part.shape[0], -1)

    in_grad = jnp.concatenate(
        [
            columns(grad_attn, 0, Q_SLAB),
            columns(grad_attn, Q_SLAB, Q_SLAB + HEAD_DIM),
            columns(grad_attn, Q_SLAB + HEAD_DIM, QKV_SLAB),
            columns(grad_mlp, 0, FF_SLAB),
            columns(grad_mlp, FF_SLAB, 2 * FF_SLAB),
        ],
        1,
    )
    out_grad = jnp.concatenate(
        [columns(grad_attn, QKV_SLAB, QKV_SLAB + Q_SLAB), columns(grad_mlp, 2 * FF_SLAB, 3 * FF_SLAB)], 1
    )
    own_gains = jnp.where(first, gain0, gain1) + swap_cores(jnp.where(first, gain1, gain0))
    gain_rows = lax.psum_scatter(relative(own_gains, shard), ("shard", "dp"), scatter_dimension=1, tiled=True)
    dx0, y1 = dx0.astype(BF16), y1.astype(BF16)
    crossed = swap_cores(jnp.where(first, y1, dx0))
    ends_mine = jnp.where(first, dx0, crossed)
    ends_others = jnp.where(first, crossed, y1)
    ends_out = relative(jnp.concatenate([ends_mine, ends_others], 0), shard)
    return ends_out[None], in_grad[None], out_grad[None], gain_rows[None]


def solution(mesh):
    in_specs = (
        P("section", ("shard", "dp"), None),
        P("section", "shard", None),
        P("section", "shard", None),
        P("section", None, None),
        P(("shard", "dp")),
    )
    out_specs = (
        P("section", ("shard", "dp"), None),
        P("section", ("shard", "dp"), None),
        P("section", ("shard", "dp"), None),
        P("section", None, ("shard", "dp")),
    )
    return jax.shard_map(local, mesh=mesh, in_specs=in_specs, out_specs=out_specs, check_vma=False)
```

time: 3240 us -> 1310 us (0.40)
  waiting for transfers between devices: 2590 us -> 399 us
  Pallas kernels: 0 us -> 377 us
  matrix products: 421 us -> 122 us
  local copies, waits for them, and re-layouts: 60.1 us -> 186 us
  starting transfers between devices: 7.8 us -> 96.1 us
  other arithmetic: 138 us -> 90.6 us
    unnamed x8 -> x2, waiting for transfers between devices: 1550 us -> 73.3 us
    all_gather x2 -> x0, waiting for transfers between devices: 1030 us -> none  [the longest x1 675 us: local(): lax.all_gather(in_weight, 'shard', axis=1, tiled=True)]
    pallas_call x0 -> x16, Pallas kernels: none -> 377 us  [the longest x8 212 us: scatter_line(): pl.pallas_call(scatter_body, out_shape=jax.ShapeDtypeStruct((rows, width)...]
    ppermute x4 -> x52, waiting for transfers between devices: 2.71 us -> 326 us  [the longest x32 240 us: hop(): return lax.ppermute(value, 'shard', [(i, i ^ bit) for i in range(peers)])]
    dot_general x49 -> x60, matrix products: 421 us -> 122 us  [the longest x32 49.5 us: mm_rows(): lax.dot_general(a, b, (((0,), (0,)), ((), ())), preferred_element_type=F32)]
    ppermute x4 -> x52, starting transfers between devices: 7.6 us -> 96.1 us  [the longest x12 64.5 us: line_exchange(): lax.ppermute(lax.dynamic_index_in_dim(blocks, to, 0, False), 'dp', line_p...]
    concatenate x14 -> x27, other arithmetic: 83.2 us -> 19.6 us  [the longest x4 6.29 us: reduce_rows(): jnp.concatenate([second[:half] + via_one, second[half:]], 0).astype(BF16)]
    unnamed x264 -> x349, local copies, waits for them, and re-layouts: 19.2 us -> 68.9 us
  transfers between devices with their start and end apart: 9 -> 53, of which waited for: 6 -> 15; matrix products, arithmetic and copies ran while one was open for 2% -> 14% of each run, Pallas kernels for 0% -> 16%
where the time goes in v1:
time: 1310 us; the launch traced here: 1300 us
  waiting for transfers between devices  399 us (30%)
  Pallas kernels  377 us (29%)
  local copies, waits for them, and re-layouts  186 us (14%)
  matrix products  122 us (9%)
  starting transfers between devices  96.1 us (7%)
  other arithmetic  90.6 us (7%)
  between operations  18.8 us (1%)
    ppermute x32, waiting for transfers between devices, hop(): return lax.ppermute(value, 'shard', [(i, i ^ bit) for i in range(peers)])  240 us
    pallas_call x8, Pallas kernels, scatter_line(): pl.pallas_call(scatter_body, out_shape=jax.ShapeDtypeStruct((rows, width)...  212 us
    pallas_call x8, Pallas kernels, gather_line(): pl.pallas_call(gather_body, out_shape=jax.ShapeDtypeStruct((blocks, rows,...  165 us
    ppermute x12, waiting for transfers between devices, line_exchange(): lax.ppermute(lax.dynamic_index_in_dim(blocks, to, 0, False), 'dp', line_p...  85.3 us
    unnamed x2, waiting for transfers between devices  73.3 us
    unnamed x349, local copies, waits for them, and re-layouts  68.9 us
    ppermute x12, starting transfers between devices, line_exchange(): lax.ppermute(lax.dynamic_index_in_dim(blocks, to, 0, False), 'dp', line_p...  64.5 us
    dot_general x32, matrix products, mm_rows(): lax.dot_general(a, b, (((0,), (0,)), ((), ())), preferred_element_type=F32)  49.5 us
  transfers between devices with their start and end apart: 53, of which 15 were waited for; matrix products, arithmetic and copies ran while one was open for 14% of the time, Pallas kernels for 16%

profile of v1, /device:TPU:20, one launch (start us, length us, event | category | flops | bytes accessed | tf_op | source)
XLA Modules:
  0.0 1295.8 jit_solution(16063634570951152003)
XLA Ops:
  7.3 4.9 dynamic-slice_bitcast_fusion.3
  21.0 6.1 all-reduce
  34.9 21.0 %gather_line.8 = bf16[8,64,2048]{2,1,0:T(8,128)(2,1)S(1)} custom-call(bf16[64,2048]{1,0:T(8,128)(2,1)S(1)} %fusion.88.x_ref), custom_call_target="tpu_custom_call" | custom-call | bytes 60000000 | tf_op jit(solution)/shard_map/gather_line/pallas_call | solution.py:131
  55.9 23.7 %gather_line.11 = bf16[8,64,2048]{2,1,0:T(8,128)(2,1)S(1)} custom-call(bf16[64,2048]{1,0:T(8,128)(2,1)S(1)} %get-tuple-element.106.x_ref), custom_call_target="tpu_custom_call" | custom-call | bytes 60000000 | tf_op jit(solution)/shard_map/gather_line/pallas_call | solution.py:131
  84.3 6.1 collective-permute-done.5
  95.3 7.2 constant_dynamic-update-slice_fusion.19
  124.4 25.8 %scatter_line.8 = f32[64,2048]{1,0:T(8,128)S(1)} custom-call(bf16[8,64,2048]{2,1,0:T(8,128)(2,1)S(1)} %bitcast.292), custom_call_target="tpu_custom_call" | custom-call | bytes 60000000 | tf_op jit(solution)/shard_map/scatter_line/pallas_call | solution.py:246
  151.2 19.8 %gather_line.9 = bf16[8,64,2048]{2,1,0:T(8,128)(2,1)S(1)} custom-call(bf16[64,2048]{1,0:T(8,128)(2,1)S(1)} %multiply_convert_fusion.9.x_ref), custom_call_target="tpu_custom_call" | custom-call | bytes 60000000 | tf_op jit(solution)/shard_map/gather_line/pallas_call | solution.py:131
  172.9 70.5 %collective-permute-done.15 = bf16[256,640]{1,0:T(8,128)(2,1)S(1)} collective-permute-done((bf16[256,640]{1,0:T(8,128)(2,1)S(1)}, bf16[256,640]{1,0:T(8,128)(2,1)S(1)}, u32[]{:S(2)}, u32[]{:S(2)}) %collective-permute-start.15) | collective-permute-done | bytes 327712 | tf_op jit(solution)/shard_map/ppermute | solution.py:266
  268.8 43.0 %collective-permute-done.10 = bf16[256,3072]{1,0:T(8,128)(2,1)S(1)} collective-permute-done((bf16[256,3072]{1,0:T(8,128)(2,1)S(1)}, bf16[256,3072]{1,0:T(8,128)(2,1)S(1)}, u32[]{:S(2)}, u32[]{:S(2)}) %collective-permute-start.10) | collective-permute-done | bytes 1572896 | tf_op jit(solution)/shard_map/ppermute | solution.py:266
  316.0 4.5 fusion.6
  325.0 32.1 %scatter_line.9 = f32[64,2048]{1,0:T(8,128)S(1)} custom-call(bf16[8,64,2048]{2,1,0:T(8,128)(2,1)S(1)} %bitcast.298), custom_call_target="tpu_custom_call" | custom-call | bytes 60000000 | tf_op jit(solution)/shard_map/scatter_line/pallas_call | solution.py:246
  357.5 19.3 %gather_line.10 = bf16[8,64,2048]{2,1,0:T(8,128)(2,1)S(1)} custom-call(bf16[64,2048]{1,0:T(8,128)(2,1)S(1)} %fusion.82.x_ref), custom_call_target="tpu_custom_call" | custom-call | bytes 60000000 | tf_op jit(solution)/shard_map/gather_line/pallas_call | solution.py:131
  405.6 25.8 %scatter_line.10 = f32[64,2048]{1,0:T(8,128)S(1)} custom-call(bf16[8,64,2048]{2,1,0:T(8,128)(2,1)S(1)} %bitcast.293), custom_call_target="tpu_custom_call" | custom-call | bytes 60000000 | tf_op jit(solution)/shard_map/scatter_line/pallas_call | solution.py:246
  431.7 20.2 %gather_line.12 = bf16[8,64,2048]{2,1,0:T(8,128)(2,1)S(1)} custom-call(bf16[64,2048]{1,0:T(8,128)(2,1)S(1)} %multiply_convert_fusion.8.x_ref), custom_call_target="tpu_custom_call" | custom-call | bytes 60000000 | tf_op jit(solution)/shard_map/gather_line/pallas_call | solution.py:131
  458.1 7.1 fusion.2
  469.7 6.3 fusion.33
  476.1 25.9 %scatter_line.11 = f32[64,2048]{1,0:T(8,128)S(1)} custom-call(bf16[8,64,2048]{2,1,0:T(8,128)(2,1)S(1)} %bitcast.299), custom_call_target="tpu_custom_call" | custom-call | bytes 60000000 | tf_op jit(solution)/shard_map/scatter_line/pallas_call | solution.py:246
  503.8 20.3 %gather_line.13 = bf16[8,64,2048]{2,1,0:T(8,128)(2,1)S(1)} custom-call(bf16[64,2048]{1,0:T(8,128)(2,1)S(1)} %get-tuple-element.30.x_ref), custom_call_target="tpu_custom_call" | custom-call | bytes 60000000 | tf_op jit(solution)/shard_map/gather_line/pallas_call | solution.py:131
  543.2 26.2 %scatter_line.12 = f32[64,2048]{1,0:T(8,128)S(1)} custom-call(bf16[8,64,2048]{2,1,0:T(8,128)(2,1)S(1)} %bitcast.296), custom_call_target="tpu_custom_call" | custom-call | bytes 60000000 | tf_op jit(solution)/shard_map/scatter_line/pallas_call | solution.py:246
  570.4 20.6 %gather_line.14 = bf16[8,64,2048]{2,1,0:T(8,128)(2,1)S(1)} custom-call(bf16[64,2048]{1,0:T(8,128)(2,1)S(1)} %fusion.87.x_ref), custom_call_target="tpu_custom_call" | custom-call | bytes 60000000 | tf_op jit(solution)/shard_map/gather_line/pallas_call | solution.py:131
  591.0 5.9 multiply_convert_fusion.2
  598.0 4.8 fusion.30
  602.8 26.1 %scatter_line.13 = f32[64,2048]{1,0:T(8,128)S(1)} custom-call(bf16[8,64,2048]{2,1,0:T(8,128)(2,1)S(1)} %bitcast.297), custom_call_target="tpu_custom_call" | custom-call | bytes 60000000 | tf_op jit(solution)/shard_map/scatter_line/pallas_call | solution.py:246
  630.0 20.3 %gather_line.15 = bf16[8,64,2048]{2,1,0:T(8,128)(2,1)S(1)} custom-call(bf16[64,2048]{1,0:T(8,128)(2,1)S(1)} %fusion.165.x_ref), custom_call_target="tpu_custom_call" | custom-call | bytes 60000000 | tf_op jit(solution)/shard_map/gather_line/pallas_call | solution.py:131
  723.4 5.0 fusion.27
  728.5 25.7 %scatter_line.14 = f32[64,2048]{1,0:T(8,128)S(1)} custom-call(bf16[8,64,2048]{2,1,0:T(8,128)(2,1)S(1)} %bitcast.295), custom_call_target="tpu_custom_call" | custom-call | bytes 60000000 | tf_op jit(solution)/shard_map/scatter_line/pallas_call | solution.py:246
  760.7 24.3 %scatter_line.15 = f32[64,2048]{1,0:T(8,128)S(1)} custom-call(bf16[8,64,2048]{2,1,0:T(8,128)(2,1)S(1)} %bitcast.294), custom_call_target="tpu_custom_call" | custom-call | bytes 60000000 | tf_op jit(solution)/shard_map/scatter_line/pallas_call | solution.py:246
  787.4 5.2 collective-permute-done.45
  799.7 26.6 %collective-permute-done.38 = bf16[256,3072]{1,0:T(8,128)(2,1)S(1)} collective-permute-done((bf16[256,3072]{1,0:T(8,128)(2,1)S(1)}, bf16[256,3072]{1,0:T(8,128)(2,1)S(1)}, u32[]{:S(2)}, u32[]{:S(2)}) %collective-permute-start.38) | collective-permute-done | bytes 1572896 | tf_op jit(solution)/shard_map/ppermute | solution.py:266
  834.9 5.0 collective-permute-done.21
  841.4 66.4 %collective-permute-done.23 = bf16[256,640]{0,1:T(8,128)(2,1)S(1)} collective-permute-done((bf16[256,640]{0,1:T(8,128)(2,1)S(1)}, bf16[256,640]{0,1:T(8,128)(2,1)S(1)}, u32[]{:S(2)}, u32[]{:S(2)}) %collective-permute-start.23) | collective-permute-done | bytes 327712 | tf_op jit(solution)/shard_map/ppermute | solution.py:266
  911.7 73.3 %reduce-scatter.4.cloned.1.call-done = f32[128,2]{1,0:T(8,128)} async-done(((f32[2048,2]{1,0:T(8,128)}), f32[128,2]{1,0:T(8,128)}) %reduce-scatter.4.cloned.1.call-update) | async-done | bytes 1040
  992.5 12.2 collective-permute-done.31
  1016.9 12.4 collective-permute-start.47
  1038.5 16.3 %collective-permute-done.47 = bf16[128,3072]{1,0:T(8,128)(2,1)S(1)} collective-permute-done((bf16[128,3072]{1,0:T(8,128)(2,1)S(1)}, bf16[128,3072]{1,0:T(8,128)(2,1)S(1)}, u32[]{:S(2)}, u32[]{:S(2)}) %collective-permute-start.47) | collective-permute-done | bytes 786464 | tf_op jit(solution)/shard_map/ppermute | solution.py:458
  1060.7 21.3 %collective-permute-done.48 = bf16[128,3072]{1,0:T(8,128)(2,1)} collective-permute-done((bf16[128,3072]{1,0:T(8,128)(2,1)}, bf16[128,3072]{1,0:T(8,128)(2,1)}, u32[]{:S(2)}, u32[]{:S(2)}) %collective-permute-start.48) | collective-permute-done | bytes 786464 | tf_op jit(solution)/shard_map/ppermute | solution.py:458
  1082.0 41.4 %collective-permute-start.32 = (bf16[128,640]{1,0:T(8,128)(2,1)}, bf16[128,640]{1,0:T(8,128)(2,1)S(1)}, u32[]{:S(2)}, u32[]{:S(2)}) collective-permute-start(bf16[128,640]{1,0:T(8,128)(2,1)} %get-tuple-element.110), channel_id=1, source_target_pairs={{0,1},{1,2},{2,3},{3,0},{4,5},{5,6},{6,7},{7,4},{8,9},{9,10},{10,1... | collective-permute-start | bytes 491528 | tf_op jit(solution)/shard_map/ppermute | solution.py:458
  1126.4 27.3 %collective-permute-done.41 = bf16[128,3072]{1,0:T(8,128)(2,1)} collective-permute-done((bf16[128,3072]{1,0:T(8,128)(2,1)}, bf16[128,3072]{1,0:T(8,128)(2,1)}, u32[]{:S(2)}, u32[]{:S(2)}) %collective-permute-start.41) | collective-permute-done | bytes 786464 | tf_op jit(solution)/shard_map/ppermute | solution.py:458
  1153.7 20.4 %collective-permute-done.42 = bf16[128,3072]{1,0:T(8,128)(2,1)} collective-permute-done((bf16[128,3072]{1,0:T(8,128)(2,1)}, bf16[128,3072]{1,0:T(8,128)(2,1)}, u32[]{:S(2)}, u32[]{:S(2)}) %collective-permute-start.42) | collective-permute-done | bytes 786464 | tf_op jit(solution)/shard_map/ppermute | solution.py:458
  1227.8 6.6 bitcast_convert_fusion
  1234.4 10.1 slice_bitcast_fusion
  1244.5 5.4 copy.196
  1254.2 5.9 copy.198
  1260.0 5.3 copy.193
  1265.3 5.3 copy.194
  1270.7 4.6 constant_dynamic-update-slice_fusion.21
  1277.5 11.3 copy.197
  (666 shorter events, 346.3 us)
Async XLA Ops:
  7.2 977.9 %reduce-scatter.4.cloned.1.call-start = ((), (), s32[]{:S(2)}) async-start(), calls=%async_computation.1 | async-start | bytes 1114112
  13.9 81.4 %collective-permute-start.7 = (bf16[512,3072]{1,0:T(8,128)(2,1)}, bf16[512,3072]{1,0:T(8,128)(2,1)}, u32[]{:S(2)}, u32[]{:S(2)}) collective-permute-start(bf16[512,3072]{1,0:T(8,128)(2,1)} %pad_maximum_fusion.2), channel_id=1, source_target_pairs={{0,16},{16,0},{1,17},{17,1},{2,18},{18,2},{3,19},{19,3},{4,20},{20... | collective-permute-start | bytes 9437192 | tf_op jit(solution)/shard_map/ppermute | solution.py:261
  16.9 13.3 %collective-permute-start.2 = (bf16[512,640]{1,0:T(8,128)(2,1)S(1)}, bf16[512,640]{1,0:T(8,128)(2,1)S(1)}, u32[]{:S(2)}, u32[]{:S(2)}) collective-permute-start(bf16[512,640]{1,0:T(8,128)(2,1)S(1)} %pad_maximum_fusion.14), channel_id=1, source_target_pairs={{0,16},{16,0},{1,17},{17,1},{2,18},{18,2},{3,19},{19,3},{4,20},{20... | collective-permute-start | bytes 1966088 | tf_op jit(solution)/shard_map/ppermute | solution.py:261
  17.4 11.9 collective-permute-start.1
  17.7 12.3 collective-permute-start
  30.7 50.5 %collective-permute-start.3 = (bf16[512,640]{1,0:T(8,128)(2,1)S(1)}, bf16[512,640]{1,0:T(8,128)(2,1)S(1)}, u32[]{:S(2)}, u32[]{:S(2)}) collective-permute-start(bf16[512,640]{1,0:T(8,128)(2,1)S(1)} %get-tuple-element.97), channel_id=1, source_target_pairs={{0,4},{4,0},{8,12},{12,8},{1,5},{5,1},{9,13},{13,9},{2,6},{6,2},{1... | collective-permute-start | bytes 1966088 | tf_op jit(solution)/shard_map/ppermute | solution.py:266
  32.2 47.4 %collective-permute-start.4 = (bf16[512,640]{1,0:T(8,128)(2,1)S(1)}, bf16[512,640]{1,0:T(8,128)(2,1)S(1)}, u32[]{:S(2)}, u32[]{:S(2)}) collective-permute-start(bf16[512,640]{1,0:T(8,128)(2,1)S(1)} %get-tuple-element.97), channel_id=1, source_target_pairs={{0,8},{4,12},{8,0},{12,4},{1,9},{5,13},{9,1},{13,5},{2,10},{6,14},... | collective-permute-start | bytes 1966088 | tf_op jit(solution)/shard_map/ppermute | solution.py:266
  32.7 50.4 %collective-permute-start.12 = (bf16[512,640]{1,0:T(8,128)(2,1)S(1)}, bf16[512,640]{1,0:T(8,128)(2,1)S(1)}, u32[]{:S(2)}, u32[]{:S(2)}) collective-permute-start(bf16[512,640]{1,0:T(8,128)(2,1)S(1)} %get-tuple-element.35), channel_id=1, source_target_pairs={{0,4},{4,0},{8,12},{12,8},{1,5},{5,1},{9,13},{13,9},{2,6},{6,2},{1... | collective-permute-start | bytes 1966088 | tf_op jit(solution)/shard_map/ppermute | solution.py:266
  32.8 49.0 %collective-permute-start.13 = (bf16[512,640]{1,0:T(8,128)(2,1)S(1)}, bf16[512,640]{1,0:T(8,128)(2,1)S(1)}, u32[]{:S(2)}, u32[]{:S(2)}) collective-permute-start(bf16[512,640]{1,0:T(8,128)(2,1)S(1)} %get-tuple-element.35), channel_id=1, source_target_pairs={{0,8},{4,12},{8,0},{12,4},{1,9},{5,13},{9,1},{13,5},{2,10},{6,14},... | collective-permute-start | bytes 1966088 | tf_op jit(solution)/shard_map/ppermute | solution.py:266
  82.5 67.9 %collective-permute-start.14 = (bf16[256,640]{1,0:T(8,128)(2,1)}, bf16[256,640]{1,0:T(8,128)(2,1)}, u32[]{:S(2)}, u32[]{:S(2)}) collective-permute-start(bf16[256,640]{1,0:T(8,128)(2,1)} %slice.460), channel_id=1, source_target_pairs={{0,4},{4,0},{8,12},{12,8},{1,5},{5,1},{9,13},{13,9},{2,6},{6,2},{1... | collective-permute-start | bytes 983048 | tf_op jit(solution)/shard_map/ppermute | solution.py:266
  102.5 145.9 %collective-permute-start.16 = (bf16[512,3072]{1,0:T(8,128)(2,1)}, bf16[512,3072]{1,0:T(8,128)(2,1)}, u32[]{:S(2)}, u32[]{:S(2)}) collective-permute-start(bf16[512,3072]{1,0:T(8,128)(2,1)} %get-tuple-element.41), channel_id=1, source_target_pairs={{0,4},{4,0},{8,12},{12,8},{1,5},{5,1},{9,13},{13,9},{2,6},{6,2},{1... | collective-permute-start | bytes 9437192 | tf_op jit(solution)/shard_map/ppermute | solution.py:266
  104.0 140.2 %collective-permute-start.17 = (bf16[512,3072]{1,0:T(8,128)(2,1)}, bf16[512,3072]{1,0:T(8,128)(2,1)}, u32[]{:S(2)}, u32[]{:S(2)}) collective-permute-start(bf16[512,3072]{1,0:T(8,128)(2,1)} %get-tuple-element.41), channel_id=1, source_target_pairs={{0,8},{4,12},{8,0},{12,4},{1,9},{5,13},{9,1},{13,5},{2,10},{6,14},... | collective-permute-start | bytes 9437192 | tf_op jit(solution)/shard_map/ppermute | solution.py:266
  104.5 149.5 %collective-permute-start.8 = (bf16[512,3072]{1,0:T(8,128)(2,1)}, bf16[512,3072]{1,0:T(8,128)(2,1)}, u32[]{:S(2)}, u32[]{:S(2)}) collective-permute-start(bf16[512,3072]{1,0:T(8,128)(2,1)} %get-tuple-element.72), channel_id=1, source_target_pairs={{0,4},{4,0},{8,12},{12,8},{1,5},{5,1},{9,13},{13,9},{2,6},{6,2},{1... | collective-permute-start | bytes 9437192 | tf_op jit(solution)/shard_map/ppermute | solution.py:266
  105.0 146.6 %collective-permute-start.9 = (bf16[512,3072]{1,0:T(8,128)(2,1)}, bf16[512,3072]{1,0:T(8,128)(2,1)}, u32[]{:S(2)}, u32[]{:S(2)}) collective-permute-start(bf16[512,3072]{1,0:T(8,128)(2,1)} %get-tuple-element.72), channel_id=1, source_target_pairs={{0,8},{4,12},{8,0},{12,4},{1,9},{5,13},{9,1},{13,5},{2,10},{6,14},... | collective-permute-start | bytes 9437192 | tf_op jit(solution)/shard_map/ppermute | solution.py:266
  150.5 92.9 %collective-permute-start.15 = (bf16[256,640]{1,0:T(8,128)(2,1)S(1)}, bf16[256,640]{1,0:T(8,128)(2,1)S(1)}, u32[]{:S(2)}, u32[]{:S(2)}) collective-permute-start(bf16[256,640]{1,0:T(8,128)(2,1)S(1)} %copy-done.102), channel_id=1, source_target_pairs={{0,8},{4,12},{8,0},{12,4},{1,9},{5,13},{9,1},{13,5},{2,10},{6,14},... | collective-permute-start | bytes 983048 | tf_op jit(solution)/shard_map/ppermute | solution.py:266
  247.0 205.0 %collective-permute-start.18 = (bf16[256,3072]{1,0:T(8,128)(2,1)}, bf16[256,3072]{1,0:T(8,128)(2,1)}, u32[]{:S(2)}, u32[]{:S(2)}) collective-permute-start(bf16[256,3072]{1,0:T(8,128)(2,1)} %slice.467), channel_id=1, source_target_pairs={{0,4},{4,0},{8,12},{12,8},{1,5},{5,1},{9,13},{13,9},{2,6},{6,2},{1... | collective-permute-start | bytes 4718600 | tf_op jit(solution)/shard_map/ppermute | solution.py:266
  251.1 204.3 %collective-permute-start.19 = (bf16[256,3072]{1,0:T(8,128)(2,1)}, bf16[256,3072]{1,0:T(8,128)(2,1)}, u32[]{:S(2)}, u32[]{:S(2)}) collective-permute-start(bf16[256,3072]{1,0:T(8,128)(2,1)} %slice.468), channel_id=1, source_target_pairs={{0,8},{4,12},{8,0},{12,4},{1,9},{5,13},{9,1},{13,5},{2,10},{6,14},... | collective-permute-start | bytes 4718600 | tf_op jit(solution)/shard_map/ppermute | solution.py:266
  253.4 58.4 %collective-permute-start.10 = (bf16[256,3072]{1,0:T(8,128)(2,1)S(1)}, bf16[256,3072]{1,0:T(8,128)(2,1)S(1)}, u32[]{:S(2)}, u32[]{:S(2)}) collective-permute-start(bf16[256,3072]{1,0:T(8,128)(2,1)S(1)} %slice.453), channel_id=1, source_target_pairs={{0,4},{4,0},{8,12},{12,8},{1,5},{5,1},{9,13},{13,9},{2,6},{6,2},{1... | collective-permute-start | bytes 4718600 | tf_op jit(solution)/shard_map/ppermute | solution.py:266
  255.5 60.4 %collective-permute-start.11 = (bf16[256,3072]{1,0:T(8,128)(2,1)S(1)}, bf16[256,3072]{1,0:T(8,128)(2,1)S(1)}, u32[]{:S(2)}, u32[]{:S(2)}) collective-permute-start(bf16[256,3072]{1,0:T(8,128)(2,1)S(1)} %slice.454), channel_id=1, source_target_pairs={{0,8},{4,12},{8,0},{12,4},{1,9},{5,13},{9,1},{13,5},{2,10},{6,14},... | collective-permute-start | bytes 4718600 | tf_op jit(solution)/shard_map/ppermute | solution.py:266
  754.5 31.9 %collective-permute-start.51 = (f32[2,2048]{1,0:T(2,128)S(1)}, f32[2,2048]{1,0:T(2,128)S(1)}, u32[]{:S(2)}, u32[]{:S(2)}) collective-permute-start(f32[2,2048]{1,0:T(2,128)S(1)} %broadcast_select_fusion.34), channel_id=1, source_target_pairs={{0,16},{16,0},{1,17},{17,1},{2,18},{18,2},{3,19},{19,3},{4,20},{20... | collective-permute-start | bytes 49160 | tf_op jit(solution)/shard_map/ppermute | solution.py:261
  754.9 40.9 %collective-permute-start.43 = (bf16[256,3072]{1,0:T(8,128)(2,1)S(1)}, bf16[256,3072]{1,0:T(8,128)(2,1)S(1)}, u32[]{:S(2)}, u32[]{:S(2)}) collective-permute-start(bf16[256,3072]{1,0:T(8,128)(2,1)S(1)} %get-tuple-element.78), channel_id=1, source_target_pairs={{0,8},{4,12},{8,0},{12,4},{1,9},{5,13},{9,1},{13,5},{2,10},{6,14},... | collective-permute-start | bytes 4718600 | tf_op jit(solution)/shard_map/ppermute | solution.py:266
  755.4 37.2 %collective-permute-start.45 = (bf16[256,3072]{1,0:T(8,128)(2,1)S(1)}, bf16[256,3072]{1,0:T(8,128)(2,1)S(1)}, u32[]{:S(2)}, u32[]{:S(2)}) collective-permute-start(bf16[256,3072]{1,0:T(8,128)(2,1)S(1)} %get-tuple-element.79), channel_id=1, source_target_pairs={{0,4},{4,0},{8,12},{12,8},{1,5},{5,1},{9,13},{13,9},{2,6},{6,2},{1... | collective-permute-start | bytes 4718600 | tf_op jit(solution)/shard_map/ppermute | solution.py:266
  756.6 72.9 %collective-permute-start.36 = (bf16[256,3072]{1,0:T(8,128)(2,1)S(1)}, bf16[256,3072]{1,0:T(8,128)(2,1)S(1)}, u32[]{:S(2)}, u32[]{:S(2)}) collective-permute-start(bf16[256,3072]{1,0:T(8,128)(2,1)S(1)} %get-tuple-element.84), channel_id=1, source_target_pairs={{0,8},{4,12},{8,0},{12,4},{1,9},{5,13},{9,1},{13,5},{2,10},{6,14},... | collective-permute-start | bytes 4718600 | tf_op jit(solution)/shard_map/ppermute | solution.py:266
  757.6 68.8 %collective-permute-start.38 = (bf16[256,3072]{1,0:T(8,128)(2,1)S(1)}, bf16[256,3072]{1,0:T(8,128)(2,1)S(1)}, u32[]{:S(2)}, u32[]{:S(2)}) collective-permute-start(bf16[256,3072]{1,0:T(8,128)(2,1)S(1)} %get-tuple-element.85), channel_id=1, source_target_pairs={{0,4},{4,0},{8,12},{12,8},{1,5},{5,1},{9,13},{13,9},{2,6},{6,2},{1... | collective-permute-start | bytes 4718600 | tf_op jit(solution)/shard_map/ppermute | solution.py:266
  786.5 46.4 %collective-permute-start.28 = (bf16[256,640]{0,1:T(8,128)(2,1)S(1)}, bf16[256,640]{0,1:T(8,128)(2,1)S(1)}, u32[]{:S(2)}, u32[]{:S(2)}) collective-permute-start(bf16[256,640]{0,1:T(8,128)(2,1)S(1)} %get-tuple-element.111), channel_id=1, source_target_pairs={{0,8},{4,12},{8,0},{12,4},{1,9},{5,13},{9,1},{13,5},{2,10},{6,14},... | collective-permute-start | bytes 983048 | tf_op jit(solution)/shard_map/ppermute | solution.py:266
  792.7 41.0 %collective-permute-start.30 = (bf16[256,640]{0,1:T(8,128)(2,1)S(1)}, bf16[256,640]{0,1:T(8,128)(2,1)S(1)}, u32[]{:S(2)}, u32[]{:S(2)}) collective-permute-start(bf16[256,640]{0,1:T(8,128)(2,1)S(1)} %get-tuple-element.112), channel_id=1, source_target_pairs={{0,4},{4,0},{8,12},{12,8},{1,5},{5,1},{9,13},{13,9},{2,6},{6,2},{1... | collective-permute-start | bytes 983048 | tf_op jit(solution)/shard_map/ppermute | solution.py:266
  795.8 44.1 %collective-permute-start.21 = (bf16[256,640]{0,1:T(8,128)(2,1)S(1)}, bf16[256,640]{0,1:T(8,128)(2,1)S(1)}, u32[]{:S(2)}, u32[]{:S(2)}) collective-permute-start(bf16[256,640]{0,1:T(8,128)(2,1)S(1)} %get-tuple-element.117), channel_id=1, source_target_pairs={{0,8},{4,12},{8,0},{12,4},{1,9},{5,13},{9,1},{13,5},{2,10},{6,14},... | collective-permute-start | bytes 983048 | tf_op jit(solution)/shard_map/ppermute | solution.py:266
  826.4 183.0 %collective-permute-start.44 = (bf16[512,3072]{1,0:T(8,128)(2,1)}, bf16[512,3072]{1,0:T(8,128)(2,1)}, u32[]{:S(2)}, u32[]{:S(2)}) collective-permute-start(bf16[512,3072]{1,0:T(8,128)(2,1)} %pad_maximum_fusion.5), channel_id=1, source_target_pairs={{0,4},{4,0},{8,12},{12,8},{1,5},{5,1},{9,13},{13,9},{2,6},{6,2},{1... | collective-permute-start | bytes 9437192 | tf_op jit(solution)/shard_map/ppermute | solution.py:266
  829.5 181.4 %collective-permute-start.46 = (bf16[512,3072]{1,0:T(8,128)(2,1)}, bf16[512,3072]{1,0:T(8,128)(2,1)}, u32[]{:S(2)}, u32[]{:S(2)}) collective-permute-start(bf16[512,3072]{1,0:T(8,128)(2,1)} %fusion.23), channel_id=1, source_target_pairs={{0,8},{4,12},{8,0},{12,4},{1,9},{5,13},{9,1},{13,5},{2,10},{6,14},... | collective-permute-start | bytes 9437192 | tf_op jit(solution)/shard_map/ppermute | solution.py:266
  832.9 74.9 %collective-permute-start.23 = (bf16[256,640]{0,1:T(8,128)(2,1)S(1)}, bf16[256,640]{0,1:T(8,128)(2,1)S(1)}, u32[]{:S(2)}, u32[]{:S(2)}) collective-permute-start(bf16[256,640]{0,1:T(8,128)(2,1)S(1)} %get-tuple-element.118), channel_id=1, source_target_pairs={{0,4},{4,0},{8,12},{12,8},{1,5},{5,1},{9,13},{13,9},{2,6},{6,2},{1... | collective-permute-start | bytes 983048 | tf_op jit(solution)/shard_map/ppermute | solution.py:266
  833.6 195.6 %collective-permute-start.37 = (bf16[512,3072]{1,0:T(8,128)(2,1)S(1)}, bf16[512,3072]{1,0:T(8,128)(2,1)}, u32[]{:S(2)}, u32[]{:S(2)}) collective-permute-start(bf16[512,3072]{1,0:T(8,128)(2,1)S(1)} %pad_maximum_fusion.3), channel_id=1, source_target_pairs={{0,4},{4,0},{8,12},{12,8},{1,5},{5,1},{9,13},{13,9},{2,6},{6,2},{1... | collective-permute-start | bytes 9437192 | tf_op jit(solution)/shard_map/ppermute | solution.py:266
  839.9 189.6 %collective-permute-start.39 = (bf16[512,3072]{1,0:T(8,128)(2,1)}, bf16[512,3072]{1,0:T(8,128)(2,1)}, u32[]{:S(2)}, u32[]{:S(2)}) collective-permute-start(bf16[512,3072]{1,0:T(8,128)(2,1)} %fusion.21), channel_id=1, source_target_pairs={{0,8},{4,12},{8,0},{12,4},{1,9},{5,13},{9,1},{13,5},{2,10},{6,14},... | collective-permute-start | bytes 9437192 | tf_op jit(solution)/shard_map/ppermute | solution.py:266
  907.8 81.0 %collective-permute-start.29 = (bf16[512,640]{0,1:T(8,128)(2,1)}, bf16[512,640]{0,1:T(8,128)(2,1)}, u32[]{:S(2)}, u32[]{:S(2)}) collective-permute-start(bf16[512,640]{0,1:T(8,128)(2,1)} %pad_maximum_fusion.17), channel_id=1, source_target_pairs={{0,4},{4,0},{8,12},{12,8},{1,5},{5,1},{9,13},{13,9},{2,6},{6,2},{1... | collective-permute-start | bytes 1966088 | tf_op jit(solution)/shard_map/ppermute | solution.py:266
  988.9 15.8 %collective-permute-start.31 = (bf16[512,640]{0,1:T(8,128)(2,1)S(1)}, bf16[512,640]{0,1:T(8,128)(2,1)S(1)}, u32[]{:S(2)}, u32[]{:S(2)}) collective-permute-start(bf16[512,640]{0,1:T(8,128)(2,1)S(1)} %fusion.77), channel_id=1, source_target_pairs={{0,8},{4,12},{8,0},{12,4},{1,9},{5,13},{9,1},{13,5},{2,10},{6,14},... | collective-permute-start | bytes 1966088 | tf_op jit(solution)/shard_map/ppermute | solution.py:266
  1004.7 32.9 %collective-permute-start.22 = (bf16[512,640]{0,1:T(8,128)(2,1)}, bf16[512,640]{0,1:T(8,128)(2,1)}, u32[]{:S(2)}, u32[]{:S(2)}) collective-permute-start(bf16[512,640]{0,1:T(8,128)(2,1)} %pad_maximum_fusion.15), channel_id=1, source_target_pairs={{0,4},{4,0},{8,12},{12,8},{1,5},{5,1},{9,13},{13,9},{2,6},{6,2},{1... | collective-permute-start | bytes 1966088 | tf_op jit(solution)/shard_map/ppermute | solution.py:266
  1009.4 29.1 %collective-permute-start.24 = (bf16[512,640]{0,1:T(8,128)(2,1)}, bf16[512,640]{0,1:T(8,128)(2,1)S(1)}, u32[]{:S(2)}, u32[]{:S(2)}) collective-permute-start(bf16[512,640]{0,1:T(8,128)(2,1)} %fusion.75), channel_id=1, source_target_pairs={{0,8},{4,12},{8,0},{12,4},{1,9},{5,13},{9,1},{13,5},{2,10},{6,14},... | collective-permute-start | bytes 1966088 | tf_op jit(solution)/shard_map/ppermute | solution.py:266
  1016.9 37.9 %collective-permute-start.47 = (bf16[128,3072]{1,0:T(8,128)(2,1)S(1)}, bf16[128,3072]{1,0:T(8,128)(2,1)S(1)}, u32[]{:S(2)}, u32[]{:S(2)}) collective-permute-start(bf16[128,3072]{1,0:T(8,128)(2,1)S(1)} %get-tuple-element.77), channel_id=1, source_target_pairs={{0,1},{1,2},{2,3},{3,0},{4,5},{5,6},{6,7},{7,4},{8,9},{9,10},{10,1... | collective-permute-start | bytes 2359304 | tf_op jit(solution)/shard_map/ppermute | solution.py:458
  1029.2 52.8 %collective-permute-start.48 = (bf16[128,3072]{1,0:T(8,128)(2,1)}, bf16[128,3072]{1,0:T(8,128)(2,1)}, u32[]{:S(2)}, u32[]{:S(2)}) collective-permute-start(bf16[128,3072]{1,0:T(8,128)(2,1)} %get-tuple-element.76), channel_id=1, source_target_pairs={{0,2},{1,3},{2,0},{3,1},{4,6},{5,7},{6,4},{7,5},{8,10},{9,11},{10,... | collective-permute-start | bytes 2359304 | tf_op jit(solution)/shard_map/ppermute | solution.py:458
  1029.5 93.9 %collective-permute-start.49 = (bf16[128,3072]{1,0:T(8,128)(2,1)}, bf16[128,3072]{1,0:T(8,128)(2,1)}, u32[]{:S(2)}, u32[]{:S(2)}) collective-permute-start(bf16[128,3072]{1,0:T(8,128)(2,1)} %get-tuple-element.75), channel_id=1, source_target_pairs={{0,3},{1,0},{2,1},{3,2},{4,7},{5,4},{6,5},{7,6},{8,11},{9,8},{10,9... | collective-permute-start | bytes 2359304 | tf_op jit(solution)/shard_map/ppermute | solution.py:458
  1037.5 116.2 %collective-permute-start.41 = (bf16[128,3072]{1,0:T(8,128)(2,1)}, bf16[128,3072]{1,0:T(8,128)(2,1)}, u32[]{:S(2)}, u32[]{:S(2)}) collective-permute-start(bf16[128,3072]{1,0:T(8,128)(2,1)} %get-tuple-element.82), channel_id=1, source_target_pairs={{0,2},{1,3},{2,0},{3,1},{4,6},{5,7},{6,4},{7,5},{8,10},{9,11},{10,... | collective-permute-start | bytes 2359304 | tf_op jit(solution)/shard_map/ppermute | solution.py:458
  1038.5 135.6 %collective-permute-start.42 = (bf16[128,3072]{1,0:T(8,128)(2,1)}, bf16[128,3072]{1,0:T(8,128)(2,1)}, u32[]{:S(2)}, u32[]{:S(2)}) collective-permute-start(bf16[128,3072]{1,0:T(8,128)(2,1)} %get-tuple-element.81), channel_id=1, source_target_pairs={{0,3},{1,0},{2,1},{3,2},{4,7},{5,4},{6,5},{7,6},{8,11},{9,8},{10,9... | collective-permute-start | bytes 2359304 | tf_op jit(solution)/shard_map/ppermute | solution.py:458
  1054.8 119.3 %collective-permute-start.40 = (bf16[128,3072]{1,0:T(8,128)(2,1)}, bf16[128,3072]{1,0:T(8,128)(2,1)}, u32[]{:S(2)}, u32[]{:S(2)}) collective-permute-start(bf16[128,3072]{1,0:T(8,128)(2,1)} %get-tuple-element.83), channel_id=1, source_target_pairs={{0,1},{1,2},{2,3},{3,0},{4,5},{5,6},{6,7},{7,4},{8,9},{9,10},{10,1... | collective-permute-start | bytes 2359304 | tf_op jit(solution)/shard_map/ppermute | solution.py:458
  1082.0 106.1 %collective-permute-start.32 = (bf16[128,640]{1,0:T(8,128)(2,1)}, bf16[128,640]{1,0:T(8,128)(2,1)S(1)}, u32[]{:S(2)}, u32[]{:S(2)}) collective-permute-start(bf16[128,640]{1,0:T(8,128)(2,1)} %get-tuple-element.110), channel_id=1, source_target_pairs={{0,1},{1,2},{2,3},{3,0},{4,5},{5,6},{6,7},{7,4},{8,9},{9,10},{10,1... | collective-permute-start | bytes 491528 | tf_op jit(solution)/shard_map/ppermute | solution.py:458
  1123.4 69.0 %collective-permute-start.33 = (bf16[128,640]{1,0:T(8,128)(2,1)}, bf16[128,640]{1,0:T(8,128)(2,1)S(1)}, u32[]{:S(2)}, u32[]{:S(2)}) collective-permute-start(bf16[128,640]{1,0:T(8,128)(2,1)} %get-tuple-element.109), channel_id=1, source_target_pairs={{0,2},{1,3},{2,0},{3,1},{4,6},{5,7},{6,4},{7,5},{8,10},{9,11},{10,... | collective-permute-start | bytes 491528 | tf_op jit(solution)/shard_map/ppermute | solution.py:458
  1153.7 38.7 %collective-permute-start.34 = (bf16[128,640]{1,0:T(8,128)(2,1)}, bf16[128,640]{1,0:T(8,128)(2,1)}, u32[]{:S(2)}, u32[]{:S(2)}) collective-permute-start(bf16[128,640]{1,0:T(8,128)(2,1)} %get-tuple-element.108), channel_id=1, source_target_pairs={{0,3},{1,0},{2,1},{3,2},{4,7},{5,4},{6,5},{7,6},{8,11},{9,8},{10,9... | collective-permute-start | bytes 491528 | tf_op jit(solution)/shard_map/ppermute | solution.py:458
  1174.1 23.2 %collective-permute-start.25 = (bf16[128,640]{1,0:T(8,128)(2,1)}, bf16[128,640]{1,0:T(8,128)(2,1)}, u32[]{:S(2)}, u32[]{:S(2)}) collective-permute-start(bf16[128,640]{1,0:T(8,128)(2,1)} %get-tuple-element.116), channel_id=1, source_target_pairs={{0,1},{1,2},{2,3},{3,0},{4,5},{5,6},{6,7},{7,4},{8,9},{9,10},{10,1... | collective-permute-start | bytes 491528 | tf_op jit(solution)/shard_map/ppermute | solution.py:458
  1174.1 23.2 %collective-permute-start.26 = (bf16[128,640]{1,0:T(8,128)(2,1)}, bf16[128,640]{1,0:T(8,128)(2,1)}, u32[]{:S(2)}, u32[]{:S(2)}) collective-permute-start(bf16[128,640]{1,0:T(8,128)(2,1)} %get-tuple-element.115), channel_id=1, source_target_pairs={{0,2},{1,3},{2,0},{3,1},{4,6},{5,7},{6,4},{7,5},{8,10},{9,11},{10,... | collective-permute-start | bytes 491528 | tf_op jit(solution)/shard_map/ppermute | solution.py:458
  1192.4 32.6 %collective-permute-start.50 = (bf16[4,128,3072]{2,1,0:T(8,128)(2,1)}, bf16[4,128,3072]{2,1,0:T(8,128)(2,1)}, u32[]{:S(2)}, u32[]{:S(2)}) collective-permute-start(bf16[4,128,3072]{2,1,0:T(8,128)(2,1)} %broadcast_select_fusion.2), channel_id=1, source_target_pairs={{0,16},{16,0},{1,17},{17,1},{2,18},{18,2},{3,19},{19,3},{4,20},{20... | collective-permute-start | bytes 9437192 | tf_op jit(solution)/shard_map/ppermute | solution.py:261
  (166 other events, 2823.6 us)
Sparse Core Ops, SparseCore 0:
  910.1 74.9 reduce-scatter.3

commit v2 on v1

--- a/solution.py
+++ b/solution.py
@@ -17,6 +17,8 @@
 F32 = jnp.float32
 CORES = 2
 LINE = KV_HEADS // CORES
+SHARDS = 4
+SLOT = 64
 Q_SLAB = GROUP * HEAD_DIM
 QKV_SLAB = Q_SLAB + 2 * HEAD_DIM
 FF_SLAB = FF // KV_HEADS
@@ -49,32 +51,32 @@
 def gather_body(x_ref, o_ref, up_send, dn_send, sib_send, z_recv, sib_recv):
     core, depth, place = line_place()
     greet(core, depth, place)
-    own = place * CORES + core
+    own = core * LINE + place
     o_ref[own] = x_ref[...]
 
     def up(where):
-        index = where * CORES + core
+        index = core * LINE + where
         return pltpu.make_async_remote_copy(
             o_ref.at[index], o_ref.at[index], up_send.at[where], z_recv.at[where],
             device_id={"dp": depth + 1},
         )
 
     def down(where):
-        index = where * CORES + core
+        index = core * LINE + where
         return pltpu.make_async_remote_copy(
             o_ref.at[index], o_ref.at[index], dn_send.at[where], z_recv.at[where],
             device_id={"dp": depth - 1},
         )
 
     def across(where):
-        index = where * CORES + core
+        index = core * LINE + where
         return pltpu.make_async_remote_copy(
             o_ref.at[index], o_ref.at[index], sib_send.at[where], sib_recv.at[where],
             device_id={"section": 1 - core},
         )
 
     def arrived(where, other):
-        index = where * CORES + other
+        index = other * LINE + where
         sem = z_recv if other is core else sib_recv
         return pltpu.make_async_remote_copy(
             o_ref.at[index], o_ref.at[index], up_send.at[where], sem.at[where],
@@ -135,7 +137,7 @@
         out_specs=pl.BlockSpec(memory_space=pltpu.VMEM),
         scratch_shapes=[sems] * 5,
         compiler_params=pltpu.CompilerParams(
-            collective_id=0, has_side_effects=True, vmem_limit_bytes=16 * 2**20
+            collective_id=1, has_side_effects=True, vmem_limit_bytes=16 * 2**20
         ),
         name="gather_line",
         cost_estimate=pl.CostEstimate(flops=0, bytes_accessed=60_000_000, transcendentals=0),
@@ -150,7 +152,7 @@
 
     def across(where):
         return pltpu.make_async_remote_copy(
-            p_ref.at[where * CORES + 1 - core], sib_buf.at[where],
+            p_ref.at[(1 - core) * LINE + where], sib_buf.at[where],
             sib_send.at[where], sib_recv.at[where], device_id={"section": 1 - core},
         )
 
@@ -167,7 +169,7 @@
         )
 
     def summed(where):
-        return p_ref[where * CORES + core].astype(F32) + sib_buf[where].astype(F32)
+        return p_ref[core * LINE + where].astype(F32) + sib_buf[where].astype(F32)
 
     for step in range(LINE - 1, 0, -1):
         @pl.when(place + step < LINE)
@@ -250,11 +252,592 @@
         out_specs=pl.BlockSpec(memory_space=pltpu.VMEM),
         scratch_shapes=[buffer] * 5 + [sems] * 6,
         compiler_params=pltpu.CompilerParams(
-            collective_id=1, has_side_effects=True, vmem_limit_bytes=24 * 2**20
+            collective_id=2, has_side_effects=True, vmem_limit_bytes=24 * 2**20
         ),
         name="scatter_line",
         cost_estimate=pl.CostEstimate(flops=0, bytes_accessed=60_000_000, transcendentals=0),
     )(partial.reshape(blocks, rows, width))
+
+
+class Here:
+    def __init__(self):
+        self.core = lax.axis_index("section")
+        self.shard = lax.axis_index("shard")
+        self.depth = lax.axis_index("dp")
+        self.place = lax.rem(self.depth, LINE)
+        self.twin = {"section": 1 - self.core}
+        self.x_shard = self.shard + 1 - 2 * lax.rem(self.shard, 2)
+        self.y_shard = lax.rem(self.shard + 2, SHARDS)
+        self.far_shard = SHARDS - 1 - self.shard
+        self.x_peer = {"shard": self.x_shard}
+        self.y_peer = {"shard": self.y_shard}
+        self.above = {"dp": self.depth + 1}
+        self.below = {"dp": self.depth - 1}
+        self.has_above = self.place < LINE - 1
+        self.has_below = self.place > 0
+
+    def greet(self):
+        barrier = pltpu.get_barrier_semaphore()
+        for peer in (self.twin, self.x_peer, self.y_peer):
+            pl.semaphore_signal(barrier, inc=1, device_id=peer)
+
+        @pl.when(self.has_above)
+        def _():
+            pl.semaphore_signal(barrier, inc=1, device_id=self.above)
+
+        @pl.when(self.has_below)
+        def _():
+            pl.semaphore_signal(barrier, inc=1, device_id=self.below)
+
+        pl.semaphore_wait(barrier, jnp.where(self.has_above & self.has_below, 5, 4))
+
+
+def remote(src, dst, send, recv, device):
+    return pltpu.make_async_remote_copy(src, dst, send, recv, device_id=device)
+
+
+def rows_at(ref, start, size):
+    return ref.at[pl.ds(pl.multiple_of(start, size), size)]
+
+
+def line_gather(here, buf, sems, meanwhile=()):
+    up_send, dn_send, sib_send, z_recv, sib_recv = sems
+    rows = buf.shape[0] // (LINE * CORES)
+    core, place = here.core, here.place
+    meanwhile = list(meanwhile) + [None] * LINE
+
+    def part(where, whose):
+        return rows_at(buf, (whose * LINE + where) * rows, rows)
+
+    def up(where):
+        mine = part(where, core)
+        return remote(mine, mine, up_send.at[where], z_recv.at[where], here.above)
+
+    def down(where):
+        mine = part(where, core)
+        return remote(mine, mine, dn_send.at[where], z_recv.at[where], here.below)
+
+    def across(where, whose):
+        mine = part(where, whose)
+        return remote(mine, mine, sib_send.at[where], sib_recv.at[where], here.twin)
+
+    @pl.when(here.has_above)
+    def _():
+        up(place).start()
+
+    @pl.when(here.has_below)
+    def _():
+        down(place).start()
+
+    across(place, core).start()
+    for step in range(1, LINE):
+        if meanwhile[step - 1] is not None:
+            meanwhile[step - 1]()
+
+        @pl.when(place >= step)
+        def _():
+            up(place - step).wait_recv()
+
+            @pl.when(here.has_above)
+            def _():
+                up(place - step).start()
+
+            across(place - step, core).start()
+
+        @pl.when(place + step < LINE)
+        def _():
+            down(place + step).wait_recv()
+
+            @pl.when(here.has_below)
+            def _():
+                down(place + step).start()
+
+            across(place + step, core).start()
+
+    if meanwhile[LINE - 1] is not None:
+        meanwhile[LINE - 1]()
+    for where in range(LINE):
+        across(where, 1 - core).wait_recv()
+        across(where, core).wait_send()
+
+        @pl.when((where <= place) & here.has_above)
+        def _():
+            up(where).wait_send()
+
+        @pl.when((where >= place) & here.has_below)
+        def _():
+            down(where).wait_send()
+
+
+def line_reduce(here, out, ours, theirs, bufs, sems, own_terms=None, meanwhile=()):
+    sib_buf, rx_up, rx_dn, tx_up, tx_dn = bufs
+    sib_send, sib_recv, up_send, up_recv, dn_send, dn_recv = sems
+    rows = out.shape[0]
+    place = here.place
+    meanwhile = list(meanwhile) + [None] * LINE
+
+    def part(ref, where):
+        return rows_at(ref, where * rows, rows)
+
+    def read(ref, where):
+        return ref[pl.ds(pl.multiple_of(where * rows, rows), rows), :].astype(F32)
+
+    def across(where):
+        return remote(part(theirs, where), part(sib_buf, where), sib_send.at[where], sib_recv.at[where], here.twin)
+
+    def up(where):
+        return remote(part(tx_up, where), part(rx_up, where), up_send.at[where], up_recv.at[where], here.above)
+
+    def down(where):
+        return remote(part(tx_dn, where), part(rx_dn, where), dn_send.at[where], dn_recv.at[where], here.below)
+
+    def summed(where):
+        return read(ours, where) + read(sib_buf, where)
+
+    def put(ref, where, value):
+        ref[pl.ds(pl.multiple_of(where * rows, rows), rows), :] = value.astype(BF16)
+
+    for step in range(LINE - 1, 0, -1):
+        @pl.when(place + step < LINE)
+        def _():
+            across(place + step).start()
+
+        @pl.when(place >= step)
+        def _():
+            across(place - step).start()
+
+    across(place).start()
+    if own_terms is not None:
+        own_terms()
+    for step in range(LINE - 1, 0, -1):
+        @pl.when(place + step < LINE)
+        def _():
+            where = place + step
+            across(where).wait_recv()
+
+            @pl.when(here.has_below)
+            def _():
+                up(where).wait_recv()
+                put(tx_up, where, summed(where) + read(rx_up, where))
+
+            @pl.when(place == 0)
+            def _():
+                put(tx_up, where, summed(where))
+
+            up(where).start()
+
+        @pl.when(place >= step)
+        def _():
+            where = place - step
+            across(where).wait_recv()
+
+            @pl.when(here.has_above)
+            def _():
+                down(where).wait_recv()
+                put(tx_dn, where, summed(where) + read(rx_dn, where))
+
+            @pl.when(place == LINE - 1)
+            def _():
+                put(tx_dn, where, summed(where))
+
+            down(where).start()
+
+        if meanwhile[LINE - 1 - step] is not None:
+            meanwhile[LINE - 1 - step]()
+
+    across(place).wait_recv()
+    out[...] = summed(place)
+
+    @pl.when(here.has_below)
+    def _():
+        up(place).wait_recv()
+        out[...] += read(rx_up, place)
+
+    @pl.when(here.has_above)
+    def _():
+        down(place).wait_recv()
+        out[...] += read(rx_dn, place)
+
+    for where in range(LINE):
+        across(where).wait_send()
+
+        @pl.when(where > place)
+        def _():
+            up(where).wait_send()
+
+        @pl.when(where < place)
+        def _():
+            down(where).wait_send()
+
+
+def dot(a, b):
+    return jnp.dot(a, b, preferred_element_type=F32)
+
+
+def dot_last(a, b):
+    return lax.dot_general(a, b, (((1,), (1,)), ((), ())), preferred_element_type=F32)
+
+
+def dot_rows(a, b):
+    return lax.dot_general(a, b, (((0,), (0,)), ((), ())), preferred_element_type=F32)
+
+
+def low_lanes(shape, size=HEAD_DIM):
+    return lax.rem(lax.broadcasted_iota(jnp.int32, shape, 1), 2 * size) < size
+
+
+def turn(block, cosine, sine):
+    half = HEAD_DIM // 2
+    other = jnp.where(low_lanes(block.shape, half), pltpu.roll(block, 128 - half, 1), pltpu.roll(block, half, 1))
+    return block * cosine + other * sine
+
+
+def spread_heads(wide):
+    low = low_lanes((wide.shape[0], 128))
+    parts = []
+    for pair in range(GROUP // 2):
+        block = wide[:, pair * 128:(pair + 1) * 128]
+        parts.append(jnp.where(low, block, 0.0))
+        parts.append(jnp.where(low, pltpu.roll(block, 64, 1), 0.0))
+    return jnp.concatenate(parts, 0)
+
+
+def join_heads(tall, from_high):
+    rows = tall.shape[0] // GROUP
+    low = low_lanes((rows, 128))
+    parts = []
+    for pair in range(GROUP // 2):
+        one = tall[2 * pair * rows:(2 * pair + 1) * rows]
+        two = tall[(2 * pair + 1) * rows:(2 * pair + 2) * rows]
+        if from_high:
+            parts.append(jnp.where(low, pltpu.roll(one, 64, 1), two))
+        else:
+            parts.append(jnp.where(low, one, pltpu.roll(two, 64, 1)))
+    return jnp.concatenate(parts, 1)
+
+
+def two_slot_probs(spread, kv, lens, pair):
+    rows = 2 * SLOT
+    q_at = lax.broadcasted_iota(jnp.int32, (rows, rows), 0)
+    k_at = lax.broadcasted_iota(jnp.int32, (rows, rows), 1)
+    first = lens[pl.ds(pl.multiple_of(16 * pair, 8), 8), :][:1]
+    second = lens[pl.ds(pl.multiple_of(16 * pair + 8, 8), 8), :][:1]
+    k_len = jnp.where(lax.broadcasted_iota(jnp.int32, (1, rows), 1) < SLOT, first, second)
+    k_pos = jnp.where(k_at < SLOT, k_at, k_at - SLOT).astype(F32)
+    allowed = (q_at >= k_at) & ((q_at < SLOT) | (k_at >= SLOT)) & (k_pos < k_len)
+    allowed = jnp.concatenate([jnp.where(allowed, 1.0, 0.0)] * GROUP, 0)
+    scores = dot_last(spread, kv) * HEAD_DIM**-0.5
+    scores = jnp.where(allowed > 0.5, scores, -1e30)
+    terms = jnp.exp(scores - jnp.max(scores, -1, keepdims=True))
+    return terms / jnp.sum(terms, -1, keepdims=True)
+
+
+def root(values):
+    return lax.rsqrt(jnp.mean(values * values, -1, keepdims=True) + EPSILON)
+
+
+Q_AT, KV_AT, AO_AT = 0, Q_SLAB, Q_SLAB + 2 * HEAD_DIM
+A_COLS = AO_AT + Q_SLAB
+
+
+def forward_body(
+    ends, lens_in, gain_in, tables, w_in, w_out,
+    wa, wg, wd, xn_out, hn_out, qkv_out, ctx_out, gu_out, hid_out, res_out, y_out, cot_out, gain_out, lens,
+    cross, k_pair, v_pair, kv_mine, kv_twin, wa_v, wg_v, wd_v, seq, hnb, qkv, ctx, gu, hid, theirs, ours, res, total,
+    sib_buf, rx_up, rx_dn, tx_up, tx_dn,
+    loc_sem, push_send, push_recv, hop_send, hop_recv, misc, misc_send, misc_recv, save,
+    *line_sems,
+):
+    gather_sems, len_sems, reduce_sems = line_sems[:5], line_sems[5:10], line_sems[10:]
+    here = Here()
+    core, shard, place = here.core, here.shard, here.place
+    width = ends.shape[1]
+    part = w_in.shape[0]
+    here.greet()
+
+    own_rows = pl.ds(pl.multiple_of(shard * part, part), part)
+
+    def cut(ref, base, size, head):
+        return ref.at[:, pl.ds(pl.multiple_of(base + head * size, size), size)]
+
+    ff0 = Q_COLS + 2 * KV_COLS
+    slabs = [
+        (lambda h: cut(w_in, 0, Q_SLAB, h), lambda l: wa.at[l, own_rows, pl.ds(Q_AT, Q_SLAB)]),
+        (lambda h: cut(w_out, 0, Q_SLAB, h), lambda l: wa.at[l, own_rows, pl.ds(AO_AT, Q_SLAB)]),
+        (None, lambda l: wa.at[l, own_rows, pl.ds(KV_AT, 2 * HEAD_DIM)]),
+        (lambda h: cut(w_in, ff0, FF_SLAB, h), lambda l: wg.at[l, own_rows, pl.ds(0, FF_SLAB)]),
+        (lambda h: cut(w_in, ff0 + FF, FF_SLAB, h), lambda l: wg.at[l, own_rows, pl.ds(FF_SLAB, FF_SLAB)]),
+        (lambda h: cut(w_out, Q_COLS, FF_SLAB, h), lambda l: wd.at[l, own_rows]),
+    ]
+    my_head, twin_head = place * CORES + core, place * CORES + 1 - core
+
+    def own_copy(i, layer):
+        src, dst = slabs[i]
+        return pltpu.make_async_copy(kv_mine if src is None else src(my_head), dst(layer), loc_sem.at[i])
+
+    def twin_copy(i, layer):
+        src, dst = slabs[i]
+        return remote(kv_twin if src is None else src(twin_head), dst(layer), push_send.at[i], push_recv.at[i], here.twin)
+
+    k_copy = pltpu.make_async_copy(cut(w_in, Q_COLS, 128, place), k_pair, misc.at[0])
+    v_copy = pltpu.make_async_copy(cut(w_in, Q_COLS + KV_COLS, 128, place), v_pair, misc.at[1])
+    k_copy.start()
+    v_copy.start()
+    for i in (0, 1):
+        twin_copy(i, core).start()
+        own_copy(i, core).start()
+    other_rows = pl.ds(pl.multiple_of((1 - core) * SLOT, SLOT), SLOT)
+    cross_copy = remote(ends.at[other_rows], cross, misc_send.at[0], misc_recv.at[0], here.twin)
+    cross_copy.start()
+    gain_copy = remote(gain_in, gain_out.at[core], misc_send.at[1], misc_recv.at[1], here.twin)
+    gain_copy.start()
+    gain_out[core] = gain_in[...]
+    k_copy.wait()
+    v_copy.wait()
+    low = low_lanes(k_pair.shape)
+    k, v = k_pair[...].astype(F32), v_pair[...].astype(F32)
+    kv0 = jnp.where(low, k, pltpu.roll(v, 64, 1)).astype(BF16)
+    kv1 = jnp.where(low, pltpu.roll(k, 64, 1), v).astype(BF16)
+    kv_mine[...] = jnp.where(core == 0, kv0, kv1)
+    kv_twin[...] = jnp.where(core == 0, kv1, kv0)
+    for i in (2, 3, 4, 5):
+        twin_copy(i, core).start()
+        own_copy(i, core).start()
+
+    PIECES = ((wa, (0, 1, 2)), (wg, (3, 4)), (wd, (5,)))
+    half = part // 2
+
+    def own_ready(layer, piece):
+        @pl.when(core == layer)
+        def _():
+            for i in PIECES[piece][1]:
+                own_copy(i, layer).wait()
+
+        @pl.when(core != layer)
+        def _():
+            for i in PIECES[piece][1]:
+                twin_copy(i, layer).wait_recv()
+
+    def hop(layer, piece, which, rows, size, peer):
+        ref = PIECES[piece][0].at[layer, pl.ds(pl.multiple_of(rows, size), size)]
+        return remote(ref, ref, hop_send.at[layer, piece, which], hop_recv.at[layer, piece, which], peer)
+
+    def hops(layer, piece):
+        return (
+            hop(layer, piece, 0, shard * part, part, here.x_peer),
+            hop(layer, piece, 1, shard * part, part, here.y_peer),
+            hop(layer, piece, 2, here.x_shard * part, half, here.y_peer),
+            hop(layer, piece, 3, here.y_shard * part + half, half, here.x_peer),
+        )
+
+    def hop_one(layer, piece):
+        own_ready(layer, piece)
+        one, two, _, _ = hops(layer, piece)
+        one.start()
+        two.start()
+
+    def hop_two(layer, piece):
+        one, two, three, four = hops(layer, piece)
+        one.wait_recv()
+        three.start()
+        two.wait_recv()
+        four.start()
+
+    def all_in(layer, piece):
+        _, _, three, four = hops(layer, piece)
+        three.wait_recv()
+        four.wait_recv()
+
+    hop_one(0, 0)
+
+    rows8 = lens_in.shape[0]
+    lens[pl.ds(pl.multiple_of((core * LINE + place) * rows8, rows8), rows8), :] = lens_in[...]
+    line_gather(here, lens, len_sems)
+    cross_copy.wait()
+    gain_copy.wait()
+    first = core == 0
+    ours0, others0 = ends[:SLOT].astype(F32), ends[SLOT:].astype(F32)
+    crossed = cross[...].astype(F32)
+    x = jnp.where(first, ours0, crossed)
+    cot_out[...] = jnp.where(first, crossed, others0).astype(BF16)
+    res[0] = x
+
+    def own_block(ref):
+        return ref.at[pl.ds(pl.multiple_of((core * LINE + place) * SLOT, SLOT), SLOT), :]
+
+    def load(src, dst, i):
+        copy = pltpu.make_async_copy(src, dst, misc.at[i])
+        copy.start()
+        copy.wait()
+
+    reduce_bufs = (sib_buf, rx_up, rx_dn, tx_up, tx_dn)
+    half_rows = LINE * SLOT
+
+    def layer(index):
+        saves = []
+
+        def keep(src, dst):
+            copy = pltpu.make_async_copy(src, dst, save.at[index, len(saves)])
+            copy.start()
+            saves.append(copy)
+
+        if index == 0:
+            x = res[0]
+        else:
+            x = y_out[...].astype(F32)
+            res[2] = x
+        own_block(seq)[...] = (x * root(x) * gain_out[index, 0:1]).astype(BF16)
+        line_gather(here, seq, gather_sems)
+        keep(seq, xn_out.at[index])
+        hop_two(index, 0)
+        hop_one(index, 1 if index == 0 else 2)
+        all_in(index, 0)
+        load(wa.at[index], wa_v, 0)
+
+        def attend(pair, _):
+            at = pl.ds(pl.multiple_of(pair * 2 * SLOT, 2 * SLOT), 2 * SLOT)
+            wide = dot(seq[at, :], wa_v[:, :AO_AT])
+            kv = turn(wide[:, KV_AT:AO_AT], tables[2], tables[3])
+            q = jnp.concatenate(
+                [turn(wide[:, 128 * i:128 * (i + 1)], tables[0], tables[1]) for i in range(GROUP // 2)], 1
+            )
+            kv_low = kv.astype(BF16)
+            qkv[at, :Q_SLAB] = q.astype(BF16)
+            qkv[at, KV_AT:AO_AT] = kv_low
+            probs = two_slot_probs(spread_heads(q).astype(BF16), kv_low, lens, pair).astype(BF16)
+            ctx[at, :] = join_heads(dot(probs, kv_low), True).astype(BF16)
+            return 0
+
+        lax.fori_loop(0, LINE, attend, 0)
+        keep(qkv, qkv_out.at[index])
+        keep(ctx, ctx_out.at[index])
+        if index == 0:
+            hop_one(0, 2)
+
+        def terms(whose, src, weights, cols, dst):
+            rows = pl.ds(pl.multiple_of(whose * half_rows, half_rows), half_rows)
+
+            def tile(n, _):
+                at = pl.ds(pl.multiple_of(n * 512, 512), 512)
+                dst[:, at] = dot_last(src[rows, :], weights[at, cols]).astype(dst.dtype)
+                return 0
+
+            lax.fori_loop(0, width // 512, tile, 0)
+
+        def reduce(src, weights, cols):
+            terms(1 - core, src, weights, cols, theirs)
+            line_reduce(here, total, ours, theirs, reduce_bufs, reduce_sems,
+                        lambda: terms(core, src, weights, cols, ours))
+
+        saves[0].wait()
+        reduce(ctx, wa_v, slice(AO_AT, A_COLS))
+        middle = x + total[...]
+        res[1 + 2 * index] = middle
+        own_block(hnb)[...] = (middle * root(middle) * gain_out[index, 1:2]).astype(BF16)
+        line_gather(here, hnb, gather_sems)
+        keep(hnb, hn_out.at[index])
+        hop_two(index, 1)
+        if index == 0:
+            hop_one(1, 0)
+        all_in(index, 1)
+        load(wg.at[index], wg_v, 0)
+
+        def gate_up(n, _):
+            at = pl.ds(pl.multiple_of(n * 256, 256), 256)
+            at_up = pl.ds(pl.multiple_of(FF_SLAB + n * 256, 256), 256)
+            gate = dot(hnb[...], wg_v[:, at])
+            up = dot(hnb[...], wg_v[:, at_up])
+            gu[:, at] = gate
+            gu[:, at_up] = up
+            hid[:, at] = (gate * jax.nn.sigmoid(gate) * up).astype(BF16)
+            return 0
+
+        lax.fori_loop(0, FF_SLAB // 256, gate_up, 0)
+        keep(gu, gu_out.at[index])
+        keep(hid, hid_out.at[index])
+        hop_two(index, 2)
+        if index == 0:
+            hop_one(1, 1)
+        all_in(index, 2)
+        load(wd.at[index], wd_v, 0)
+        saves[3].wait()
+        reduce(hid, wd_v, slice(None))
+        y_out[...] = (res[1 + 2 * index] + total[...]).astype(BF16)
+        for i in (1, 2, 4, 5):
+            saves[i].wait()
+
+    layer(0)
+    layer(1)
+    for i in range(4):
+        pltpu.make_async_copy(res.at[i], res_out.at[i], misc.at[i]).start()
+    for i in range(4):
+        pltpu.make_async_copy(res.at[i], res_out.at[i], misc.at[i]).wait()
+    for i in range(6):
+        twin_copy(i, core).wait_send()
+    for index in range(2):
+        for piece in range(3):
+            for move in hops(index, piece):
+                move.wait_send()
+
+
+def forward_call(ends, lens, gain, tables, w_in, w_out):
+    width = ends.shape[1]
+    rows = LINE * CORES * SLOT
+    hbm = pl.BlockSpec(memory_space=pl.ANY)
+    vmem = pl.BlockSpec(memory_space=pltpu.VMEM)
+    shape = jax.ShapeDtypeStruct
+    dma = pltpu.SemaphoreType.DMA
+    line = dma((LINE,))
+    block = pltpu.VMEM((LINE * SLOT, width), BF16)
+    return pl.pallas_call(
+        forward_body,
+        out_shape=[
+            shape((2, width, A_COLS), BF16),
+            shape((2, width, 2 * FF_SLAB), BF16),
+            shape((2, width, FF_SLAB), BF16),
+            shape((2, rows, width), BF16),
+            shape((2, rows, width), BF16),
+            shape((2, rows, AO_AT), BF16),
+            shape((2, rows, Q_SLAB), BF16),
+            shape((2, rows, 2 * FF_SLAB), F32),
+            shape((2, rows, FF_SLAB), BF16),
+            shape((4, SLOT, width), F32),
+            shape((SLOT, width), BF16),
+            shape((SLOT, width), BF16),
+            shape((2, 2, width), F32),
+            shape((LINE * CORES * 8, 128), F32),
+        ],
+        in_specs=[vmem, vmem, vmem, vmem, hbm, hbm],
+        out_specs=[hbm] * 10 + [vmem] * 4,
+        scratch_shapes=[
+            pltpu.VMEM((SLOT, width), BF16),
+            pltpu.VMEM((w_in.shape[0], 128), BF16),
+            pltpu.VMEM((w_in.shape[0], 128), BF16),
+            pltpu.VMEM((w_in.shape[0], 128), BF16),
+            pltpu.VMEM((w_in.shape[0], 128), BF16),
+            pltpu.VMEM((width, A_COLS), BF16),
+            pltpu.VMEM((width, 2 * FF_SLAB), BF16),
+            pltpu.VMEM((width, FF_SLAB), BF16),
+            pltpu.VMEM((rows, width), BF16),
+            pltpu.VMEM((rows, width), BF16),
+            pltpu.VMEM((rows, AO_AT), BF16),
+            pltpu.VMEM((rows, Q_SLAB), BF16),
+            pltpu.VMEM((rows, 2 * FF_SLAB), F32),
+            pltpu.VMEM((rows, FF_SLAB), BF16),
+            block,
+            pltpu.VMEM((LINE * SLOT, width), F32),
+            pltpu.VMEM((4, SLOT, width), F32),
+            pltpu.VMEM((SLOT, width), F32),
+            block, block, block, block, block,
+            dma((6,)), dma((6,)), dma((6,)), dma((2, 3, 4)), dma((2, 3, 4)),
+            dma((4,)), dma((2,)), dma((2,)), dma((2, 6)),
+        ] + [line] * 16,
+        compiler_params=pltpu.CompilerParams(
+            collective_id=0, has_side_effects=True, vmem_limit_bytes=56 * 2**20
+        ),
+        name="forward_two_layers",
+        cost_estimate=pl.CostEstimate(flops=16_000_000_000, bytes_accessed=600_000_000, transcendentals=0),
+    )(ends, lens, gain, tables, w_in, w_out)
 
 
 def swap_cores(value):
@@ -467,39 +1050,42 @@
     first = core == 0
     replicas = lax.axis_size("dp") // LINE
     w_in, w_out = in_weight[0], out_weight[0]
-    head = place * CORES + core
-    sibling = place * CORES + 1 - core
     rows = ends_in.shape[1] // CORES
 
     def by_layer(mine, others):
         return jnp.where(first, mine, others), jnp.where(first, others, mine)
 
-    attn = by_layer(attn_slab(w_in, w_out, head), swap_cores(attn_slab(w_in, w_out, sibling)))
-    mlp = by_layer(mlp_slab(w_in, w_out, head), swap_cores(mlp_slab(w_in, w_out, sibling)))
-
-    def layer_weights(index):
-        a = gather_rows(attn[index])
-        m = gather_rows(mlp[index])
-        return (a[:, :QKV_SLAB], a[:, QKV_SLAB:], m[:, :2 * FF_SLAB], m[:, 2 * FF_SLAB:])
-
-    weights = [layer_weights(0), layer_weights(1)]
-    own_gain = relative(norm_gain[0], shard)
-    gains = by_layer(own_gain, swap_cores(own_gain))
-    ends = relative(ends_in[0], shard)
-    mine, others = ends[:rows], ends[rows:]
-    crossed = swap_cores(jnp.where(first, others, mine))
-    x = jnp.where(first, mine, crossed).astype(F32)
-    cot = jnp.where(first, crossed, others).astype(F32)
-    line_groups = [
-        [r * LINE + p for p in range(LINE)] for r in range(replicas)
-    ]
-    lengths = lax.all_gather(seq_len, "dp", tiled=True, axis_index_groups=line_groups if replicas > 1 else None)
     own_length = jnp.where(first, seq_len[0], seq_len[1])
     valid = (jnp.arange(rows) < own_length).astype(F32)[:, None]
     tables = rope_tables(rows)
-
-    y0, kept0 = forward_layer(x, weights[0], gains[0], lengths, tables)
-    y1, kept1 = forward_layer(y0.astype(BF16).astype(F32), weights[1], gains[1], lengths, tables)
+    cos, sin = tables[0][0, :, 0], tables[1][0, :, 0]
+    one, zero = jnp.ones((rows, HEAD_DIM), F32), jnp.zeros((rows, HEAD_DIM), F32)
+    rope = jnp.stack([
+        jnp.tile(jnp.concatenate([cos] * 4, 1), (2, 1)),
+        jnp.tile(jnp.concatenate([-sin, sin] * 2, 1), (2, 1)),
+        jnp.tile(jnp.concatenate([cos, cos, one], 1), (2, 1)),
+        jnp.tile(jnp.concatenate([-sin, sin, zero], 1), (2, 1)),
+    ])
+    lens_block = jnp.full((8, 128), own_length.astype(F32))
+    (wa, wg, wd, xn, hn, qkv, ctx, gu, hid, res, y1, cot, gains, lens) = forward_call(
+        ends_in[0], lens_block, norm_gain[0], rope, w_in, w_out
+    )
+    lengths = lens[::8, 0].astype(jnp.int32)
+    cot = cot.astype(F32)
+    slots = LINE * CORES
+    weights = [(wa[l, :, :AO_AT], wa[l, :, AO_AT:], wg[l], wd[l]) for l in range(2)]
+
+    def kept_of(l):
+        x, middle = res[2 * l], res[2 * l + 1]
+        queries = qkv[l, :, :Q_SLAB].reshape(slots, rows, GROUP, HEAD_DIM)
+        keys = qkv[l, :, Q_SLAB:Q_SLAB + HEAD_DIM].reshape(slots, rows, HEAD_DIM)
+        values = qkv[l, :, Q_SLAB + HEAD_DIM:].reshape(slots, rows, HEAD_DIM)
+        scores = masked_scores(queries, keys, lengths)
+        log_total = jax.nn.logsumexp(scores, -1, keepdims=True)
+        return (x, rms_scale(x), xn[l], queries, keys, values, log_total, ctx[l], middle,
+                rms_scale(middle), hn[l], gu[l, :, :FF_SLAB], gu[l, :, FF_SLAB:], hid[l])
+
+    kept0, kept1 = kept_of(0), kept_of(1)
     dx1, mlp1, attn1, gain1 = backward_layer(kept1, cot * valid, weights[1], gains[1], lengths, tables)
     dx0, mlp0, attn0, gain0 = backward_layer(
         kept0, dx1.astype(BF16).astype(F32), weights[0], gains[0], lengths, tables
@@ -509,9 +1095,11 @@
         (in_rows, in_cols), (out_rows, out_cols) = pairs
 
         def term(k):
-            part = slice(k * in_rows.shape[1] // 4, (k + 1) * in_rows.shape[1] // 4)
+            size = in_rows.shape[1] // 4
+            at = jnp.bitwise_xor(shard, k) * size
+            cut = lambda v: lax.dynamic_slice_in_dim(v, at, size, 1)
             return jnp.concatenate(
-                [mm_rows(in_rows[:, part], in_cols), mm_rows(out_rows[:, part], out_cols)], 1
+                [mm_rows(cut(in_rows), in_cols), mm_rows(cut(out_rows), out_cols)], 1
             ).astype(BF16)
 
         total = reduce_rows(term)
@@ -561,12 +1149,12 @@
         [columns(grad_attn, QKV_SLAB, QKV_SLAB + Q_SLAB), columns(grad_mlp, 2 * FF_SLAB, 3 * FF_SLAB)], 1
     )
     own_gains = jnp.where(first, gain0, gain1) + swap_cores(jnp.where(first, gain1, gain0))
-    gain_rows = lax.psum_scatter(relative(own_gains, shard), ("shard", "dp"), scatter_dimension=1, tiled=True)
-    dx0, y1 = dx0.astype(BF16), y1.astype(BF16)
+    gain_rows = lax.psum_scatter(own_gains, ("shard", "dp"), scatter_dimension=1, tiled=True)
+    dx0 = dx0.astype(BF16)
     crossed = swap_cores(jnp.where(first, y1, dx0))
     ends_mine = jnp.where(first, dx0, crossed)
     ends_others = jnp.where(first, crossed, y1)
-    ends_out = relative(jnp.concatenate([ends_mine, ends_others], 0), shard)
+    ends_out = jnp.concatenate([ends_mine, ends_others], 0)
     return ends_out[None], in_grad[None], out_grad[None], gain_rows[None]
 
 

time: 1310 us -> 1260 us (0.962)
  Pallas kernels: 377 us -> 573 us
  waiting for transfers between devices: 399 us -> 297 us
  local copies, waits for them, and re-layouts: 186 us -> 111 us
  starting transfers between devices: 96.1 us -> 52.3 us
  matrix products: 122 us -> 105 us
    pallas_call x0 -> x1, Pallas kernels: none -> 388 us  [forward_call(): pl.pallas_call(forward_body, out_shape=[shape((2, width, A_COLS), BF16),...]
    pallas_call x8 -> x4, Pallas kernels: 212 us -> 104 us  [scatter_line(): pl.pallas_call(scatter_body, out_shape=jax.ShapeDtypeStruct((rows, width)...]
    pallas_call x8 -> x4, Pallas kernels: 165 us -> 81 us  [gather_line(): pl.pallas_call(gather_body, out_shape=jax.ShapeDtypeStruct((blocks, rows,...]
    unnamed x2, waiting for transfers between devices: 73.3 us -> 0.04 us
    ppermute x32 -> x16, waiting for transfers between devices: 240 us -> 195 us  [hop(): return lax.ppermute(value, 'shard', [(i, i ^ bit) for i in range(peers)])]
    unnamed x349 -> x226, local copies, waits for them, and re-layouts: 68.9 us -> 34.4 us
    ppermute x12, starting transfers between devices: 64.5 us -> 39.6 us  [line_exchange(): lax.ppermute(lax.dynamic_index_in_dim(blocks, to, 0, False), 'dp', line_p...]
    ppermute x32 -> x16, starting transfers between devices: 29.7 us -> 12.2 us  [hop(): return lax.ppermute(value, 'shard', [(i, i ^ bit) for i in range(peers)])]
  transfers between devices with their start and end apart: 53 -> 33, of which waited for: 15 -> 13; matrix products, arithmetic and copies ran while one was open for 14% -> 12% of each run, Pallas kernels for 16% -> 0%
where the time goes in v2:
time: 1260 us; the launch traced here: 1240 us
  Pallas kernels  573 us (45%)
  waiting for transfers between devices  297 us (24%)
  local copies, waits for them, and re-layouts  111 us (9%)
  matrix products  105 us (8%)
  other arithmetic  82.3 us (7%)
  starting transfers between devices  52.3 us (4%)
  between operations  17.5 us (1%)
    pallas_call x1, Pallas kernels, forward_call(): pl.pallas_call(forward_body, out_shape=[shape((2, width, A_COLS), BF16),...  388 us
    ppermute x16, waiting for transfers between devices, hop(): return lax.ppermute(value, 'shard', [(i, i ^ bit) for i in range(peers)])  195 us
    pallas_call x4, Pallas kernels, scatter_line(): pl.pallas_call(scatter_body, out_shape=jax.ShapeDtypeStruct((rows, width)...  104 us
    ppermute x12, waiting for transfers between devices, line_exchange(): lax.ppermute(lax.dynamic_index_in_dim(blocks, to, 0, False), 'dp', line_p...  101 us
    pallas_call x4, Pallas kernels, gather_line(): pl.pallas_call(gather_body, out_shape=jax.ShapeDtypeStruct((blocks, rows,...  81 us
    dot_general x32, matrix products, mm_rows(): lax.dot_general(a, b, (((0,), (0,)), ((), ())), preferred_element_type=F32)  57.8 us
    ppermute x12, starting transfers between devices, line_exchange(): lax.ppermute(lax.dynamic_index_in_dim(blocks, to, 0, False), 'dp', line_p...  39.6 us
    transpose x10, local copies, waits for them, and re-layouts, columns(): part = values[:, :, lo:hi].transpose(1, 0, 2)  36.3 us
  transfers between devices with their start and end apart: 33, of which 13 were waited for; matrix products, arithmetic and copies ran while one was open for 12% of the time, Pallas kernels for 0%

profile of v2, /device:TPU:20, one launch (start us, length us, event | category | flops | bytes accessed | tf_op | source)
XLA Modules:
  0.0 1238.3 jit_solution(7242846606958015660)
XLA Ops:
  12.1 388.1 %forward_two_layers.1 = (bf16[2,2048,640]{2,1,0:T(8,128)(2,1)}, bf16[2,2048,2048]{2,1,0:T(8,128)(2,1)}, bf16[2,2048,1024]{2,1,0:T(8,128)(2,1)}, bf16[2,512,2048]...) custom-call(bf16[128,2048]{1,0:T(8,128)(2,1)} %bitcast.566, ...), custom_call_target="tpu_custom_call" | custom-call | flops 16000000000 | bytes 600000000 | tf_op jit(solution)/shard_map/forward_two_layers/pallas_call | solution.py:792
  404.2 19.5 %gather_line.4 = bf16[8,64,2048]{2,1,0:T(8,128)(2,1)S(1)} custom-call(bf16[64,2048]{1,0:T(8,128)(2,1)S(1)} %fusion.186.x_ref), custom_call_target="tpu_custom_call" | custom-call | bytes 60000000 | tf_op jit(solution)/shard_map/gather_line/pallas_call | solution.py:133
  423.7 7.1 fusion.40
  430.8 8.7 fusion.20
  439.5 25.1 %scatter_line.4 = f32[64,2048]{1,0:T(8,128)S(1)} custom-call(bf16[8,64,2048]{2,1,0:T(8,128)(2,1)S(1)} %bitcast.492), custom_call_target="tpu_custom_call" | custom-call | bytes 60000000 | tf_op jit(solution)/shard_map/scatter_line/pallas_call | solution.py:248
  467.4 20.3 %gather_line.5 = bf16[8,64,2048]{2,1,0:T(8,128)(2,1)S(1)} custom-call(bf16[64,2048]{1,0:T(8,128)(2,1)S(1)} %get-tuple-element.57.x_ref), custom_call_target="tpu_custom_call" | custom-call | bytes 60000000 | tf_op jit(solution)/shard_map/gather_line/pallas_call | solution.py:133
  503.5 26.2 %scatter_line.5 = f32[64,2048]{1,0:T(8,128)S(1)} custom-call(bf16[8,64,2048]{2,1,0:T(8,128)(2,1)S(1)} %bitcast.493), custom_call_target="tpu_custom_call" | custom-call | bytes 60000000 | tf_op jit(solution)/shard_map/scatter_line/pallas_call | solution.py:248
  530.2 20.7 %gather_line.6 = bf16[8,64,2048]{2,1,0:T(8,128)(2,1)S(1)} custom-call(bf16[64,2048]{1,0:T(8,128)(2,1)S(1)} %fusion.139.x_ref), custom_call_target="tpu_custom_call" | custom-call | bytes 60000000 | tf_op jit(solution)/shard_map/gather_line/pallas_call | solution.py:133
  550.9 7.1 fusion.31
  558.0 8.7 fusion.23
  566.7 26.3 %scatter_line.6 = f32[64,2048]{1,0:T(8,128)S(1)} custom-call(bf16[8,64,2048]{2,1,0:T(8,128)(2,1)S(1)} %bitcast.490), custom_call_target="tpu_custom_call" | custom-call | bytes 60000000 | tf_op jit(solution)/shard_map/scatter_line/pallas_call | solution.py:248
  594.8 20.6 %gather_line.7 = bf16[8,64,2048]{2,1,0:T(8,128)(2,1)S(1)} custom-call(bf16[64,2048]{1,0:T(8,128)(2,1)S(1)} %get-tuple-element.55.x_ref), custom_call_target="tpu_custom_call" | custom-call | bytes 60000000 | tf_op jit(solution)/shard_map/gather_line/pallas_call | solution.py:133
  629.9 26.6 %scatter_line.7 = f32[64,2048]{1,0:T(8,128)S(1)} custom-call(bf16[8,64,2048]{2,1,0:T(8,128)(2,1)S(1)} %bitcast.491), custom_call_target="tpu_custom_call" | custom-call | bytes 60000000 | tf_op jit(solution)/shard_map/scatter_line/pallas_call | solution.py:248
  661.6 3.1 convolution_convert_fusion.1
  682.0 4.5 convolution_convert_fusion.2
  689.2 4.4 convolution_convert_fusion
  696.4 4.5 convolution_convert_fusion.3
  703.7 4.5 convolution_convert_fusion.7
  734.9 11.4 collective-permute-done.8
  761.4 22.2 %collective-permute-done.18 = bf16[256,3072]{1,0:T(8,128)(2,1)S(1)} collective-permute-done((bf16[256,3072]{1,0:T(8,128)(2,1)S(1)}, bf16[256,3072]{1,0:T(8,128)(2,1)S(1)}, u32[]{:S(2)}, u32[]{:S(2)}) %collective-permute-start.18) | collective-permute-done | bytes 1572896 | tf_op jit(solution)/shard_map/ppermute | solution.py:849
  793.3 71.8 %collective-permute-done.3 = bf16[256,640]{0,1:T(8,128)(2,1)S(1)} collective-permute-done((bf16[256,640]{0,1:T(8,128)(2,1)S(1)}, bf16[256,640]{0,1:T(8,128)(2,1)S(1)}, u32[]{:S(2)}, u32[]{:S(2)}) %collective-permute-start.3) | collective-permute-done | bytes 327712 | tf_op jit(solution)/shard_map/ppermute | solution.py:849
  869.1 76.2 %collective-permute-done.9 = bf16[512,640]{0,1:T(8,128)(2,1)} collective-permute-done((bf16[512,640]{0,1:T(8,128)(2,1)}, bf16[512,640]{0,1:T(8,128)(2,1)}, u32[]{:S(2)}, u32[]{:S(2)}) %collective-permute-start.9) | collective-permute-done | bytes 655392 | tf_op jit(solution)/shard_map/ppermute | solution.py:849
  948.8 12.0 collective-permute-done.11
  963.5 4.2 add_convert_fusion
  969.1 12.4 collective-permute-start.27
  984.1 3.6 add_convert_fusion.1
  991.6 17.5 %collective-permute-done.27 = bf16[128,3072]{1,0:T(8,128)(2,1)S(1)} collective-permute-done((bf16[128,3072]{1,0:T(8,128)(2,1)S(1)}, bf16[128,3072]{1,0:T(8,128)(2,1)S(1)}, u32[]{:S(2)}, u32[]{:S(2)}) %collective-permute-start.27) | collective-permute-done | bytes 786464 | tf_op jit(solution)/shard_map/ppermute | solution.py:1041
  1015.2 18.6 %collective-permute-done.28 = bf16[128,3072]{1,0:T(8,128)(2,1)} collective-permute-done((bf16[128,3072]{1,0:T(8,128)(2,1)}, bf16[128,3072]{1,0:T(8,128)(2,1)}, u32[]{:S(2)}, u32[]{:S(2)}) %collective-permute-start.28) | collective-permute-done | bytes 786464 | tf_op jit(solution)/shard_map/ppermute | solution.py:1041
  1033.8 8.1 collective-permute-start.12
  1041.8 41.1 %collective-permute-done.29 = bf16[128,3072]{1,0:T(8,128)(2,1)} collective-permute-done((bf16[128,3072]{1,0:T(8,128)(2,1)}, bf16[128,3072]{1,0:T(8,128)(2,1)}, u32[]{:S(2)}, u32[]{:S(2)}) %collective-permute-start.29) | collective-permute-done | bytes 786464 | tf_op jit(solution)/shard_map/ppermute | solution.py:1041
  1085.9 4.3 gather_fusion.3
  1090.2 4.2 collective-permute-done.20
  1094.4 10.5 collective-permute-done.21
  1105.0 11.4 collective-permute-start.5
  1116.4 9.0 collective-permute-done.22
  1125.3 3.1 pad_maximum_fusion.2
  1128.4 4.3 gather_fusion.2
  1132.7 5.1 broadcast_select_fusion.2
  1166.1 3.3 select_bitcast_fusion.1
  1170.0 6.6 bitcast_convert_fusion
  1176.6 10.1 slice_bitcast_fusion
  1186.7 5.4 copy.156
  1192.2 4.2 maximum_bitcast_fusion
  1196.4 5.9 copy.158
  1202.3 5.3 copy.153
  1207.6 5.4 copy.154
  1212.9 4.6 constant_dynamic-update-slice_fusion.1
  1219.7 11.3 copy.157
  (455 shorter events, 182.0 us)
Async XLA Ops:
  7.2 1135.6 %reduce-scatter.4.cloned.1.call-start = ((), (), s32[]{:S(2)}) async-start(), calls=%async_computation.1 | async-start | bytes 1114112
  7.4 392.9 %copy-start.36 = (f32[64,32]{0,1:T(8,128)}, f32[64,32]{0,1:T(8,128)S(1)}, u32[]{:S(2)}) copy-start(f32[64,32]{0,1:T(8,128)S(1)} %get-tuple-element.124) | copy-start | bytes 24580
  503.5 26.5 %copy-start.21 = (f32[64,2048]{1,0:T(8,128)S(1)}, f32[64,2048]{1,0:T(8,128)}, u32[]{:S(2)}) copy-start(f32[64,2048]{1,0:T(8,128)} %get-tuple-element.58) | copy-start | bytes 1572868
  530.0 128.4 %copy-start.68 = (f32[2048]{0:T(1024)}, f32[2048]{0:T(1024)S(1)}, u32[]{:S(2)}) copy-start(f32[2048]{0:T(1024)S(1)} %get-tuple-element.46) | copy-start | bytes 24580
  593.7 64.6 %copy-start.70 = (f32[2048]{0:T(1024)}, f32[2048]{0:T(1024)S(1)}, u32[]{:S(2)}) copy-start(f32[2048]{0:T(1024)S(1)} %get-tuple-element.44) | copy-start | bytes 24580
  626.9 32.1 %copy-start.15 = (bf16[2,512,2048]{2,1,0:T(8,128)(2,1)S(1)}, bf16[2,512,2048]{2,1,0:T(8,128)(2,1)}, u32[]{:S(2)}) copy-start(bf16[2,512,2048]{2,1,0:T(8,128)(2,1)} %get-tuple-element.32) | copy-start | bytes 12582916
  629.8 26.7 %copy-start.91 = (f32[64]{0:T(128)S(1)}, f32[64]{0:T(128)}, u32[]{:S(2)}) copy-start(f32[64]{0:T(128)} %get-tuple-element.50) | copy-start | bytes 772
  629.8 26.7 %copy-start.64 = (f32[1,1,2048]{2,1,0:T(1,128)S(1)}, f32[1,1,2048]{2,1,0:T(1,128)}, u32[]{:S(2)}) copy-start(f32[1,1,2048]{2,1,0:T(1,128)} %get-tuple-element.118) | copy-start | bytes 24580
  629.9 28.5 %copy-start.67 = (f32[2048]{0:T(1024)S(1)}, f32[2048]{0:T(1024)}, u32[]{:S(2)}) copy-start(f32[2048]{0:T(1024)} %get-tuple-element.48) | copy-start | bytes 24580
  659.0 127.9 %collective-permute-start.31 = (f32[2,2048]{1,0:T(2,128)}, f32[2,2048]{1,0:T(2,128)}, u32[]{:S(2)}, u32[]{:S(2)}) collective-permute-start(f32[2,2048]{1,0:T(2,128)} %broadcast_select_fusion.11), channel_id=1, source_target_pairs={{0,16},{16,0},{1,17},{17,1},{2,18},{18,2},{3,19},{19,3},{4,20},{20... | collective-permute-start | bytes 49160 | tf_op jit(solution)/shard_map/ppermute | solution.py:844
  668.4 79.4 %collective-permute-start.23 = (bf16[256,3072]{1,0:T(8,128)(2,1)}, bf16[256,3072]{1,0:T(8,128)(2,1)}, u32[]{:S(2)}, u32[]{:S(2)}) collective-permute-start(bf16[256,3072]{1,0:T(8,128)(2,1)} %get-tuple-element.76), channel_id=1, source_target_pairs={{0,8},{4,12},{8,0},{12,4},{1,9},{5,13},{9,1},{13,5},{2,10},{6,14},... | collective-permute-start | bytes 4718600 | tf_op jit(solution)/shard_map/ppermute | solution.py:849
  669.0 82.5 %collective-permute-start.25 = (bf16[256,3072]{1,0:T(8,128)(2,1)}, bf16[256,3072]{1,0:T(8,128)(2,1)}, u32[]{:S(2)}, u32[]{:S(2)}) collective-permute-start(bf16[256,3072]{1,0:T(8,128)(2,1)} %get-tuple-element.77), channel_id=1, source_target_pairs={{0,4},{4,0},{8,12},{12,8},{1,5},{5,1},{9,13},{13,9},{2,6},{6,2},{1... | collective-permute-start | bytes 4718600 | tf_op jit(solution)/shard_map/ppermute | solution.py:849
  675.6 82.8 %collective-permute-start.16 = (bf16[256,3072]{1,0:T(8,128)(2,1)}, bf16[256,3072]{1,0:T(8,128)(2,1)}, u32[]{:S(2)}, u32[]{:S(2)}) collective-permute-start(bf16[256,3072]{1,0:T(8,128)(2,1)} %get-tuple-element.82), channel_id=1, source_target_pairs={{0,8},{4,12},{8,0},{12,4},{1,9},{5,13},{9,1},{13,5},{2,10},{6,14},... | collective-permute-start | bytes 4718600 | tf_op jit(solution)/shard_map/ppermute | solution.py:849
  680.7 65.6 %collective-permute-start.8 = (bf16[256,640]{0,1:T(8,128)(2,1)}, bf16[256,640]{0,1:T(8,128)(2,1)}, u32[]{:S(2)}, u32[]{:S(2)}) collective-permute-start(bf16[256,640]{0,1:T(8,128)(2,1)} %get-tuple-element.104), channel_id=1, source_target_pairs={{0,8},{4,12},{8,0},{12,4},{1,9},{5,13},{9,1},{13,5},{2,10},{6,14},... | collective-permute-start | bytes 983048 | tf_op jit(solution)/shard_map/ppermute | solution.py:849
  746.3 37.3 %collective-permute-start.18 = (bf16[256,3072]{1,0:T(8,128)(2,1)S(1)}, bf16[256,3072]{1,0:T(8,128)(2,1)S(1)}, u32[]{:S(2)}, u32[]{:S(2)}) collective-permute-start(bf16[256,3072]{1,0:T(8,128)(2,1)S(1)} %copy-done.27), channel_id=1, source_target_pairs={{0,4},{4,0},{8,12},{12,8},{1,5},{5,1},{9,13},{13,9},{2,6},{6,2},{1... | collective-permute-start | bytes 4718600 | tf_op jit(solution)/shard_map/ppermute | solution.py:849
  747.9 42.7 %collective-permute-start.10 = (bf16[256,640]{0,1:T(8,128)(2,1)S(1)}, bf16[256,640]{0,1:T(8,128)(2,1)S(1)}, u32[]{:S(2)}, u32[]{:S(2)}) collective-permute-start(bf16[256,640]{0,1:T(8,128)(2,1)S(1)} %copy-done.47), channel_id=1, source_target_pairs={{0,4},{4,0},{8,12},{12,8},{1,5},{5,1},{9,13},{13,9},{2,6},{6,2},{1... | collective-permute-start | bytes 983048 | tf_op jit(solution)/shard_map/ppermute | solution.py:849
  751.5 39.6 %collective-permute-start.1 = (bf16[256,640]{0,1:T(8,128)(2,1)S(1)}, bf16[256,640]{0,1:T(8,128)(2,1)S(1)}, u32[]{:S(2)}, u32[]{:S(2)}) collective-permute-start(bf16[256,640]{0,1:T(8,128)(2,1)S(1)} %get-tuple-element.110), channel_id=1, source_target_pairs={{0,8},{4,12},{8,0},{12,4},{1,9},{5,13},{9,1},{13,5},{2,10},{6,14},... | collective-permute-start | bytes 983048 | tf_op jit(solution)/shard_map/ppermute | solution.py:849
  758.4 204.5 %collective-permute-start.24 = (bf16[512,3072]{1,0:T(8,128)(2,1)}, bf16[512,3072]{1,0:T(8,128)(2,1)}, u32[]{:S(2)}, u32[]{:S(2)}) collective-permute-start(bf16[512,3072]{1,0:T(8,128)(2,1)} %pad_maximum_fusion.3), channel_id=1, source_target_pairs={{0,4},{4,0},{8,12},{12,8},{1,5},{5,1},{9,13},{13,9},{2,6},{6,2},{1... | collective-permute-start | bytes 9437192 | tf_op jit(solution)/shard_map/ppermute | solution.py:849
  783.6 180.0 %collective-permute-start.26 = (bf16[512,3072]{1,0:T(8,128)(2,1)}, bf16[512,3072]{1,0:T(8,128)(2,1)}, u32[]{:S(2)}, u32[]{:S(2)}) collective-permute-start(bf16[512,3072]{1,0:T(8,128)(2,1)} %fusion.19), channel_id=1, source_target_pairs={{0,8},{4,12},{8,0},{12,4},{1,9},{5,13},{9,1},{13,5},{2,10},{6,14},... | collective-permute-start | bytes 9437192 | tf_op jit(solution)/shard_map/ppermute | solution.py:849
  786.9 78.8 %copy-start.69 = (f32[2048]{0:T(1024)S(1)}, f32[2048]{0:T(1024)}, u32[]{:S(2)}) copy-start(f32[2048]{0:T(1024)} %copy-done.68) | copy-start | bytes 24580
  786.9 78.8 %copy-start.71 = (f32[2048]{0:T(1024)S(1)}, f32[2048]{0:T(1024)}, u32[]{:S(2)}) copy-start(f32[2048]{0:T(1024)} %copy-done.70) | copy-start | bytes 24580
  786.9 78.8 %copy-start.73 = (f32[2048]{0:T(1024)S(1)}, f32[2048]{0:T(1024)}, u32[]{:S(2)}) copy-start(f32[2048]{0:T(1024)} %copy-done.72) | copy-start | bytes 24580
  786.9 78.1 %collective-permute-start.3 = (bf16[256,640]{0,1:T(8,128)(2,1)S(1)}, bf16[256,640]{0,1:T(8,128)(2,1)S(1)}, u32[]{:S(2)}, u32[]{:S(2)}) collective-permute-start(bf16[256,640]{0,1:T(8,128)(2,1)S(1)} %get-tuple-element.111), channel_id=1, source_target_pairs={{0,4},{4,0},{8,12},{12,8},{1,5},{5,1},{9,13},{13,9},{2,6},{6,2},{1... | collective-permute-start | bytes 983048 | tf_op jit(solution)/shard_map/ppermute | solution.py:849
  790.6 74.4 %copy-start.50 = (bf16[256,640]{0,1:T(8,128)(2,1)}, bf16[256,640]{0,1:T(8,128)(2,1)S(1)}, u32[]{:S(2)}) copy-start(bf16[256,640]{0,1:T(8,128)(2,1)S(1)} %collective-permute-done.10) | copy-start | bytes 983044
  790.6 190.9 %collective-permute-start.17 = (bf16[512,3072]{1,0:T(8,128)(2,1)}, bf16[512,3072]{1,0:T(8,128)(2,1)}, u32[]{:S(2)}, u32[]{:S(2)}) collective-permute-start(bf16[512,3072]{1,0:T(8,128)(2,1)} %pad_maximum_fusion.1), channel_id=1, source_target_pairs={{0,4},{4,0},{8,12},{12,8},{1,5},{5,1},{9,13},{13,9},{2,6},{6,2},{1... | collective-permute-start | bytes 9437192 | tf_op jit(solution)/shard_map/ppermute | solution.py:849
  791.1 78.0 %copy-start.48 = (bf16[256,640]{0,1:T(8,128)(2,1)}, bf16[256,640]{0,1:T(8,128)(2,1)S(1)}, u32[]{:S(2)}) copy-start(bf16[256,640]{0,1:T(8,128)(2,1)S(1)} %collective-permute-done.1) | copy-start | bytes 983044
  791.1 190.4 %collective-permute-start.19 = (bf16[512,3072]{1,0:T(8,128)(2,1)}, bf16[512,3072]{1,0:T(8,128)(2,1)}, u32[]{:S(2)}, u32[]{:S(2)}) collective-permute-start(bf16[512,3072]{1,0:T(8,128)(2,1)} %fusion.17), channel_id=1, source_target_pairs={{0,8},{4,12},{8,0},{12,4},{1,9},{5,13},{9,1},{13,5},{2,10},{6,14},... | collective-permute-start | bytes 9437192 | tf_op jit(solution)/shard_map/ppermute | solution.py:849
  865.0 80.3 %collective-permute-start.9 = (bf16[512,640]{0,1:T(8,128)(2,1)}, bf16[512,640]{0,1:T(8,128)(2,1)}, u32[]{:S(2)}, u32[]{:S(2)}) collective-permute-start(bf16[512,640]{0,1:T(8,128)(2,1)} %pad_maximum_fusion.13), channel_id=1, source_target_pairs={{0,4},{4,0},{8,12},{12,8},{1,5},{5,1},{9,13},{13,9},{2,6},{6,2},{1... | collective-permute-start | bytes 1966088 | tf_op jit(solution)/shard_map/ppermute | solution.py:849
  869.1 78.8 %copy-start.49 = (bf16[256,640]{0,1:T(8,128)(2,1)S(1)}, bf16[256,640]{0,1:T(8,128)(2,1)}, u32[]{:S(2)}) copy-start(bf16[256,640]{0,1:T(8,128)(2,1)} %copy-done.48) | copy-start | bytes 983044
  945.3 15.5 %collective-permute-start.11 = (bf16[512,640]{0,1:T(8,128)(2,1)S(1)}, bf16[512,640]{0,1:T(8,128)(2,1)S(1)}, u32[]{:S(2)}, u32[]{:S(2)}) collective-permute-start(bf16[512,640]{0,1:T(8,128)(2,1)S(1)} %fusion.95), channel_id=1, source_target_pairs={{0,8},{4,12},{8,0},{12,4},{1,9},{5,13},{9,1},{13,5},{2,10},{6,14},... | collective-permute-start | bytes 1966088 | tf_op jit(solution)/shard_map/ppermute | solution.py:849
  960.8 28.5 %collective-permute-start.2 = (bf16[512,640]{0,1:T(8,128)(2,1)}, bf16[512,640]{0,1:T(8,128)(2,1)}, u32[]{:S(2)}, u32[]{:S(2)}) collective-permute-start(bf16[512,640]{0,1:T(8,128)(2,1)} %pad_maximum_fusion.11), channel_id=1, source_target_pairs={{0,4},{4,0},{8,12},{12,8},{1,5},{5,1},{9,13},{13,9},{2,6},{6,2},{1... | collective-permute-start | bytes 1966088 | tf_op jit(solution)/shard_map/ppermute | solution.py:849
  962.9 26.4 %collective-permute-start.4 = (bf16[512,640]{0,1:T(8,128)(2,1)}, bf16[512,640]{0,1:T(8,128)(2,1)S(1)}, u32[]{:S(2)}, u32[]{:S(2)}) collective-permute-start(bf16[512,640]{0,1:T(8,128)(2,1)} %fusion.93), channel_id=1, source_target_pairs={{0,8},{4,12},{8,0},{12,4},{1,9},{5,13},{9,1},{13,5},{2,10},{6,14},... | collective-permute-start | bytes 1966088 | tf_op jit(solution)/shard_map/ppermute | solution.py:849
  969.1 40.0 %collective-permute-start.27 = (bf16[128,3072]{1,0:T(8,128)(2,1)S(1)}, bf16[128,3072]{1,0:T(8,128)(2,1)S(1)}, u32[]{:S(2)}, u32[]{:S(2)}) collective-permute-start(bf16[128,3072]{1,0:T(8,128)(2,1)S(1)} %get-tuple-element.75), channel_id=1, source_target_pairs={{0,1},{1,2},{2,3},{3,0},{4,5},{5,6},{6,7},{7,4},{8,9},{9,10},{10,1... | collective-permute-start | bytes 2359304 | tf_op jit(solution)/shard_map/ppermute | solution.py:1041
  981.5 52.3 %collective-permute-start.28 = (bf16[128,3072]{1,0:T(8,128)(2,1)}, bf16[128,3072]{1,0:T(8,128)(2,1)}, u32[]{:S(2)}, u32[]{:S(2)}) collective-permute-start(bf16[128,3072]{1,0:T(8,128)(2,1)} %get-tuple-element.74), channel_id=1, source_target_pairs={{0,2},{1,3},{2,0},{3,1},{4,6},{5,7},{6,4},{7,5},{8,10},{9,11},{10,... | collective-permute-start | bytes 2359304 | tf_op jit(solution)/shard_map/ppermute | solution.py:1041
  981.5 101.4 %collective-permute-start.29 = (bf16[128,3072]{1,0:T(8,128)(2,1)}, bf16[128,3072]{1,0:T(8,128)(2,1)}, u32[]{:S(2)}, u32[]{:S(2)}) collective-permute-start(bf16[128,3072]{1,0:T(8,128)(2,1)} %get-tuple-element.73), channel_id=1, source_target_pairs={{0,3},{1,0},{2,1},{3,2},{4,7},{5,4},{6,5},{7,6},{8,11},{9,8},{10,9... | collective-permute-start | bytes 2359304 | tf_op jit(solution)/shard_map/ppermute | solution.py:1041
  989.3 105.2 %collective-permute-start.20 = (bf16[128,3072]{1,0:T(8,128)(2,1)}, bf16[128,3072]{1,0:T(8,128)(2,1)}, u32[]{:S(2)}, u32[]{:S(2)}) collective-permute-start(bf16[128,3072]{1,0:T(8,128)(2,1)} %get-tuple-element.81), channel_id=1, source_target_pairs={{0,1},{1,2},{2,3},{3,0},{4,5},{5,6},{6,7},{7,4},{8,9},{9,10},{10,1... | collective-permute-start | bytes 2359304 | tf_op jit(solution)/shard_map/ppermute | solution.py:1041
  989.3 115.7 %collective-permute-start.21 = (bf16[128,3072]{1,0:T(8,128)(2,1)}, bf16[128,3072]{1,0:T(8,128)(2,1)}, u32[]{:S(2)}, u32[]{:S(2)}) collective-permute-start(bf16[128,3072]{1,0:T(8,128)(2,1)} %get-tuple-element.80), channel_id=1, source_target_pairs={{0,2},{1,3},{2,0},{3,1},{4,6},{5,7},{6,4},{7,5},{8,10},{9,11},{10,... | collective-permute-start | bytes 2359304 | tf_op jit(solution)/shard_map/ppermute | solution.py:1041
  1010.0 115.3 %collective-permute-start.22 = (bf16[128,3072]{1,0:T(8,128)(2,1)}, bf16[128,3072]{1,0:T(8,128)(2,1)}, u32[]{:S(2)}, u32[]{:S(2)}) collective-permute-start(bf16[128,3072]{1,0:T(8,128)(2,1)} %get-tuple-element.79), channel_id=1, source_target_pairs={{0,3},{1,0},{2,1},{3,2},{4,7},{5,4},{6,5},{7,6},{8,11},{9,8},{10,9... | collective-permute-start | bytes 2359304 | tf_op jit(solution)/shard_map/ppermute | solution.py:1041
  1012.4 70.5 %copy-start.40 = (bf16[128,3072]{1,0:T(8,128)(2,1)S(1)}, bf16[128,3072]{1,0:T(8,128)(2,1)}, u32[]{:S(2)}) copy-start(bf16[128,3072]{1,0:T(8,128)(2,1)} %copy-done.39) | copy-start | bytes 2359300
  1033.8 104.1 %collective-permute-start.12 = (bf16[128,640]{1,0:T(8,128)(2,1)}, bf16[128,640]{1,0:T(8,128)(2,1)S(1)}, u32[]{:S(2)}, u32[]{:S(2)}) collective-permute-start(bf16[128,640]{1,0:T(8,128)(2,1)} %get-tuple-element.103), channel_id=1, source_target_pairs={{0,1},{1,2},{2,3},{3,0},{4,5},{5,6},{6,7},{7,4},{8,9},{9,10},{10,1... | collective-permute-start | bytes 491528 | tf_op jit(solution)/shard_map/ppermute | solution.py:1041
  1082.9 57.8 %collective-permute-start.13 = (bf16[128,640]{1,0:T(8,128)(2,1)}, bf16[128,640]{1,0:T(8,128)(2,1)S(1)}, u32[]{:S(2)}, u32[]{:S(2)}) collective-permute-start(bf16[128,640]{1,0:T(8,128)(2,1)} %get-tuple-element.102), channel_id=1, source_target_pairs={{0,2},{1,3},{2,0},{3,1},{4,6},{5,7},{6,4},{7,5},{8,10},{9,11},{10,... | collective-permute-start | bytes 491528 | tf_op jit(solution)/shard_map/ppermute | solution.py:1041
  1094.4 49.8 %collective-permute-start.14 = (bf16[128,640]{1,0:T(8,128)(2,1)}, bf16[128,640]{1,0:T(8,128)(2,1)S(1)}, u32[]{:S(2)}, u32[]{:S(2)}) collective-permute-start(bf16[128,640]{1,0:T(8,128)(2,1)} %get-tuple-element.101), channel_id=1, source_target_pairs={{0,3},{1,0},{2,1},{3,2},{4,7},{5,4},{6,5},{7,6},{8,11},{9,8},{10,9... | collective-permute-start | bytes 491528 | tf_op jit(solution)/shard_map/ppermute | solution.py:1041
  1105.0 41.6 %collective-permute-start.5 = (bf16[128,640]{1,0:T(8,128)(2,1)}, bf16[128,640]{1,0:T(8,128)(2,1)S(1)}, u32[]{:S(2)}, u32[]{:S(2)}) collective-permute-start(bf16[128,640]{1,0:T(8,128)(2,1)} %get-tuple-element.109), channel_id=1, source_target_pairs={{0,1},{1,2},{2,3},{3,0},{4,5},{5,6},{6,7},{7,4},{8,9},{9,10},{10,1... | collective-permute-start | bytes 491528 | tf_op jit(solution)/shard_map/ppermute | solution.py:1041
  1125.3 21.3 %collective-permute-start.6 = (bf16[128,640]{1,0:T(8,128)(2,1)S(1)}, bf16[128,640]{1,0:T(8,128)(2,1)}, u32[]{:S(2)}, u32[]{:S(2)}) collective-permute-start(bf16[128,640]{1,0:T(8,128)(2,1)S(1)} %get-tuple-element.108), channel_id=1, source_target_pairs={{0,2},{1,3},{2,0},{3,1},{4,6},{5,7},{6,4},{7,5},{8,10},{9,11},{10,... | collective-permute-start | bytes 491528 | tf_op jit(solution)/shard_map/ppermute | solution.py:1041
  1137.9 8.8 collective-permute-start.7
  1140.7 25.5 %collective-permute-start.30 = (bf16[4,128,3072]{2,1,0:T(8,128)(2,1)}, bf16[4,128,3072]{2,1,0:T(8,128)(2,1)}, u32[]{:S(2)}, u32[]{:S(2)}) collective-permute-start(bf16[4,128,3072]{2,1,0:T(8,128)(2,1)} %broadcast_select_fusion.2), channel_id=1, source_target_pairs={{0,16},{16,0},{1,17},{17,1},{2,18},{18,2},{3,19},{19,3},{4,20},{20... | collective-permute-start | bytes 9437192 | tf_op jit(solution)/shard_map/ppermute | solution.py:844
  1144.9 5.0 collective-permute-start
  1149.3 2.3 collective-permute-start.15
  (94 other events, 641.6 us)
Sparse Core Ops, SparseCore 0:
  868.1 74.6 reduce-scatter.3

commit v3 on v2

v3 whole, which is shorter than its diff:
```python
import functools

import jax
import jax.numpy as jnp
from jax import lax
from jax.experimental import pallas as pl
from jax.experimental.pallas import tpu as pltpu
from jax.sharding import PartitionSpec as P

HEADS = 32
KV_HEADS = 8
GROUP = HEADS // KV_HEADS
HEAD_DIM = 64
FF = 8192
EPSILON = 1e-05
BF16 = jnp.bfloat16
F32 = jnp.float32
CORES = 2
LINE = KV_HEADS // CORES
SHARDS = 4
SLOT = 64
Q_SLAB = GROUP * HEAD_DIM
QKV_SLAB = Q_SLAB + 2 * HEAD_DIM
FF_SLAB = FF // KV_HEADS
Q_COLS = HEADS * HEAD_DIM
KV_COLS = KV_HEADS * HEAD_DIM


class Here:
    def __init__(self):
        self.core = lax.axis_index("section")
        self.shard = lax.axis_index("shard")
        self.depth = lax.axis_index("dp")
        self.place = lax.rem(self.depth, LINE)
        self.twin = {"section": 1 - self.core}
        self.x_shard = self.shard + 1 - 2 * lax.rem(self.shard, 2)
        self.y_shard = lax.rem(self.shard + 2, SHARDS)
        self.far_shard = SHARDS - 1 - self.shard
        self.x_peer = {"shard": self.x_shard}
        self.y_peer = {"shard": self.y_shard}
        self.above = {"dp": self.depth + 1}
        self.below = {"dp": self.depth - 1}
        self.has_above = self.place < LINE - 1
        self.has_below = self.place > 0

    def greet(self):
        barrier = pltpu.get_barrier_semaphore()
        for peer in (self.twin, self.x_peer, self.y_peer):
            pl.semaphore_signal(barrier, inc=1, device_id=peer)

        @pl.when(self.has_above)
        def _():
            pl.semaphore_signal(barrier, inc=1, device_id=self.above)

        @pl.when(self.has_below)
        def _():
            pl.semaphore_signal(barrier, inc=1, device_id=self.below)

        pl.semaphore_wait(barrier, jnp.where(self.has_above & self.has_below, 5, 4))


def remote(src, dst, send, recv, device):
    return pltpu.make_async_remote_copy(src, dst, send, recv, device_id=device)


def rows_at(ref, start, size):
    return ref.at[pl.ds(pl.multiple_of(start, size), size)]


def line_gather(here, buf, sems, meanwhile=()):
    up_send, dn_send, sib_send, z_recv, sib_recv = sems
    rows = buf.shape[0] // (LINE * CORES)
    core, place = here.core, here.place
    meanwhile = list(meanwhile) + [None] * LINE

    def part(where, whose):
        return rows_at(buf, (whose * LINE + where) * rows, rows)

    def up(where):
        mine = part(where, core)
        return remote(mine, mine, up_send.at[where], z_recv.at[where], here.above)

    def down(where):
        mine = part(where, core)
        return remote(mine, mine, dn_send.at[where], z_recv.at[where], here.below)

    def across(where, whose):
        mine = part(where, whose)
        return remote(mine, mine, sib_send.at[where], sib_recv.at[where], here.twin)

    @pl.when(here.has_above)
    def _():
        up(place).start()

    @pl.when(here.has_below)
    def _():
        down(place).start()

    across(place, core).start()
    for step in range(1, LINE):
        if meanwhile[step - 1] is not None:
            meanwhile[step - 1]()

        @pl.when(place >= step)
        def _():
            up(place - step).wait_recv()

            @pl.when(here.has_above)
            def _():
                up(place - step).start()

            across(place - step, core).start()

        @pl.when(place + step < LINE)
        def _():
            down(place + step).wait_recv()

            @pl.when(here.has_below)
            def _():
                down(place + step).start()

            across(place + step, core).start()

    if meanwhile[LINE - 1] is not None:
        meanwhile[LINE - 1]()
    for where in range(LINE):
        across(where, 1 - core).wait_recv()
        across(where, core).wait_send()

        @pl.when((where <= place) & here.has_above)
        def _():
            up(where).wait_send()

        @pl.when((where >= place) & here.has_below)
        def _():
            down(where).wait_send()


def line_reduce(here, out, ours, theirs, bufs, sems, own_terms=None, meanwhile=()):
    sib_buf, rx_up, rx_dn, tx_up, tx_dn = bufs
    sib_send, sib_recv, up_send, up_recv, dn_send, dn_recv = sems
    rows = out.shape[0]
    place = here.place
    meanwhile = list(meanwhile) + [None] * LINE

    def part(ref, where):
        return rows_at(ref, where * rows, rows)

    def read(ref, where):
        return ref[pl.ds(pl.multiple_of(where * rows, rows), rows), :].astype(F32)

    def across(where):
        return remote(part(theirs, where), part(sib_buf, where), sib_send.at[where], sib_recv.at[where], here.twin)

    def up(where):
        return remote(part(tx_up, where), part(rx_up, where), up_send.at[where], up_recv.at[where], here.above)

    def down(where):
        return remote(part(tx_dn, where), part(rx_dn, where), dn_send.at[where], dn_recv.at[where], here.below)

    def summed(where):
        return read(ours, where) + read(sib_buf, where)

    def put(ref, where, value):
        ref[pl.ds(pl.multiple_of(where * rows, rows), rows), :] = value.astype(BF16)

    for step in range(LINE - 1, 0, -1):
        @pl.when(place + step < LINE)
        def _():
            across(place + step).start()

        @pl.when(place >= step)
        def _():
            across(place - step).start()

    across(place).start()
    if own_terms is not None:
        own_terms()
    for step in range(LINE - 1, 0, -1):
        @pl.when(place + step < LINE)
        def _():
            where = place + step
            across(where).wait_recv()

            @pl.when(here.has_below)
            def _():
                up(where).wait_recv()
                put(tx_up, where, summed(where) + read(rx_up, where))

            @pl.when(place == 0)
            def _():
                put(tx_up, where, summed(where))

            up(where).start()

        @pl.when(place >= step)
        def _():
            where = place - step
            across(where).wait_recv()

            @pl.when(here.has_above)
            def _():
                down(where).wait_recv()
                put(tx_dn, where, summed(where) + read(rx_dn, where))

            @pl.when(place == LINE - 1)
            def _():
                put(tx_dn, where, summed(where))

            down(where).start()

        if meanwhile[LINE - 1 - step] is not None:
            meanwhile[LINE - 1 - step]()

    across(place).wait_recv()
    out[...] = summed(place)

    @pl.when(here.has_below)
    def _():
        up(place).wait_recv()
        out[...] += read(rx_up, place)

    @pl.when(here.has_above)
    def _():
        down(place).wait_recv()
        out[...] += read(rx_dn, place)

    for where in range(LINE):
        across(where).wait_send()

        @pl.when(where > place)
        def _():
            up(where).wait_send()

        @pl.when(where < place)
        def _():
            down(where).wait_send()


def dot(a, b):
    return jnp.dot(a, b, preferred_element_type=F32)


def dot_last(a, b):
    return lax.dot_general(a, b, (((1,), (1,)), ((), ())), preferred_element_type=F32)


def dot_rows(a, b):
    return lax.dot_general(a, b, (((0,), (0,)), ((), ())), preferred_element_type=F32)


def low_lanes(shape, size=HEAD_DIM):
    return lax.rem(lax.broadcasted_iota(jnp.int32, shape, 1), 2 * size) < size


def turn(block, cosine, sine):
    half = HEAD_DIM // 2
    other = jnp.where(low_lanes(block.shape, half), pltpu.roll(block, 128 - half, 1), pltpu.roll(block, half, 1))
    return block * cosine + other * sine


def spread_heads(wide):
    low = low_lanes((wide.shape[0], 128))
    parts = []
    for pair in range(GROUP // 2):
        block = wide[:, pair * 128:(pair + 1) * 128]
        parts.append(jnp.where(low, block, 0.0))
        parts.append(jnp.where(low, pltpu.roll(block, 64, 1), 0.0))
    return jnp.concatenate(parts, 0)


def join_heads(tall, from_high):
    rows = tall.shape[0] // GROUP
    low = low_lanes((rows, 128))
    parts = []
    for pair in range(GROUP // 2):
        one = tall[2 * pair * rows:(2 * pair + 1) * rows]
        two = tall[(2 * pair + 1) * rows:(2 * pair + 2) * rows]
        if from_high:
            parts.append(jnp.where(low, pltpu.roll(one, 64, 1), two))
        else:
            parts.append(jnp.where(low, one, pltpu.roll(two, 64, 1)))
    return jnp.concatenate(parts, 1)


def two_slot_probs(spread, kv, lens, pair):
    rows = 2 * SLOT
    q_at = lax.broadcasted_iota(jnp.int32, (rows, rows), 0)
    k_at = lax.broadcasted_iota(jnp.int32, (rows, rows), 1)
    first = lens[pl.ds(pl.multiple_of(16 * pair, 8), 8), :][:1]
    second = lens[pl.ds(pl.multiple_of(16 * pair + 8, 8), 8), :][:1]
    k_len = jnp.where(lax.broadcasted_iota(jnp.int32, (1, rows), 1) < SLOT, first, second)
    k_pos = jnp.where(k_at < SLOT, k_at, k_at - SLOT).astype(F32)
    allowed = (q_at >= k_at) & ((q_at < SLOT) | (k_at >= SLOT)) & (k_pos < k_len)
    allowed = jnp.concatenate([jnp.where(allowed, 1.0, 0.0)] * GROUP, 0)
    scores = dot_last(spread, kv) * HEAD_DIM**-0.5
    scores = jnp.where(allowed > 0.5, scores, -1e30)
    terms = jnp.exp(scores - jnp.max(scores, -1, keepdims=True))
    return terms / jnp.sum(terms, -1, keepdims=True)


def root(values):
    return lax.rsqrt(jnp.mean(values * values, -1, keepdims=True) + EPSILON)


Q_AT, KV_AT, AO_AT = 0, Q_SLAB, Q_SLAB + 2 * HEAD_DIM
A_COLS = AO_AT + Q_SLAB


def forward_body(
    ends, lens_in, gain_in, tables, w_in, w_out,
    wa_out, wg_out, wd_out, xn_out, hn_out, qkv_out, ctx_out, gu_out, hid_out, res_out, y_out, cot_out, gain_out, lens,
    cross, k_pair, v_pair, kv_mine, kv_twin, wa, wg, wd, seq, hnb, qkv, ctx, gu, hid, theirs, ours, res, total,
    sib_buf, rx_up, rx_dn, tx_up, tx_dn,
    loc_sem, push_send, push_recv, hop_send, hop_recv, misc, misc_send, misc_recv, save, w_save,
    *line_sems,
):
    gather_sems, len_sems, reduce_sems = line_sems[:5], line_sems[5:10], line_sems[10:]
    here = Here()
    core, shard, place = here.core, here.shard, here.place
    width = ends.shape[1]
    part = w_in.shape[0]
    here.greet()

    own_rows = pl.ds(pl.multiple_of(shard * part, part), part)

    def cut(ref, base, size, head):
        return ref.at[:, pl.ds(pl.multiple_of(base + head * size, size), size)]

    ff0 = Q_COLS + 2 * KV_COLS
    slabs = [
        (lambda h: cut(w_in, 0, Q_SLAB, h), lambda l: wa.at[l, own_rows, pl.ds(Q_AT, Q_SLAB)]),
        (lambda h: cut(w_out, 0, Q_SLAB, h), lambda l: wa.at[l, own_rows, pl.ds(AO_AT, Q_SLAB)]),
        (None, lambda l: wa.at[l, own_rows, pl.ds(KV_AT, 2 * HEAD_DIM)]),
        (lambda h: cut(w_in, ff0, FF_SLAB, h), lambda l: wg.at[l, own_rows, pl.ds(0, FF_SLAB)]),
        (lambda h: cut(w_in, ff0 + FF, FF_SLAB, h), lambda l: wg.at[l, own_rows, pl.ds(FF_SLAB, FF_SLAB)]),
        (lambda h: cut(w_out, Q_COLS, FF_SLAB, h), lambda l: wd.at[l, own_rows]),
    ]
    my_head, twin_head = place * CORES + core, place * CORES + 1 - core

    def own_copy(i, layer):
        src, dst = slabs[i]
        return pltpu.make_async_copy(kv_mine if src is None else src(my_head), dst(layer), loc_sem.at[i])

    def twin_copy(i, layer):
        src, dst = slabs[i]
        return remote(kv_twin if src is None else src(twin_head), dst(layer), push_send.at[i], push_recv.at[i], here.twin)

    k_copy = pltpu.make_async_copy(cut(w_in, Q_COLS, 128, place), k_pair, misc.at[0])
    v_copy = pltpu.make_async_copy(cut(w_in, Q_COLS + KV_COLS, 128, place), v_pair, misc.at[1])
    k_copy.start()
    v_copy.start()
    for i in (0, 1):
        twin_copy(i, core).start()
        own_copy(i, core).start()
    other_rows = pl.ds(pl.multiple_of((1 - core) * SLOT, SLOT), SLOT)
    cross_copy = remote(ends.at[other_rows], cross, misc_send.at[0], misc_recv.at[0], here.twin)
    cross_copy.start()
    gain_copy = remote(gain_in, gain_out.at[core], misc_send.at[1], misc_recv.at[1], here.twin)
    gain_copy.start()
    gain_out[core] = gain_in[...]
    k_copy.wait()
    v_copy.wait()
    low = low_lanes(k_pair.shape)
    k, v = k_pair[...].astype(F32), v_pair[...].astype(F32)
    kv0 = jnp.where(low, k, pltpu.roll(v, 64, 1)).astype(BF16)
    kv1 = jnp.where(low, pltpu.roll(k, 64, 1), v).astype(BF16)
    kv_mine[...] = jnp.where(core == 0, kv0, kv1)
    kv_twin[...] = jnp.where(core == 0, kv1, kv0)
    for i in (2, 3, 4, 5):
        twin_copy(i, core).start()
        own_copy(i, core).start()

    PIECES = ((wa, (0, 1, 2)), (wg, (3, 4)), (wd, (5,)))
    half = part // 2

    def own_ready(layer, piece):
        @pl.when(core == layer)
        def _():
            for i in PIECES[piece][1]:
                own_copy(i, layer).wait()

        @pl.when(core != layer)
        def _():
            for i in PIECES[piece][1]:
                twin_copy(i, layer).wait_recv()

    def hop(layer, piece, which, rows, size, peer):
        ref = PIECES[piece][0].at[layer, pl.ds(pl.multiple_of(rows, size), size)]
        return remote(ref, ref, hop_send.at[layer, piece, which], hop_recv.at[layer, piece, which], peer)

    def hops(layer, piece):
        return (
            hop(layer, piece, 0, shard * part, part, here.x_peer),
            hop(layer, piece, 1, shard * part, part, here.y_peer),
            hop(layer, piece, 2, here.x_shard * part, half, here.y_peer),
            hop(layer, piece, 3, here.y_shard * part + half, half, here.x_peer),
        )

    def hop_one(layer, piece):
        own_ready(layer, piece)
        one, two, _, _ = hops(layer, piece)
        one.start()
        two.start()

    def hop_two(layer, piece):
        one, two, three, four = hops(layer, piece)
        one.wait_recv()
        three.start()
        two.wait_recv()
        four.start()

    def all_in(layer, piece):
        _, _, three, four = hops(layer, piece)
        three.wait_recv()
        four.wait_recv()

    hop_one(0, 0)

    rows8 = lens_in.shape[0]
    lens[pl.ds(pl.multiple_of((core * LINE + place) * rows8, rows8), rows8), :] = lens_in[...]
    line_gather(here, lens, len_sems)
    cross_copy.wait()
    gain_copy.wait()
    first = core == 0
    ours0, others0 = ends[:SLOT].astype(F32), ends[SLOT:].astype(F32)
    crossed = cross[...].astype(F32)
    x = jnp.where(first, ours0, crossed)
    cot_out[...] = jnp.where(first, crossed, others0).astype(BF16)
    res[0] = x

    def own_block(ref):
        return ref.at[pl.ds(pl.multiple_of((core * LINE + place) * SLOT, SLOT), SLOT), :]

    def weight_out(layer, piece):
        dst = (wa_out, wg_out, wd_out)[piece].at[layer]
        return pltpu.make_async_copy(PIECES[piece][0].at[layer], dst, w_save.at[layer, piece])

    reduce_bufs = (sib_buf, rx_up, rx_dn, tx_up, tx_dn)
    half_rows = LINE * SLOT

    def layer(index):
        saves = []

        def keep(src, dst):
            copy = pltpu.make_async_copy(src, dst, save.at[index, len(saves)])
            copy.start()
            saves.append(copy)

        if index == 0:
            x = res[0]
        else:
            x = y_out[...].astype(F32)
            res[2] = x
        own_block(seq)[...] = (x * root(x) * gain_out[index, 0:1]).astype(BF16)
        line_gather(here, seq, gather_sems)
        keep(seq, xn_out.at[index])
        hop_two(index, 0)
        hop_one(index, 1 if index == 0 else 2)
        all_in(index, 0)
        weight_out(index, 0).start()

        def attend(pair, _):
            at = pl.ds(pl.multiple_of(pair * 2 * SLOT, 2 * SLOT), 2 * SLOT)
            wide = dot(seq[at, :], wa[index, :, :AO_AT])
            kv = turn(wide[:, KV_AT:AO_AT], tables[2], tables[3])
            q = jnp.concatenate(
                [turn(wide[:, 128 * i:128 * (i + 1)], tables[0], tables[1]) for i in range(GROUP // 2)], 1
            )
            kv_low = kv.astype(BF16)
            qkv[at, :Q_SLAB] = q.astype(BF16)
            qkv[at, KV_AT:AO_AT] = kv_low
            probs = two_slot_probs(spread_heads(q).astype(BF16), kv_low, lens, pair).astype(BF16)
            ctx[at, :] = join_heads(dot(probs, kv_low), True).astype(BF16)
            return 0

        lax.fori_loop(0, LINE, attend, 0)
        keep(qkv, qkv_out.at[index])
        keep(ctx, ctx_out.at[index])
        if index == 0:
            hop_one(0, 2)

        def terms(whose, src, weights, cols, dst):
            rows = pl.ds(pl.multiple_of(whose * half_rows, half_rows), half_rows)

            def tile(n, _):
                at = pl.ds(pl.multiple_of(n * 512, 512), 512)
                dst[:, at] = dot_last(src[rows, :], weights[index, at, cols]).astype(dst.dtype)
                return 0

            lax.fori_loop(0, width // 512, tile, 0)

        def reduce(src, weights, cols):
            terms(1 - core, src, weights, cols, theirs)
            line_reduce(here, total, ours, theirs, reduce_bufs, reduce_sems,
                        lambda: terms(core, src, weights, cols, ours))

        saves[0].wait()
        reduce(ctx, wa, slice(AO_AT, A_COLS))
        middle = x + total[...]
        res[1 + 2 * index] = middle
        own_block(hnb)[...] = (middle * root(middle) * gain_out[index, 1:2]).astype(BF16)
        line_gather(here, hnb, gather_sems)
        keep(hnb, hn_out.at[index])
        hop_two(index, 1)
        if index == 0:
            hop_one(1, 0)
        all_in(index, 1)
        weight_out(index, 1).start()

        def gate_up(n, _):
            at = pl.ds(pl.multiple_of(n * 256, 256), 256)
            at_up = pl.ds(pl.multiple_of(FF_SLAB + n * 256, 256), 256)
            gate = dot(hnb[...], wg[index, :, at])
            up = dot(hnb[...], wg[index, :, at_up])
            gu[:, at] = gate
            gu[:, at_up] = up
            hid[:, at] = (gate * jax.nn.sigmoid(gate) * up).astype(BF16)
            return 0

        lax.fori_loop(0, FF_SLAB // 256, gate_up, 0)
        keep(gu, gu_out.at[index])
        keep(hid, hid_out.at[index])
        hop_two(index, 2)
        if index == 0:
            hop_one(1, 1)
        all_in(index, 2)
        weight_out(index, 2).start()
        saves[3].wait()
        reduce(hid, wd, slice(None))
        y_out[...] = (res[1 + 2 * index] + total[...]).astype(BF16)
        for i in (1, 2, 4, 5):
            saves[i].wait()

    layer(0)
    layer(1)
    for i in range(4):
        pltpu.make_async_copy(res.at[i], res_out.at[i], misc.at[i]).start()
    for i in range(4):
        pltpu.make_async_copy(res.at[i], res_out.at[i], misc.at[i]).wait()
    for i in range(6):
        twin_copy(i, core).wait_send()
    for index in range(2):
        for piece in range(3):
            weight_out(index, piece).wait()
            for move in hops(index, piece):
                move.wait_send()


def forward_call(ends, lens, gain, tables, w_in, w_out):
    width = ends.shape[1]
    rows = LINE * CORES * SLOT
    hbm = pl.BlockSpec(memory_space=pl.ANY)
    vmem = pl.BlockSpec(memory_space=pltpu.VMEM)
    shape = jax.ShapeDtypeStruct
    dma = pltpu.SemaphoreType.DMA
    line = dma((LINE,))
    block = pltpu.VMEM((LINE * SLOT, width), BF16)
    return pl.pallas_call(
        forward_body,
        out_shape=[
            shape((2, width, A_COLS), BF16),
            shape((2, width, 2 * FF_SLAB), BF16),
            shape((2, width, FF_SLAB), BF16),
            shape((2, rows, width), BF16),
            shape((2, rows, width), BF16),
            shape((2, rows, AO_AT), BF16),
            shape((2, rows, Q_SLAB), BF16),
            shape((2, rows, 2 * FF_SLAB), F32),
            shape((2, rows, FF_SLAB), BF16),
            shape((4, SLOT, width), F32),
            shape((SLOT, width), BF16),
            shape((SLOT, width), BF16),
            shape((2, 2, width), F32),
            shape((LINE * CORES * 8, 128), F32),
        ],
        in_specs=[vmem, vmem, vmem, vmem, hbm, hbm],
        out_specs=[hbm] * 10 + [vmem] * 4,
        scratch_shapes=[
            pltpu.VMEM((SLOT, width), BF16),
            pltpu.VMEM((w_in.shape[0], 128), BF16),
            pltpu.VMEM((w_in.shape[0], 128), BF16),
            pltpu.VMEM((w_in.shape[0], 128), BF16),
            pltpu.VMEM((w_in.shape[0], 128), BF16),
            pltpu.VMEM((2, width, A_COLS), BF16),
            pltpu.VMEM((2, width, 2 * FF_SLAB), BF16),
            pltpu.VMEM((2, width, FF_SLAB), BF16),
            pltpu.VMEM((rows, width), BF16),
            pltpu.VMEM((rows, width), BF16),
            pltpu.VMEM((rows, AO_AT), BF16),
            pltpu.VMEM((rows, Q_SLAB), BF16),
            pltpu.VMEM((rows, 2 * FF_SLAB), F32),
            pltpu.VMEM((rows, FF_SLAB), BF16),
            block,
            pltpu.VMEM((LINE * SLOT, width), F32),
            pltpu.VMEM((4, SLOT, width), F32),
            pltpu.VMEM((SLOT, width), F32),
            block, block, block, block, block,
            dma((6,)), dma((6,)), dma((6,)), dma((2, 3, 4)), dma((2, 3, 4)),
            dma((4,)), dma((2,)), dma((2,)), dma((2, 6)), dma((2, 3)),
        ] + [line] * 16,
        compiler_params=pltpu.CompilerParams(
            collective_id=0, has_side_effects=True, vmem_limit_bytes=60 * 2**20
        ),
        name="forward_two_layers",
        cost_estimate=pl.CostEstimate(flops=16_000_000_000, bytes_accessed=600_000_000, transcendentals=0),
    )(ends, lens, gain, tables, w_in, w_out)


def spread_heads_high(wide):
    low = low_lanes((wide.shape[0], 128))
    parts = []
    for pair in range(GROUP // 2):
        block = wide[:, pair * 128:(pair + 1) * 128]
        parts.append(jnp.where(low, 0.0, pltpu.roll(block, 64, 1)))
        parts.append(jnp.where(low, 0.0, block))
    return jnp.concatenate(parts, 0)


CHUNKS = ((0, FF_SLAB), (FF_SLAB, FF_SLAB), (2 * FF_SLAB, FF_SLAB), (3 * FF_SLAB, A_COLS))
SLAB = 3 * FF_SLAB + A_COLS


def backward_body(
    replicas,
    cot_in, y_in, gain, lens, tables, res_in, wa_in, wg_in, wd_in, xn_in, hn_in, qkv_in, ctx_in, gu_in, hid_in,
    fin, ends_out, gain_out, far_rx, near_rx,
    wa, wg, wd, xn, hn, qkv, ctx, gu, hid, dm, da, dgu, dqkv, theirs, ours, total, res,
    sib_buf, rx_up, rx_dn, tx_up, tx_dn, tx_far, tx_x, tx_y, tx_fin, stage, gain_loc, gain_x, gain_y, gain_line,
    end_tx, end_rx,
    load_sem, gu_sem, res_sem, far_send, far_recv, near_send, near_recv, fin_send, fin_recv, stage_sem, misc_send, misc_recv,
    *line_sems,
):
    gather_sems, gain_sems, reduce_sems = line_sems[:5], line_sems[5:10], line_sems[10:]
    here = Here()
    core, shard, place = here.core, here.shard, here.place
    width = cot_in.shape[1]
    part = width // SHARDS
    half = part // 2
    half_rows = LINE * SLOT
    base = here.depth - place

    barrier = pltpu.get_barrier_semaphore()
    for peer in (here.x_peer, here.y_peer):
        pl.semaphore_signal(barrier, inc=1, device_id=peer)
    for other in range(CORES):
        for where in range(LINE):
            @pl.when((core != other) | (place != where))
            def _():
                pl.semaphore_signal(barrier, inc=1, device_id={"section": other, "dp": base + where})

    pl.semaphore_wait(barrier, 2 + CORES * LINE - 1)

    NAMES = ("wd", "wg", "wa", "hid", "qkv", "ctx", "hn", "xn")
    VIEWS = {
        "wd": (wd_in, lambda l: wd), "wg": (wg_in, lambda l: wg), "wa": (wa_in, lambda l: wa),
        "hid": (hid_in, lambda l: hid), "qkv": (qkv_in, lambda l: qkv.at[l]), "ctx": (ctx_in, lambda l: ctx.at[l]),
        "hn": (hn_in, lambda l: hn), "xn": (xn_in, lambda l: xn),
    }

    def load(name, layer):
        src, dst = VIEWS[name]
        return pltpu.make_async_copy(src.at[layer], dst(layer), load_sem.at[layer, NAMES.index(name)])

    def gu_loads(layer, tile):
        return [
            pltpu.make_async_copy(
                gu_in.at[layer, :, pl.ds(i * FF_SLAB + tile * 256, 256)],
                gu.at[tile % 2, :, pl.ds(i * 256, 256)], gu_sem.at[tile % 2, i])
            for i in range(2)
        ]

    for tile in range(2):
        for copy in gu_loads(1, tile):
            copy.start()
    for name in NAMES:
        load(name, 1).start()

    ready = set()

    def need(name, layer):
        if (name, layer) not in ready:
            ready.add((name, layer))
            load(name, layer).wait()

    gain_loc[...] = jnp.zeros_like(gain_loc)

    pending = {}

    def claim(key):
        for move in pending.pop(key, ()):
            move.wait_send()

    def products(layer, chunk, block, put):
        at = pl.ds(pl.multiple_of(block * part, part), part)
        need("hn" if chunk < 2 else "hid" if chunk == 2 else "xn", layer)

        def tiles(lhs, rhs, size, to):
            for lo in range(0, size, 512):
                hi = min(lo + 512, size)
                put(slice(to + lo, to + hi), dot_rows(lhs[:, at], rhs[:, lo:hi]))

        if chunk < 2:
            tiles(hn, dgu.at[layer, :, pl.ds(chunk * FF_SLAB, FF_SLAB)], FF_SLAB, 0)
        elif chunk == 2:
            tiles(dm.at[layer], hid, FF_SLAB, 0)
        else:
            tiles(xn, dqkv.at[layer], AO_AT, 0)
            tiles(da.at[layer], ctx.at[layer], Q_SLAB, AO_AT)

    def far_moves(layer, chunk):
        lo, size = CHUNKS[chunk]
        src = tx_far.at[chunk % 2]
        cols = pl.ds(0, size)
        return [
            remote(src.at[pl.ds(i * half, half), cols], far_rx.at[layer, i, :, pl.ds(lo, size)],
                   far_send.at[layer, chunk, i], far_recv.at[layer, chunk, i], peer)
            for i, peer in ((0, here.x_peer), (1, here.y_peer))
        ]

    def near_moves(layer, chunk):
        lo, size = CHUNKS[chunk]
        cols = pl.ds(0, size)
        return [
            remote(src.at[chunk % 2, :, cols], near_rx.at[layer, i, :, pl.ds(lo, size)],
                   near_send.at[layer, chunk, i], near_recv.at[layer, chunk, i], peer)
            for i, (src, peer) in enumerate(((tx_x, here.x_peer), (tx_y, here.y_peer)))
        ]

    def stage_far(layer, chunk, i):
        lo, size = CHUNKS[chunk]
        return pltpu.make_async_copy(
            far_rx.at[layer, i, :, pl.ds(lo, size)], stage.at[i, pl.ds(0, half), pl.ds(0, size)], stage_sem.at[i])

    def stage_near(layer, chunk, i):
        lo, size = CHUNKS[chunk]
        return pltpu.make_async_copy(
            near_rx.at[layer, i, :, pl.ds(lo, size)], stage.at[i, :, pl.ds(0, size)], stage_sem.at[i])

    def step_one(layer, chunk):
        claim(("far", chunk % 2))

        def put(cols, value):
            tx_far[chunk % 2, :, cols] = value.astype(BF16)

        products(layer, chunk, here.far_shard, put)
        moves = far_moves(layer, chunk)
        for move in moves:
            move.start()
        pending["far", chunk % 2] = moves

    def step_two(layer, chunk):
        arrivals = far_moves(layer, chunk)
        for i in (1, 0):
            arrivals[i].wait_recv()
            stage_far(layer, chunk, i).start()
        claim(("near", chunk % 2))
        moves = near_moves(layer, chunk)

        def put_x(cols, value):
            tx_x[chunk % 2, :half, cols] = value[:half].astype(BF16)
            tx_x[chunk % 2, half:, cols] = (value[half:] + stage[1, :half, cols].astype(F32)).astype(BF16)

        def put_y(cols, value):
            tx_y[chunk % 2, :half, cols] = (value[:half] + stage[0, :half, cols].astype(F32)).astype(BF16)
            tx_y[chunk % 2, half:, cols] = value[half:].astype(BF16)

        stage_far(layer, chunk, 1).wait()
        products(layer, chunk, here.x_shard, put_x)
        moves[0].start()
        stage_far(layer, chunk, 0).wait()
        products(layer, chunk, here.y_shard, put_y)
        moves[1].start()
        pending["near", chunk % 2] = moves

    piece = part // (replicas * LINE)

    def fin_moves(layer, chunk):
        lo, size = CHUNKS[chunk]
        head = place * CORES + core
        moves = []
        for rep in range(replicas):
            for where in range(LINE):
                src = tx_fin.at[chunk % 2, pl.ds((rep * LINE + where) * piece, piece), pl.ds(0, size)]
                dst = fin.at[head, pl.ds(rep * piece, piece), pl.ds(lo, size)]
                same = (core == layer) & (place == where)
                move = remote(src, dst, fin_send.at[layer, chunk, rep, where], fin_recv.at[rep, head, chunk],
                              {"section": layer, "dp": base + where})
                stay = pltpu.make_async_copy(src, dst, fin_send.at[layer, chunk, rep, where])
                moves.append((same, move, stay))
        return moves

    class Leave:
        def __init__(self, entry):
            self.same, self.move, self.stay = entry

        def start(self):
            @pl.when(self.same)
            def _():
                self.stay.start()

            @pl.when(jnp.logical_not(self.same))
            def _():
                self.move.start()

        def wait_send(self):
            @pl.when(self.same)
            def _():
                self.stay.wait()

            @pl.when(jnp.logical_not(self.same))
            def _():
                self.move.wait_send()

    def step_three(layer, chunk):
        arrivals = near_moves(layer, chunk)
        for i in range(2):
            arrivals[i].wait_recv()
            stage_near(layer, chunk, i).start()
        claim(("fin", chunk % 2))
        stage_near(layer, chunk, 0).wait()
        stage_near(layer, chunk, 1).wait()

        def put(cols, value):
            tx_fin[chunk % 2, :, cols] = (
                value + stage[0, :, cols].astype(F32) + stage[1, :, cols].astype(F32)
            ).astype(BF16)

        products(layer, chunk, shard, put)
        moves = [Leave(entry) for entry in fin_moves(layer, chunk)]
        for move in moves:
            move.start()
        pending["fin", chunk % 2] = moves

    def steps(*todo):
        def run():
            for kind, layer, chunk in todo:
                (step_one, step_two, step_three)[kind - 1](layer, chunk)
                if layer == 1 and kind == 3 and chunk == 1:
                    load("hn", 0).start()
                if layer == 1 and kind == 3 and chunk == 2:
                    load("hid", 0).start()
                if layer == 1 and kind == 3 and chunk == 3:
                    load("xn", 0).start()
        return run

    reduce_bufs = (sib_buf, rx_up, rx_dn, tx_up, tx_dn)

    def own_block(ref, layer):
        return ref.at[layer, pl.ds(pl.multiple_of((core * LINE + place) * SLOT, SLOT), SLOT), :]

    def terms(whose, src, weights, cols, dst):
        rows = pl.ds(pl.multiple_of(whose * half_rows, half_rows), half_rows)

        def tile(n, _):
            at = pl.ds(pl.multiple_of(n * 512, 512), 512)
            dst[:, at] = dot_last(src[rows, :], weights[at, cols]).astype(dst.dtype)
            return 0

        lax.fori_loop(0, width // 512, tile, 0)

    def reduce(slot, src, weights, cols, meanwhile):
        res_load(slot).start()
        terms(1 - core, src, weights, cols, theirs)
        line_reduce(here, total, ours, theirs, reduce_bufs, reduce_sems,
                    lambda: terms(core, src, weights, cols, ours), meanwhile)

    def res_load(slot):
        return pltpu.make_async_copy(res_in.at[slot], res, res_sem.at[slot])

    def norm_back(gain_row, slot):
        res_load(slot).wait()
        values = res[...]
        scale = root(values)
        grad = total[...]
        hat = grad * gain_row
        gain_loc[slot:slot + 1, :] = jnp.sum(grad * values * scale, 0, keepdims=True)
        inner = jnp.mean(hat * values, -1, keepdims=True)
        return scale * hat - values * (scale * scale * scale * inner)

    def layer_back(layer, grad_out, jobs):
        own_block(dm, layer)[...] = grad_out.astype(BF16)
        line_gather(here, dm.at[layer], gather_sems, jobs[0])
        need("wd", layer)
        tiles = FF_SLAB // 256
        for tile in range(tiles):
            at = slice(tile * 256, tile * 256 + 256)
            at_up = slice(FF_SLAB + tile * 256, FF_SLAB + tile * 256 + 256)
            grad = dot(dm[layer], wd[:, at])
            for copy in gu_loads(layer, tile):
                copy.wait()
            gate, up = gu[tile % 2, :, :256], gu[tile % 2, :, 256:]
            sig = jax.nn.sigmoid(gate)
            dgu[layer, :, at] = (grad * up * sig * (1.0 + gate * (1.0 - sig))).astype(BF16)
            dgu[layer, :, at_up] = (grad * gate * sig).astype(BF16)
            ahead = (layer, tile + 2) if tile + 2 < tiles else (layer - 1, tile + 2 - tiles)
            if ahead[0] >= 0:
                for copy in gu_loads(*ahead):
                    copy.start()
        need("wg", layer)
        if layer == 1:
            load("wd", 0).start()
        reduce(2 * layer + 1, dgu.at[layer], wg, slice(None), jobs[1])
        if layer == 1:
            load("wg", 0).start()
        grad_mid = grad_out + norm_back(gain[layer, 1:2], 2 * layer + 1)
        own_block(da, layer)[...] = grad_mid.astype(BF16)
        line_gather(here, da.at[layer], gather_sems, jobs[2])
        need("wa", layer)
        need("qkv", layer)
        need("ctx", layer)

        def attend(pair, _):
            at = pl.ds(pl.multiple_of(pair * 2 * SLOT, 2 * SLOT), 2 * SLOT)
            grad_ctx = dot(da[layer, at, :], wa[:, AO_AT:A_COLS]).astype(BF16).astype(F32)
            kv = qkv[layer, at, KV_AT:AO_AT]
            q = spread_heads(qkv[layer, at, :Q_SLAB].astype(F32)).astype(BF16)
            probs = two_slot_probs(q, kv, lens, pair)
            grad_high = spread_heads_high(grad_ctx).astype(BF16)
            grad_probs = dot_last(grad_high, kv)
            inner = jnp.sum(grad_probs * probs, -1, keepdims=True)
            grad_scores = (probs * (grad_probs - inner)).astype(BF16)
            grad_q = join_heads(dot(grad_scores, kv), False) * HEAD_DIM**-0.5
            grad_kv = dot_rows(grad_scores, q) * HEAD_DIM**-0.5 + dot_rows(probs.astype(BF16), grad_high)
            for i in range(GROUP // 2):
                cols = slice(128 * i, 128 * (i + 1))
                dqkv[layer, at, cols] = turn(grad_q[:, cols], tables[0], -tables[1]).astype(BF16)
            dqkv[layer, at, KV_AT:AO_AT] = turn(grad_kv, tables[2], -tables[3]).astype(BF16)
            return 0

        lax.fori_loop(0, LINE, attend, 0)
        reduce(2 * layer, dqkv.at[layer], wa, slice(0, AO_AT), jobs[3])
        if layer == 1:
            load("wa", 0).start()
            load("qkv", 0).start()
            load("ctx", 0).start()
        return grad_mid + norm_back(gain[layer, 0:1], 2 * layer)

    own_len = lens[pl.ds(pl.multiple_of((core * LINE + place) * 8, 8), 8), :][:1]
    live = lax.broadcasted_iota(jnp.int32, (SLOT, 128), 0).astype(F32) < own_len
    valid = jnp.where(live, 1.0, 0.0)[:, :1]
    dx1 = layer_back(1, cot_in[...].astype(F32) * valid, (
        (),
        (steps((1, 1, 0)), steps((1, 1, 1)), steps((1, 1, 2))),
        (steps((2, 1, 0)), None, steps((2, 1, 1))),
        (steps((2, 1, 2)), steps((1, 1, 3)), steps((3, 1, 0))),
    ))
    dx0 = layer_back(0, dx1.astype(BF16).astype(F32), (
        (steps((2, 1, 3)), steps((3, 1, 1)), None),
        (steps((1, 0, 0)), steps((3, 1, 2)), steps((1, 0, 1))),
        (steps((1, 0, 2)), steps((2, 0, 0), (3, 1, 3)), steps((2, 0, 1))),
        (steps((2, 0, 2)), steps((1, 0, 3)), steps((3, 0, 0))),
    ))

    first = core == 0
    dx0 = dx0.astype(BF16).astype(F32)
    y1 = y_in[...].astype(F32)
    end_tx[...] = jnp.where(first, y1, dx0).astype(BF16)
    end_move = remote(end_tx, end_rx, misc_send.at[0], misc_recv.at[0], here.twin)
    end_move.start()

    gain_x_move = remote(gain_loc, gain_x, misc_send.at[1], misc_recv.at[1], here.x_peer)
    gain_x_move.start()
    steps((2, 0, 3))()
    gain_x_move.wait()
    gain_loc[...] += gain_x[...]
    gain_y_move = remote(gain_loc, gain_y, misc_send.at[2], misc_recv.at[2], here.y_peer)
    gain_y_move.start()
    steps((3, 0, 1))()
    gain_y_move.wait()
    cols = pl.ds(pl.multiple_of(shard * part, part), part)
    own_gains = pl.ds(pl.multiple_of((core * LINE + place) * 8, 8), 8)
    gain_line[own_gains, :] = gain_loc[:, cols] + gain_y[:, cols]
    line_gather(here, gain_line, gain_sems)
    gain_sum = gain_line[0:8, :]
    for i in range(1, LINE * CORES):
        gain_sum += gain_line[8 * i:8 * i + 8, :]
    gain_out[...] = gain_sum
    end_move.wait()
    crossed = end_rx[...].astype(F32)
    ends_out[:SLOT] = jnp.where(first, dx0, crossed).astype(BF16)
    ends_out[SLOT:] = jnp.where(first, crossed, y1).astype(BF16)
    steps((3, 0, 2))()
    steps((3, 0, 3))()
    for key in list(pending):
        claim(key)
    for rep in range(replicas):
        for where in range(LINE):
            for other in range(CORES):
                head = where * CORES + other

                @pl.when((core != other) | (place != where))
                def _():
                    for chunk, (lo, size) in enumerate(CHUNKS):
                        src = tx_fin.at[0, pl.ds(0, piece), pl.ds(0, size)]
                        dst = fin.at[head, pl.ds(rep * piece, piece), pl.ds(lo, size)]
                        remote(src, dst, fin_send.at[0, 0, 0, 0], fin_recv.at[rep, head, chunk], here.twin).wait_recv()


def backward_call(replicas, cot, y, gain, lens, tables, res, wa, wg, wd, xn, hn, qkv, ctx, gu, hid):
    width = cot.shape[1]
    rows = LINE * CORES * SLOT
    part = width // SHARDS
    hbm = pl.BlockSpec(memory_space=pl.ANY)
    vmem = pl.BlockSpec(memory_space=pltpu.VMEM)
    shape = jax.ShapeDtypeStruct
    dma = pltpu.SemaphoreType.DMA
    line = dma((LINE,))
    vm = pltpu.VMEM
    block = vm((LINE * SLOT, width), BF16)
    move = vm((2, part, FF_SLAB), BF16)
    return pl.pallas_call(
        functools.partial(backward_body, replicas),
        out_shape=[
            shape((KV_HEADS, part // LINE, SLAB), BF16),
            shape((CORES * SLOT, width), BF16),
            shape((8, part), F32),
            shape((2, 2, part // 2, SLAB), BF16),
            shape((2, 2, part, SLAB), BF16),
        ],
        in_specs=[vmem] * 5 + [hbm] * 10,
        out_specs=[hbm, vmem, vmem, hbm, hbm],
        scratch_shapes=[
            vm((width, A_COLS), BF16), vm((width, 2 * FF_SLAB), BF16), vm((width, FF_SLAB), BF16),
            vm((rows, width), BF16), vm((rows, width), BF16), vm((2, rows, AO_AT), BF16), vm((2, rows, Q_SLAB), BF16),
            vm((2, rows, 512), F32), vm((rows, FF_SLAB), BF16),
            vm((2, rows, width), BF16), vm((2, rows, width), BF16),
            vm((2, rows, 2 * FF_SLAB), BF16), vm((2, rows, AO_AT), BF16),
            block, vm((LINE * SLOT, width), F32), vm((SLOT, width), F32), vm((SLOT, width), F32),
            block, block, block, block, block,
            move, move, move, move, move,
            vm((8, width), F32), vm((8, width), F32), vm((8, width), F32), vm((8 * LINE * CORES, part), F32),
            vm((SLOT, width), BF16), vm((SLOT, width), BF16),
            dma((2, 8)), dma((2, 2)), dma((4,)), dma((2, 4, 2)), dma((2, 4, 2)), dma((2, 4, 2)), dma((2, 4, 2)),
            dma((2, 4, replicas, LINE)), dma((replicas, KV_HEADS, 4)), dma((2,)), dma((3,)), dma((3,)),
        ] + [line] * 16,
        compiler_params=pltpu.CompilerParams(
            collective_id=1, has_side_effects=True, vmem_limit_bytes=61 * 2**20
        ),
        name="backward_two_layers",
        cost_estimate=pl.CostEstimate(flops=32_000_000_000, bytes_accessed=600_000_000, transcendentals=0),
    )(cot, y, gain, lens, tables, res, wa, wg, wd, xn, hn, qkv, ctx, gu, hid)


def place_body(fin, in_out, out_out, held, wide_in, wide_out, load_sem, save_sem):
    steps = KV_HEADS // 2
    q_two, ff_two = 2 * Q_SLAB, 2 * FF_SLAB
    ff0 = Q_COLS + 2 * KV_COLS

    def fetch(step):
        return pltpu.make_async_copy(fin.at[pl.ds(2 * step, 2)], held.at[step % 2], load_sem.at[step % 2])

    def saves(step):
        slot = step % 2
        moves = []
        for i, (src, lo, dst, to, size) in enumerate((
            (wide_in, 0, in_out, step * q_two, q_two),
            (wide_in, q_two, in_out, Q_COLS + step * 128, 128),
            (wide_in, q_two + 128, in_out, Q_COLS + KV_COLS + step * 128, 128),
            (wide_in, q_two + 256, in_out, ff0 + step * ff_two, ff_two),
            (wide_in, q_two + 256 + ff_two, in_out, ff0 + FF + step * ff_two, ff_two),
            (wide_out, 0, out_out, step * q_two, q_two),
            (wide_out, q_two, out_out, Q_COLS + step * ff_two, ff_two),
        )):
            moves.append(pltpu.make_async_copy(
                src.at[slot, :, pl.ds(lo, size)], dst.at[:, pl.ds(to, size)], save_sem.at[slot, i]))
        return moves

    fetch(0).start()
    a_at = 3 * FF_SLAB
    for step in range(steps):
        slot = step % 2
        if step + 1 < steps:
            fetch(step + 1).start()
        fetch(step).wait()
        if step >= 2:
            for move in saves(step - 2):
                move.wait()
        for i in range(2):
            q_to = i * Q_SLAB
            wide_in[slot, :, q_to:q_to + Q_SLAB] = held[slot, i, :, a_at:a_at + Q_SLAB].astype(F32)
            wide_out[slot, :, q_to:q_to + Q_SLAB] = held[slot, i, :, a_at + AO_AT:a_at + A_COLS].astype(F32)
            for k, (src_ref, to) in enumerate(((wide_in, q_two + 256), (wide_in, q_two + 256 + ff_two), (wide_out, q_two))):
                at = to + i * FF_SLAB
                src_ref[slot, :, at:at + FF_SLAB] = held[slot, i, :, k * FF_SLAB:(k + 1) * FF_SLAB].astype(F32)
        one = held[slot, 0, :, a_at + KV_AT:a_at + AO_AT].astype(F32)
        two = held[slot, 1, :, a_at + KV_AT:a_at + AO_AT].astype(F32)
        low = low_lanes(one.shape)
        wide_in[slot, :, q_two:q_two + 128] = jnp.where(low, one, pltpu.roll(two, 64, 1))
        wide_in[slot, :, q_two + 128:q_two + 256] = jnp.where(low, pltpu.roll(one, 64, 1), two)
        for move in saves(step):
            move.start()
    for step in range(max(steps - 2, 0), steps):
        for move in saves(step):
            move.wait()


def place_call(fin, in_cols, out_cols):
    rows = fin.shape[1]
    hbm = pl.BlockSpec(memory_space=pl.ANY)
    q_two, ff_two = 2 * Q_SLAB, 2 * FF_SLAB
    return pl.pallas_call(
        place_body,
        out_shape=[jax.ShapeDtypeStruct((rows, in_cols), F32), jax.ShapeDtypeStruct((rows, out_cols), F32)],
        in_specs=[hbm],
        out_specs=[hbm, hbm],
        scratch_shapes=[
            pltpu.VMEM((2, 2, rows, SLAB), BF16),
            pltpu.VMEM((2, rows, q_two + 256 + 2 * ff_two), F32),
            pltpu.VMEM((2, rows, q_two + ff_two), F32),
            pltpu.SemaphoreType.DMA((2,)),
            pltpu.SemaphoreType.DMA((2, 7)),
        ],
        compiler_params=pltpu.CompilerParams(vmem_limit_bytes=32 * 2**20),
        name="place_columns",
    )(fin)


def rope_blocks():
    half_dim = HEAD_DIM // 2
    inverse = 500000.0 ** (-(jnp.arange(half_dim, dtype=F32) * 2.0 / HEAD_DIM))
    angles = jnp.arange(SLOT, dtype=F32)[:, None] * inverse[None, :]
    cos, sin = jnp.cos(angles), jnp.sin(angles)
    one, zero = jnp.ones((SLOT, HEAD_DIM), F32), jnp.zeros((SLOT, HEAD_DIM), F32)
    rows = [
        jnp.concatenate([cos] * 4, 1),
        jnp.concatenate([-sin, sin] * 2, 1),
        jnp.concatenate([cos, cos, one], 1),
        jnp.concatenate([-sin, sin, zero], 1),
    ]
    return jnp.stack([jnp.tile(block, (2, 1)) for block in rows])


def local(ends_in, in_weight, out_weight, norm_gain, seq_len):
    core = lax.axis_index("section")
    replicas = lax.axis_size("dp") // LINE
    own_length = jnp.where(core == 0, seq_len[0], seq_len[1])
    lens_block = jnp.full((8, 128), own_length.astype(F32))
    rope = rope_blocks()
    (wa, wg, wd, xn, hn, qkv, ctx, gu, hid, res, y1, cot, gains, lens) = forward_call(
        ends_in[0], lens_block, norm_gain[0], rope, in_weight[0], out_weight[0]
    )
    fin, ends_out, gain_sum, _, _ = backward_call(
        replicas, cot, y1, gains, lens, rope, res, wa, wg, wd, xn, hn, qkv, ctx, gu, hid
    )
    own_gain = lax.dynamic_slice_in_dim(gain_sum, 2 * core, 2, 0)
    if replicas > 1:
        groups = [[r * LINE + p for r in range(replicas)] for p in range(LINE)]
        fin = lax.psum_scatter(fin, "dp", scatter_dimension=1, tiled=True, axis_index_groups=groups)
        own_gain = lax.psum(own_gain, "dp", axis_index_groups=groups)
    in_grad, out_grad = place_call(fin, in_weight.shape[2], out_weight.shape[2])
    size = own_gain.shape[1] // lax.axis_size("dp")
    own_gain = lax.dynamic_slice_in_dim(own_gain, lax.axis_index("dp") * size, size, 1)
    return ends_out[None], in_grad[None], out_grad[None], own_gain[None]


def solution(mesh):
    in_specs = (
        P("section", ("shard", "dp"), None),
        P("section", "shard", None),
        P("section", "shard", None),
        P("section", None, None),
        P(("shard", "dp")),
    )
    out_specs = (
        P("section", ("shard", "dp"), None),
        P("section", ("shard", "dp"), None),
        P("section", ("shard", "dp"), None),
        P("section", None, ("shard", "dp")),
    )
    return jax.shard_map(local, mesh=mesh, in_specs=in_specs, out_specs=out_specs, check_vma=False)
```

time: 1260 us -> 752 us (0.60)
  waiting for transfers between devices: 297 us -> 0 us
  Pallas kernels: 573 us -> 730 us
  matrix products: 105 us -> 0 us
  local copies, waits for them, and re-layouts: 111 us -> 7.39 us
  other arithmetic: 82.3 us -> 0.99 us
  starting transfers between devices: 52.3 us -> 0 us
  between operations: 17.5 us -> 2.47 us
    ppermute x32 -> x0, waiting for transfers between devices: 297 us -> none  [the longest x16 195 us: hop(): return lax.ppermute(value, 'shard', [(i, i ^ bit) for i in range(peers)])]
    pallas_call x8 -> x2, Pallas kernels: 185 us -> 399 us  [the longest x1 393 us: backward_call(): pl.pallas_call(functools.partial(backward_body, replicas), out_shape=[sha...]
    dot_general x50 -> x0, matrix products: 105 us -> none  [the longest x32 57.8 us: mm_rows(): lax.dot_general(a, b, (((0,), (0,)), ((), ())), preferred_element_type=F32)]
    pallas_call x1, Pallas kernels: 388 us -> 331 us  [forward_call(): pl.pallas_call(forward_body, out_shape=[shape((2, width, A_COLS), BF16),...]
    ppermute x32 -> x0, starting transfers between devices: 52.3 us -> none  [the longest x12 39.6 us: line_exchange(): lax.ppermute(lax.dynamic_index_in_dim(blocks, to, 0, False), 'dp', line_p...]
    transpose x10 -> x0, local copies, waits for them, and re-layouts: 36.3 us -> none  [columns(): part = values[:, :, lo:hi].transpose(1, 0, 2)]
    unnamed x226 -> x5, local copies, waits for them, and re-layouts: 34.4 us -> 3.96 us
    another operation x20 -> x1, other arithmetic: 24.2 us -> 0.72 us  [rope_blocks(): return jnp.stack([jnp.tile(block, (2, 1)) for block in rows])]
  transfers between devices with their start and end apart: 33 -> 0, of which waited for: 13 -> 0; matrix products, arithmetic and copies ran while one was open for 12% -> 0% of each run, Pallas kernels for 0% -> 0%
where the time goes in v3:
time: 752 us; the launch traced here: 740 us
  Pallas kernels  730 us (97%)
    pallas_call x1, Pallas kernels, backward_call(): pl.pallas_call(functools.partial(backward_body, replicas), out_shape=[sha...  393 us
    pallas_call x1, Pallas kernels, forward_call(): pl.pallas_call(forward_body, out_shape=[shape((2, width, A_COLS), BF16),...  331 us

profile of v3, /device:TPU:20, one launch (start us, length us, event | category | flops | bytes accessed | tf_op | source)
XLA Modules:
  0.0 740.4 jit_solution(12648058168064336493)
XLA Ops:
  0.7 0.1 pad.9.clone
  0.7 0.1 pad.6.clone
  0.8 1.3 fusion.5
  3.4 0.6 broadcast_in_dim.23.lens_in
  4.0 0.1 fusion.3
  4.2 0.1 pad_maximum_fusion.1
  4.4 0.7 pad_maximum_fusion.tables
  5.1 330.6 %forward_two_layers.1 = (bf16[2,2048,640]{2,1,0:T(8,128)(2,1)}, bf16[2,2048,2048]{2,1,0:T(8,128)(2,1)}, bf16[2,2048,1024]{2,1,0:T(8,128)(2,1)}, bf16[2,512,2048]...) custom-call(bf16[128,2048]{1,0:T(8,128)(2,1)} %bitcast.24, ...), custom_call_target="tpu_custom_call" | custom-call | flops 16000000000 | bytes 600000000 | tf_op jit(solution)/shard_map/forward_two_layers/pallas_call | solution.py:559
  335.7 392.8 %backward_two_layers.1 = (bf16[8,128,3712]{2,1,0:T(8,128)(2,1)}, bf16[128,2048]{1,0:T(8,128)(2,1)}, f32[8,512]{1,0:T(8,128)}, bf16[2,2,256,3712]{3,2,1,0:T(8,128)(2,1)}, bf16[2,2,512,3712]{3,2,1,0:T(8,128)(2,1)}) custom-call(bf16[64,2048]{1,0:T(8,128)(2,1)} %get-tuple-element.23.cot_in, bf16[64,2048]{1,0:T(8,128)(2,1)} %get-tuple-element.24.y_in, ...), custom_call_target="tpu_custom_call" | custom-call | flops 32000000000 | bytes 600000000 | tf_op jit(solution)/shard_map/backward_two_layers/pallas_call | solution.py:1012
  728.6 1.3 dynamic-slice_bitcast_fusion
  729.9 0.0 copy-start
  729.9 3.2 copy-done
  733.1 0.0 copy-start.1
  733.1 6.1 place_columns.1
  739.1 0.0 copy-done.1
  739.2 0.8 copy.10
  (7 shorter events, 0.0 us)
Async XLA Ops:
  729.9 3.2 copy-start
  733.1 6.1 copy-start.1

commit v4 on v3

--- a/solution.py
+++ b/solution.py
@@ -19,6 +19,7 @@
 LINE = KV_HEADS // CORES
 SHARDS = 4
 SLOT = 64
+SUBS = 2
 Q_SLAB = GROUP * HEAD_DIM
 QKV_SLAB = Q_SLAB + 2 * HEAD_DIM
 FF_SLAB = FF // KV_HEADS
@@ -67,174 +68,199 @@
     return ref.at[pl.ds(pl.multiple_of(start, size), size)]
 
 
-def line_gather(here, buf, sems, meanwhile=()):
+def line_gather(here, buf, sems, meanwhile=(), subs=SUBS):
     up_send, dn_send, sib_send, z_recv, sib_recv = sems
     rows = buf.shape[0] // (LINE * CORES)
+    size = rows // subs
     core, place = here.core, here.place
-    meanwhile = list(meanwhile) + [None] * LINE
-
-    def part(where, whose):
-        return rows_at(buf, (whose * LINE + where) * rows, rows)
-
-    def up(where):
-        mine = part(where, core)
-        return remote(mine, mine, up_send.at[where], z_recv.at[where], here.above)
-
-    def down(where):
-        mine = part(where, core)
-        return remote(mine, mine, dn_send.at[where], z_recv.at[where], here.below)
-
-    def across(where, whose):
-        mine = part(where, whose)
-        return remote(mine, mine, sib_send.at[where], sib_recv.at[where], here.twin)
-
-    @pl.when(here.has_above)
-    def _():
-        up(place).start()
-
-    @pl.when(here.has_below)
-    def _():
-        down(place).start()
-
-    across(place, core).start()
+    meanwhile = list(meanwhile) + [None] * (LINE + 1)
+
+    def part(where, whose, sub):
+        return rows_at(buf, (whose * LINE + where) * rows + sub * size, size)
+
+    def up(where, sub):
+        mine = part(where, core, sub)
+        return remote(mine, mine, up_send.at[where, sub], z_recv.at[where, sub], here.above)
+
+    def down(where, sub):
+        mine = part(where, core, sub)
+        return remote(mine, mine, dn_send.at[where, sub], z_recv.at[where, sub], here.below)
+
+    def across(where, whose, sub):
+        mine = part(where, whose, sub)
+        return remote(mine, mine, sib_send.at[where, sub], sib_recv.at[where, sub], here.twin)
+
+    for sub in range(subs):
+        @pl.when(here.has_above)
+        def _():
+            up(place, sub).start()
+
+        @pl.when(here.has_below)
+        def _():
+            down(place, sub).start()
+
+    for sub in range(subs):
+        across(place, core, sub).start()
     for step in range(1, LINE):
         if meanwhile[step - 1] is not None:
             meanwhile[step - 1]()
-
-        @pl.when(place >= step)
-        def _():
-            up(place - step).wait_recv()
-
-            @pl.when(here.has_above)
-            def _():
-                up(place - step).start()
-
-            across(place - step, core).start()
-
-        @pl.when(place + step < LINE)
-        def _():
-            down(place + step).wait_recv()
-
-            @pl.when(here.has_below)
-            def _():
-                down(place + step).start()
-
-            across(place + step, core).start()
+        for sub in range(subs):
+            @pl.when(place >= step)
+            def _():
+                up(place - step, sub).wait_recv()
+
+                @pl.when(here.has_above)
+                def _():
+                    up(place - step, sub).start()
+
+                across(place - step, core, sub).start()
+
+            @pl.when(place + step < LINE)
+            def _():
+                down(place + step, sub).wait_recv()
+
+                @pl.when(here.has_below)
+                def _():
+                    down(place + step, sub).start()
+
+                across(place + step, core, sub).start()
 
     if meanwhile[LINE - 1] is not None:
         meanwhile[LINE - 1]()
     for where in range(LINE):
-        across(where, 1 - core).wait_recv()
-        across(where, core).wait_send()
-
-        @pl.when((where <= place) & here.has_above)
-        def _():
-            up(where).wait_send()
-
-        @pl.when((where >= place) & here.has_below)
-        def _():
-            down(where).wait_send()
-
-
-def line_reduce(here, out, ours, theirs, bufs, sems, own_terms=None, meanwhile=()):
+        for sub in range(subs):
+            across(where, 1 - core, sub).wait_recv()
+
+    for where in range(LINE):
+        for sub in range(subs):
+            across(where, core, sub).wait_send()
+
+            @pl.when((where <= place) & here.has_above)
+            def _():
+                up(where, sub).wait_send()
+
+            @pl.when((where >= place) & here.has_below)
+            def _():
+                down(where, sub).wait_send()
+
+
+def line_reduce(here, out, ours, theirs, bufs, sems, terms, meanwhile=()):
     sib_buf, rx_up, rx_dn, tx_up, tx_dn = bufs
     sib_send, sib_recv, up_send, up_recv, dn_send, dn_recv = sems
-    rows = out.shape[0]
-    place = here.place
-    meanwhile = list(meanwhile) + [None] * LINE
-
-    def part(ref, where):
-        return rows_at(ref, where * rows, rows)
-
-    def read(ref, where):
-        return ref[pl.ds(pl.multiple_of(where * rows, rows), rows), :].astype(F32)
-
-    def across(where):
-        return remote(part(theirs, where), part(sib_buf, where), sib_send.at[where], sib_recv.at[where], here.twin)
-
-    def up(where):
-        return remote(part(tx_up, where), part(rx_up, where), up_send.at[where], up_recv.at[where], here.above)
-
-    def down(where):
-        return remote(part(tx_dn, where), part(rx_dn, where), dn_send.at[where], dn_recv.at[where], here.below)
-
-    def summed(where):
-        return read(ours, where) + read(sib_buf, where)
-
-    def put(ref, where, value):
-        ref[pl.ds(pl.multiple_of(where * rows, rows), rows), :] = value.astype(BF16)
-
-    for step in range(LINE - 1, 0, -1):
-        @pl.when(place + step < LINE)
-        def _():
-            across(place + step).start()
-
-        @pl.when(place >= step)
-        def _():
-            across(place - step).start()
-
-    across(place).start()
-    if own_terms is not None:
-        own_terms()
-    for step in range(LINE - 1, 0, -1):
+    rows, width = out.shape
+    size = width // SUBS
+    place, core = here.place, here.core
+    meanwhile = list(meanwhile) + [None] * (LINE + 1)
+
+    def cols(sub):
+        return slice(sub * size, (sub + 1) * size)
+
+    def part(ref, where, sub):
+        return ref.at[pl.ds(pl.multiple_of(where * rows, rows), rows), pl.ds(sub * size, size)]
+
+    def read(ref, where, sub):
+        return ref[pl.ds(pl.multiple_of(where * rows, rows), rows), cols(sub)].astype(F32)
+
+    def across(where, sub):
+        return remote(part(theirs, where, sub), part(sib_buf, where, sub),
+                      sib_send.at[where, sub], sib_recv.at[where, sub], here.twin)
+
+    def up(where, sub):
+        return remote(part(tx_up, where, sub), part(rx_up, where, sub),
+                      up_send.at[where, sub], up_recv.at[where, sub], here.above)
+
+    def down(where, sub):
+        return remote(part(tx_dn, where, sub), part(rx_dn, where, sub),
+                      dn_send.at[where, sub], dn_recv.at[where, sub], here.below)
+
+    def summed(where, sub):
+        return read(ours, where, sub) + read(sib_buf, where, sub)
+
+    def put(ref, where, sub, value):
+        ref[pl.ds(pl.multiple_of(where * rows, rows), rows), cols(sub)] = value.astype(BF16)
+
+    def begin(sub):
+        terms(1 - core, theirs, sub)
+        for step in range(LINE - 1, 0, -1):
+            @pl.when(place + step < LINE)
+            def _():
+                across(place + step, sub).start()
+
+            @pl.when(place >= step)
+            def _():
+                across(place - step, sub).start()
+
+        across(place, sub).start()
+        terms(core, ours, sub)
+
+    def turn_on(step, sub):
         @pl.when(place + step < LINE)
         def _():
             where = place + step
-            across(where).wait_recv()
+            across(where, sub).wait_recv()
 
             @pl.when(here.has_below)
             def _():
-                up(where).wait_recv()
-                put(tx_up, where, summed(where) + read(rx_up, where))
+                up(where, sub).wait_recv()
+                put(tx_up, where, sub, summed(where, sub) + read(rx_up, where, sub))
 
             @pl.when(place == 0)
             def _():
-                put(tx_up, where, summed(where))
-
-            up(where).start()
+                put(tx_up, where, sub, summed(where, sub))
+
+            up(where, sub).start()
 
         @pl.when(place >= step)
         def _():
             where = place - step
-            across(where).wait_recv()
+            across(where, sub).wait_recv()
 
             @pl.when(here.has_above)
             def _():
-                down(where).wait_recv()
-                put(tx_dn, where, summed(where) + read(rx_dn, where))
+                down(where, sub).wait_recv()
+                put(tx_dn, where, sub, summed(where, sub) + read(rx_dn, where, sub))
 
             @pl.when(place == LINE - 1)
             def _():
-                put(tx_dn, where, summed(where))
-
-            down(where).start()
-
-        if meanwhile[LINE - 1 - step] is not None:
-            meanwhile[LINE - 1 - step]()
-
-    across(place).wait_recv()
-    out[...] = summed(place)
-
-    @pl.when(here.has_below)
-    def _():
-        up(place).wait_recv()
-        out[...] += read(rx_up, place)
-
-    @pl.when(here.has_above)
-    def _():
-        down(place).wait_recv()
-        out[...] += read(rx_dn, place)
+                put(tx_dn, where, sub, summed(where, sub))
+
+            down(where, sub).start()
+
+    for sub in range(SUBS):
+        begin(sub)
+        turn_on(LINE - 1, sub)
+    for step in range(LINE - 2, -1, -1):
+        if meanwhile[LINE - 2 - step] is not None:
+            meanwhile[LINE - 2 - step]()
+        if step > 0:
+            for sub in range(SUBS):
+                turn_on(step, sub)
+
+    for sub in range(SUBS):
+        across(place, sub).wait_recv()
+        out[:, cols(sub)] = summed(place, sub)
+
+        @pl.when(here.has_below)
+        def _():
+            up(place, sub).wait_recv()
+            out[:, cols(sub)] += read(rx_up, place, sub)
+
+        @pl.when(here.has_above)
+        def _():
+            down(place, sub).wait_recv()
+            out[:, cols(sub)] += read(rx_dn, place, sub)
 
     for where in range(LINE):
-        across(where).wait_send()
-
-        @pl.when(where > place)
-        def _():
-            up(where).wait_send()
-
-        @pl.when(where < place)
-        def _():
-            down(where).wait_send()
+        for sub in range(SUBS):
+            across(where, sub).wait_send()
+
+            @pl.when(where > place)
+            def _():
+                up(where, sub).wait_send()
+
+            @pl.when(where < place)
+            def _():
+                down(where, sub).wait_send()
 
 
 def dot(a, b):
@@ -419,7 +445,7 @@
 
     rows8 = lens_in.shape[0]
     lens[pl.ds(pl.multiple_of((core * LINE + place) * rows8, rows8), rows8), :] = lens_in[...]
-    line_gather(here, lens, len_sems)
+    line_gather(here, lens, len_sems, (), 1)
     cross_copy.wait()
     gain_copy.wait()
     first = core == 0
@@ -453,10 +479,11 @@
             x = y_out[...].astype(F32)
             res[2] = x
         own_block(seq)[...] = (x * root(x) * gain_out[index, 0:1]).astype(BF16)
-        line_gather(here, seq, gather_sems)
+        if index == 0:
+            line_gather(here, seq, gather_sems, (None, None, lambda: (hop_two(0, 0), hop_one(0, 1))))
+        else:
+            line_gather(here, seq, gather_sems, (None, lambda: hop_one(1, 2)))
         keep(seq, xn_out.at[index])
-        hop_two(index, 0)
-        hop_one(index, 1 if index == 0 else 2)
         all_in(index, 0)
         weight_out(index, 0).start()
 
@@ -477,34 +504,27 @@
         lax.fori_loop(0, LINE, attend, 0)
         keep(qkv, qkv_out.at[index])
         keep(ctx, ctx_out.at[index])
-        if index == 0:
-            hop_one(0, 2)
-
-        def terms(whose, src, weights, cols, dst):
-            rows = pl.ds(pl.multiple_of(whose * half_rows, half_rows), half_rows)
-
-            def tile(n, _):
-                at = pl.ds(pl.multiple_of(n * 512, 512), 512)
-                dst[:, at] = dot_last(src[rows, :], weights[index, at, cols]).astype(dst.dtype)
-                return 0
-
-            lax.fori_loop(0, width // 512, tile, 0)
-
-        def reduce(src, weights, cols):
-            terms(1 - core, src, weights, cols, theirs)
-            line_reduce(here, total, ours, theirs, reduce_bufs, reduce_sems,
-                        lambda: terms(core, src, weights, cols, ours))
+
+        def reduce(src, weights, cols, meanwhile):
+            def terms(whose, dst, sub):
+                rows = pl.ds(pl.multiple_of(whose * half_rows, half_rows), half_rows)
+                size = width // SUBS
+                for lo in range(sub * size, (sub + 1) * size, 512):
+                    at = slice(lo, lo + 512)
+                    dst[:, at] = dot_last(src[rows, :], weights[index, at, cols]).astype(dst.dtype)
+
+            line_reduce(here, total, ours, theirs, reduce_bufs, reduce_sems, terms, meanwhile)
 
         saves[0].wait()
-        reduce(ctx, wa, slice(AO_AT, A_COLS))
+        reduce(ctx, wa, slice(AO_AT, A_COLS), () if index == 0 else (None, None, lambda: hop_two(1, 1)))
         middle = x + total[...]
         res[1 + 2 * index] = middle
         own_block(hnb)[...] = (middle * root(middle) * gain_out[index, 1:2]).astype(BF16)
-        line_gather(here, hnb, gather_sems)
+        if index == 0:
+            line_gather(here, hnb, gather_sems, (None, lambda: hop_one(0, 2), None, lambda: hop_two(0, 1)))
+        else:
+            line_gather(here, hnb, gather_sems, (None, None, lambda: hop_two(1, 2)))
         keep(hnb, hn_out.at[index])
-        hop_two(index, 1)
-        if index == 0:
-            hop_one(1, 0)
         all_in(index, 1)
         weight_out(index, 1).start()
 
@@ -521,13 +541,14 @@
         lax.fori_loop(0, FF_SLAB // 256, gate_up, 0)
         keep(gu, gu_out.at[index])
         keep(hid, hid_out.at[index])
-        hop_two(index, 2)
         if index == 0:
+            hop_one(1, 0)
+            hop_two(0, 2)
             hop_one(1, 1)
         all_in(index, 2)
         weight_out(index, 2).start()
         saves[3].wait()
-        reduce(hid, wd, slice(None))
+        reduce(hid, wd, slice(None), (None, lambda: hop_two(1, 0)) if index == 0 else ())
         y_out[...] = (res[1 + 2 * index] + total[...]).astype(BF16)
         for i in (1, 2, 4, 5):
             saves[i].wait()
@@ -554,7 +575,7 @@
     vmem = pl.BlockSpec(memory_space=pltpu.VMEM)
     shape = jax.ShapeDtypeStruct
     dma = pltpu.SemaphoreType.DMA
-    line = dma((LINE,))
+    line = dma((LINE, SUBS))
     block = pltpu.VMEM((LINE * SLOT, width), BF16)
     return pl.pallas_call(
         forward_body,
@@ -849,21 +870,17 @@
     def own_block(ref, layer):
         return ref.at[layer, pl.ds(pl.multiple_of((core * LINE + place) * SLOT, SLOT), SLOT), :]
 
-    def terms(whose, src, weights, cols, dst):
-        rows = pl.ds(pl.multiple_of(whose * half_rows, half_rows), half_rows)
-
-        def tile(n, _):
-            at = pl.ds(pl.multiple_of(n * 512, 512), 512)
-            dst[:, at] = dot_last(src[rows, :], weights[at, cols]).astype(dst.dtype)
-            return 0
-
-        lax.fori_loop(0, width // 512, tile, 0)
-
     def reduce(slot, src, weights, cols, meanwhile):
         res_load(slot).start()
-        terms(1 - core, src, weights, cols, theirs)
-        line_reduce(here, total, ours, theirs, reduce_bufs, reduce_sems,
-                    lambda: terms(core, src, weights, cols, ours), meanwhile)
+
+        def terms(whose, dst, sub):
+            rows = pl.ds(pl.multiple_of(whose * half_rows, half_rows), half_rows)
+            size = width // SUBS
+            for lo in range(sub * size, (sub + 1) * size, 512):
+                at = slice(lo, lo + 512)
+                dst[:, at] = dot_last(src[rows, :], weights[at, cols]).astype(dst.dtype)
+
+        line_reduce(here, total, ours, theirs, reduce_bufs, reduce_sems, terms, meanwhile)
 
     def res_load(slot):
         return pltpu.make_async_copy(res_in.at[slot], res, res_sem.at[slot])
@@ -943,13 +960,13 @@
         (),
         (steps((1, 1, 0)), steps((1, 1, 1)), steps((1, 1, 2))),
         (steps((2, 1, 0)), None, steps((2, 1, 1))),
-        (steps((2, 1, 2)), steps((1, 1, 3)), steps((3, 1, 0))),
+        (steps((1, 1, 3)), steps((2, 1, 2)), steps((3, 1, 0))),
     ))
     dx0 = layer_back(0, dx1.astype(BF16).astype(F32), (
-        (steps((2, 1, 3)), steps((3, 1, 1)), None),
-        (steps((1, 0, 0)), steps((3, 1, 2)), steps((1, 0, 1))),
-        (steps((1, 0, 2)), steps((2, 0, 0), (3, 1, 3)), steps((2, 0, 1))),
-        (steps((2, 0, 2)), steps((1, 0, 3)), steps((3, 0, 0))),
+        (None, None, None, steps((3, 1, 1))),
+        (steps((1, 0, 0)), steps((1, 0, 1))),
+        (steps((2, 1, 3), (3, 1, 2)), None, steps((1, 0, 2), (2, 0, 0))),
+        (steps((2, 0, 1)), steps((3, 1, 3)), steps((1, 0, 3))),
     ))
 
     first = core == 0
@@ -961,7 +978,7 @@
 
     gain_x_move = remote(gain_loc, gain_x, misc_send.at[1], misc_recv.at[1], here.x_peer)
     gain_x_move.start()
-    steps((2, 0, 3))()
+    steps((2, 0, 2), (3, 0, 0))()
     gain_x_move.wait()
     gain_loc[...] += gain_x[...]
     gain_y_move = remote(gain_loc, gain_y, misc_send.at[2], misc_recv.at[2], here.y_peer)
@@ -971,7 +988,7 @@
     cols = pl.ds(pl.multiple_of(shard * part, part), part)
     own_gains = pl.ds(pl.multiple_of((core * LINE + place) * 8, 8), 8)
     gain_line[own_gains, :] = gain_loc[:, cols] + gain_y[:, cols]
-    line_gather(here, gain_line, gain_sems)
+    line_gather(here, gain_line, gain_sems, (), 1)
     gain_sum = gain_line[0:8, :]
     for i in range(1, LINE * CORES):
         gain_sum += gain_line[8 * i:8 * i + 8, :]
@@ -980,8 +997,7 @@
     crossed = end_rx[...].astype(F32)
     ends_out[:SLOT] = jnp.where(first, dx0, crossed).astype(BF16)
     ends_out[SLOT:] = jnp.where(first, crossed, y1).astype(BF16)
-    steps((3, 0, 2))()
-    steps((3, 0, 3))()
+    steps((2, 0, 3), (3, 0, 2), (3, 0, 3))()
     for key in list(pending):
         claim(key)
     for rep in range(replicas):
@@ -994,7 +1010,8 @@
                     for chunk, (lo, size) in enumerate(CHUNKS):
                         src = tx_fin.at[0, pl.ds(0, piece), pl.ds(0, size)]
                         dst = fin.at[head, pl.ds(rep * piece, piece), pl.ds(lo, size)]
-                        remote(src, dst, fin_send.at[0, 0, 0, 0], fin_recv.at[rep, head, chunk], here.twin).wait_recv()
+                        remote(src, dst, fin_send.at[0, 0, 0, 0], fin_recv.at[rep, head, chunk],
+                               {"section": 1 - core, "dp": base + where}).wait_recv()
 
 
 def backward_call(replicas, cot, y, gain, lens, tables, res, wa, wg, wd, xn, hn, qkv, ctx, gu, hid):
@@ -1005,7 +1022,7 @@
     vmem = pl.BlockSpec(memory_space=pltpu.VMEM)
     shape = jax.ShapeDtypeStruct
     dma = pltpu.SemaphoreType.DMA
-    line = dma((LINE,))
+    line = dma((LINE, SUBS))
     vm = pltpu.VMEM
     block = vm((LINE * SLOT, width), BF16)
     move = vm((2, part, FF_SLAB), BF16)

time: 752 us -> 674 us (0.90)
  Pallas kernels: 730 us -> 652 us
    pallas_call x1, Pallas kernels: 331 us -> 286 us  [forward_call(): pl.pallas_call(forward_body, out_shape=[shape((2, width, A_COLS), BF16),...]
    pallas_call x1, Pallas kernels: 393 us -> 360 us  [backward_call(): pl.pallas_call(functools.partial(backward_body, replicas), out_shape=[sha...]
where the time goes in v4:
time: 674 us; the launch traced here: 662 us
  Pallas kernels  652 us (97%)
  local copies, waits for them, and re-layouts  7.39 us (1%)
    pallas_call x1, Pallas kernels, backward_call(): pl.pallas_call(functools.partial(backward_body, replicas), out_shape=[sha...  360 us
    pallas_call x1, Pallas kernels, forward_call(): pl.pallas_call(forward_body, out_shape=[shape((2, width, A_COLS), BF16),...  286 us

profile of v4, /device:TPU:20, one launch (start us, length us, event | category | flops | bytes accessed | tf_op | source)
XLA Modules:
  0.0 662.5 jit_solution(8502399144660152606)
XLA Ops:
  0.7 0.1 pad.9.clone
  0.7 0.1 pad.6.clone
  0.8 1.3 fusion.5
  3.4 0.6 broadcast_in_dim.23.lens_in
  4.0 0.1 fusion.3
  4.2 0.1 pad_maximum_fusion.1
  4.4 0.7 pad_maximum_fusion.tables
  5.1 286.0 %forward_two_layers.1 = (bf16[2,2048,640]{2,1,0:T(8,128)(2,1)}, bf16[2,2048,2048]{2,1,0:T(8,128)(2,1)}, bf16[2,2048,1024]{2,1,0:T(8,128)(2,1)}, bf16[2,512,2048]...) custom-call(bf16[128,2048]{1,0:T(8,128)(2,1)} %bitcast.24, ...), custom_call_target="tpu_custom_call" | custom-call | flops 16000000000 | bytes 600000000 | tf_op jit(solution)/shard_map/forward_two_layers/pallas_call | solution.py:580
  291.0 359.6 %backward_two_layers.1 = (bf16[8,128,3712]{2,1,0:T(8,128)(2,1)}, bf16[128,2048]{1,0:T(8,128)(2,1)}, f32[8,512]{1,0:T(8,128)}, bf16[2,2,256,3712]{3,2,1,0:T(8,128)(2,1)}, bf16[2,2,512,3712]{3,2,1,0:T(8,128)(2,1)}) custom-call(bf16[64,2048]{1,0:T(8,128)(2,1)} %get-tuple-element.23.cot_in, bf16[64,2048]{1,0:T(8,128)(2,1)} %get-tuple-element.24.y_in, ...), custom_call_target="tpu_custom_call" | custom-call | flops 32000000000 | bytes 600000000 | tf_op jit(solution)/shard_map/backward_two_layers/pallas_call | solution.py:1029
  650.7 1.3 dynamic-slice_bitcast_fusion
  652.0 0.0 copy-start
  652.0 3.2 copy-done
  655.2 0.0 copy-start.1
  655.2 6.1 place_columns.1
  661.2 0.0 copy-done.1
  661.2 0.8 copy.10
  (7 shorter events, 0.0 us)
Async XLA Ops:
  652.0 3.2 copy-start
  655.2 6.1 copy-start.1

commit v5 on v4

--- a/solution.py
+++ b/solution.py
@@ -335,13 +335,13 @@
 
 def forward_body(
     ends, lens_in, gain_in, tables, w_in, w_out,
-    wa_out, wg_out, wd_out, xn_out, hn_out, qkv_out, ctx_out, gu_out, hid_out, res_out, y_out, cot_out, gain_out, lens,
-    cross, k_pair, v_pair, kv_mine, kv_twin, wa, wg, wd, seq, hnb, qkv, ctx, gu, hid, theirs, ours, res, total,
+    wa_out, wg_out, wd_out, xn_out, hn_out, qkv_out, ctx_out, gu_out, hid_out, res_out, dm_out, cot_out, gain_out, lens,
+    cross, k_pair, v_pair, kv_mine, kv_twin, wa, wg, wd, seq, hnb, qkv, ctx, gu, hid, theirs, ours, res, total, dm,
     sib_buf, rx_up, rx_dn, tx_up, tx_dn,
     loc_sem, push_send, push_recv, hop_send, hop_recv, misc, misc_send, misc_recv, save, w_save,
     *line_sems,
 ):
-    gather_sems, len_sems, reduce_sems = line_sems[:5], line_sems[5:10], line_sems[10:]
+    gather_sems, len_sems, dm_sems, reduce_sems = line_sems[:5], line_sems[5:10], line_sems[10:15], line_sems[15:]
     here = Here()
     core, shard, place = here.core, here.shard, here.place
     width = ends.shape[1]
@@ -452,7 +452,10 @@
     ours0, others0 = ends[:SLOT].astype(F32), ends[SLOT:].astype(F32)
     crossed = cross[...].astype(F32)
     x = jnp.where(first, ours0, crossed)
-    cot_out[...] = jnp.where(first, crossed, others0).astype(BF16)
+    own_len = lens[pl.ds(pl.multiple_of((core * LINE + place) * 8, 8), 8), :][:1]
+    live = lax.broadcasted_iota(jnp.int32, (SLOT, 128), 0).astype(F32) < own_len
+    valid = jnp.where(live, 1.0, 0.0)[:, :1]
+    cot_out[...] = (jnp.where(first, crossed, others0) * valid).astype(BF16)
     res[0] = x
 
     def own_block(ref):
@@ -473,11 +476,7 @@
             copy.start()
             saves.append(copy)
 
-        if index == 0:
-            x = res[0]
-        else:
-            x = y_out[...].astype(F32)
-            res[2] = x
+        x = res[2 * index]
         own_block(seq)[...] = (x * root(x) * gain_out[index, 0:1]).astype(BF16)
         if index == 0:
             line_gather(here, seq, gather_sems, (None, None, lambda: (hop_two(0, 0), hop_one(0, 1))))
@@ -522,6 +521,9 @@
         own_block(hnb)[...] = (middle * root(middle) * gain_out[index, 1:2]).astype(BF16)
         if index == 0:
             line_gather(here, hnb, gather_sems, (None, lambda: hop_one(0, 2), None, lambda: hop_two(0, 1)))
+            own_block(dm)[...] = cot_out[...]
+            line_gather(here, dm, dm_sems)
+            pltpu.make_async_copy(dm, dm_out, misc.at[0]).start()
         else:
             line_gather(here, hnb, gather_sems, (None, None, lambda: hop_two(1, 2)))
         keep(hnb, hn_out.at[index])
@@ -548,13 +550,15 @@
         all_in(index, 2)
         weight_out(index, 2).start()
         saves[3].wait()
-        reduce(hid, wd, slice(None), (None, lambda: hop_two(1, 0)) if index == 0 else ())
-        y_out[...] = (res[1 + 2 * index] + total[...]).astype(BF16)
+        if index == 0:
+            reduce(hid, wd, slice(None), (None, lambda: hop_two(1, 0)))
+            res[2] = (res[1] + total[...]).astype(BF16).astype(F32)
         for i in (1, 2, 4, 5):
             saves[i].wait()
 
     layer(0)
     layer(1)
+    pltpu.make_async_copy(dm, dm_out, misc.at[0]).wait()
     for i in range(4):
         pltpu.make_async_copy(res.at[i], res_out.at[i], misc.at[i]).start()
     for i in range(4):
@@ -590,13 +594,13 @@
             shape((2, rows, 2 * FF_SLAB), F32),
             shape((2, rows, FF_SLAB), BF16),
             shape((4, SLOT, width), F32),
-            shape((SLOT, width), BF16),
+            shape((rows, width), BF16),
             shape((SLOT, width), BF16),
             shape((2, 2, width), F32),
             shape((LINE * CORES * 8, 128), F32),
         ],
         in_specs=[vmem, vmem, vmem, vmem, hbm, hbm],
-        out_specs=[hbm] * 10 + [vmem] * 4,
+        out_specs=[hbm] * 11 + [vmem] * 3,
         scratch_shapes=[
             pltpu.VMEM((SLOT, width), BF16),
             pltpu.VMEM((w_in.shape[0], 128), BF16),
@@ -616,10 +620,11 @@
             pltpu.VMEM((LINE * SLOT, width), F32),
             pltpu.VMEM((4, SLOT, width), F32),
             pltpu.VMEM((SLOT, width), F32),
+            pltpu.VMEM((rows, width), BF16),
             block, block, block, block, block,
             dma((6,)), dma((6,)), dma((6,)), dma((2, 3, 4)), dma((2, 3, 4)),
             dma((4,)), dma((2,)), dma((2,)), dma((2, 6)), dma((2, 3)),
-        ] + [line] * 16,
+        ] + [line] * 21,
         compiler_params=pltpu.CompilerParams(
             collective_id=0, has_side_effects=True, vmem_limit_bytes=60 * 2**20
         ),
@@ -640,11 +645,13 @@
 
 CHUNKS = ((0, FF_SLAB), (FF_SLAB, FF_SLAB), (2 * FF_SLAB, FF_SLAB), (3 * FF_SLAB, A_COLS))
 SLAB = 3 * FF_SLAB + A_COLS
+FAR_SLOT = (1, 0, 0, 1)
+WINDOW, EACH = 16, 16
 
 
 def backward_body(
     replicas,
-    cot_in, y_in, gain, lens, tables, res_in, wa_in, wg_in, wd_in, xn_in, hn_in, qkv_in, ctx_in, gu_in, hid_in,
+    cot_in, gain, lens, tables, res_in, dm_in, wa_in, wg_in, wd_in, xn_in, hn_in, qkv_in, ctx_in, gu_in, hid_in,
     fin, ends_out, gain_out, far_rx, near_rx,
     wa, wg, wd, xn, hn, qkv, ctx, gu, hid, dm, da, dgu, dqkv, theirs, ours, total, res,
     sib_buf, rx_up, rx_dn, tx_up, tx_dn, tx_far, tx_x, tx_y, tx_fin, stage, gain_loc, gain_x, gain_y, gain_line,
@@ -672,7 +679,7 @@
 
     pl.semaphore_wait(barrier, 2 + CORES * LINE - 1)
 
-    NAMES = ("wd", "wg", "wa", "hid", "qkv", "ctx", "hn", "xn")
+    NAMES = ("dm", "wd", "wg", "wa", "hid", "qkv", "ctx", "hn", "xn")
     VIEWS = {
         "wd": (wd_in, lambda l: wd), "wg": (wg_in, lambda l: wg), "wa": (wa_in, lambda l: wa),
         "hid": (hid_in, lambda l: hid), "qkv": (qkv_in, lambda l: qkv.at[l]), "ctx": (ctx_in, lambda l: ctx.at[l]),
@@ -680,6 +687,8 @@
     }
 
     def load(name, layer):
+        if name == "dm":
+            return pltpu.make_async_copy(dm_in, dm.at[1], load_sem.at[1, 0])
         src, dst = VIEWS[name]
         return pltpu.make_async_copy(src.at[layer], dst(layer), load_sem.at[layer, NAMES.index(name)])
 
@@ -708,8 +717,19 @@
 
     pending = {}
 
+    waiting = []
+
+    def pump(count):
+        for _ in range(min(count, len(waiting))):
+            waiting.pop(0).start()
+
     def claim(key):
-        for move in pending.pop(key, ()):
+        moves = pending.pop(key, ())
+        for move in moves:
+            if move in waiting:
+                waiting.remove(move)
+                move.start()
+        for move in moves:
             move.wait_send()
 
     def products(layer, chunk, block, put):
@@ -731,7 +751,7 @@
 
     def far_moves(layer, chunk):
         lo, size = CHUNKS[chunk]
-        src = tx_far.at[chunk % 2]
+        src = tx_far.at[FAR_SLOT[chunk]]
         cols = pl.ds(0, size)
         return [
             remote(src.at[pl.ds(i * half, half), cols], far_rx.at[layer, i, :, pl.ds(lo, size)],
@@ -759,16 +779,16 @@
             near_rx.at[layer, i, :, pl.ds(lo, size)], stage.at[i, :, pl.ds(0, size)], stage_sem.at[i])
 
     def step_one(layer, chunk):
-        claim(("far", chunk % 2))
+        claim(("far", FAR_SLOT[chunk]))
 
         def put(cols, value):
-            tx_far[chunk % 2, :, cols] = value.astype(BF16)
+            tx_far[FAR_SLOT[chunk], :, cols] = value.astype(BF16)
 
         products(layer, chunk, here.far_shard, put)
         moves = far_moves(layer, chunk)
         for move in moves:
             move.start()
-        pending["far", chunk % 2] = moves
+        pending["far", FAR_SLOT[chunk]] = moves
 
     def step_two(layer, chunk):
         arrivals = far_moves(layer, chunk)
@@ -801,13 +821,14 @@
         head = place * CORES + core
         moves = []
         for rep in range(replicas):
-            for where in range(LINE):
-                src = tx_fin.at[chunk % 2, pl.ds((rep * LINE + where) * piece, piece), pl.ds(0, size)]
+            for turn_by in (2, 3, 1, 0):
+                where = lax.rem(place + turn_by, LINE)
+                src = tx_fin.at[chunk % 2, pl.ds(pl.multiple_of((rep * LINE + where) * piece, piece), piece), pl.ds(0, size)]
                 dst = fin.at[head, pl.ds(rep * piece, piece), pl.ds(lo, size)]
                 same = (core == layer) & (place == where)
-                move = remote(src, dst, fin_send.at[layer, chunk, rep, where], fin_recv.at[rep, head, chunk],
+                move = remote(src, dst, fin_send.at[layer, chunk, rep, turn_by], fin_recv.at[rep, head, chunk],
                               {"section": layer, "dp": base + where})
-                stay = pltpu.make_async_copy(src, dst, fin_send.at[layer, chunk, rep, where])
+                stay = pltpu.make_async_copy(src, dst, fin_send.at[layer, chunk, rep, turn_by])
                 moves.append((same, move, stay))
         return moves
 
@@ -849,18 +870,18 @@
 
         products(layer, chunk, shard, put)
         moves = [Leave(entry) for entry in fin_moves(layer, chunk)]
-        for move in moves:
-            move.start()
+        waiting.extend(moves)
+        if layer == 0:
+            pump(len(waiting))
         pending["fin", chunk % 2] = moves
 
     def steps(*todo):
         def run():
+            pump(EACH)
             for kind, layer, chunk in todo:
                 (step_one, step_two, step_three)[kind - 1](layer, chunk)
-                if layer == 1 and kind == 3 and chunk == 1:
+                if layer == 1 and kind == 3 and chunk == 0:
                     load("hn", 0).start()
-                if layer == 1 and kind == 3 and chunk == 2:
-                    load("hid", 0).start()
                 if layer == 1 and kind == 3 and chunk == 3:
                     load("xn", 0).start()
         return run
@@ -896,8 +917,13 @@
         return scale * hat - values * (scale * scale * scale * inner)
 
     def layer_back(layer, grad_out, jobs):
-        own_block(dm, layer)[...] = grad_out.astype(BF16)
-        line_gather(here, dm.at[layer], gather_sems, jobs[0])
+        if layer == 1:
+            need("dm", 1)
+        else:
+            own_block(dm, layer)[...] = grad_out.astype(BF16)
+            line_gather(here, dm.at[layer], gather_sems, jobs[0])
+        pump(WINDOW)
+        step_one(layer, 2)
         need("wd", layer)
         tiles = FF_SLAB // 256
         for tile in range(tiles):
@@ -914,15 +940,17 @@
             if ahead[0] >= 0:
                 for copy in gu_loads(*ahead):
                     copy.start()
-        need("wg", layer)
         if layer == 1:
             load("wd", 0).start()
+        step_one(layer, 0)
+        need("wg", layer)
         reduce(2 * layer + 1, dgu.at[layer], wg, slice(None), jobs[1])
         if layer == 1:
             load("wg", 0).start()
         grad_mid = grad_out + norm_back(gain[layer, 1:2], 2 * layer + 1)
         own_block(da, layer)[...] = grad_mid.astype(BF16)
         line_gather(here, da.at[layer], gather_sems, jobs[2])
+        pump(WINDOW)
         need("wa", layer)
         need("qkv", layer)
         need("ctx", layer)
@@ -953,37 +981,33 @@
             load("ctx", 0).start()
         return grad_mid + norm_back(gain[layer, 0:1], 2 * layer)
 
-    own_len = lens[pl.ds(pl.multiple_of((core * LINE + place) * 8, 8), 8), :][:1]
-    live = lax.broadcasted_iota(jnp.int32, (SLOT, 128), 0).astype(F32) < own_len
-    valid = jnp.where(live, 1.0, 0.0)[:, :1]
-    dx1 = layer_back(1, cot_in[...].astype(F32) * valid, (
+    dx1 = layer_back(1, cot_in[...].astype(F32), (
         (),
-        (steps((1, 1, 0)), steps((1, 1, 1)), steps((1, 1, 2))),
-        (steps((2, 1, 0)), None, steps((2, 1, 1))),
-        (steps((1, 1, 3)), steps((2, 1, 2)), steps((3, 1, 0))),
+        (steps((1, 1, 1)), steps((2, 1, 2))),
+        (None, steps((2, 1, 1))),
+        (steps((1, 1, 3), (2, 1, 0)), steps((3, 1, 2))),
     ))
+    load("hid", 0).start()
+
     dx0 = layer_back(0, dx1.astype(BF16).astype(F32), (
-        (None, None, None, steps((3, 1, 1))),
-        (steps((1, 0, 0)), steps((1, 0, 1))),
-        (steps((2, 1, 3), (3, 1, 2)), None, steps((1, 0, 2), (2, 0, 0))),
-        (steps((2, 0, 1)), steps((3, 1, 3)), steps((1, 0, 3))),
+        (steps((3, 1, 1)), None, steps((3, 1, 0), (2, 1, 3))),
+        (steps((3, 1, 3), (1, 0, 1)), steps((2, 0, 2))),
+        (None, steps((2, 0, 1))),
+        (steps((1, 0, 3), (2, 0, 0)), steps((3, 0, 2))),
     ))
 
-    first = core == 0
-    dx0 = dx0.astype(BF16).astype(F32)
-    y1 = y_in[...].astype(F32)
-    end_tx[...] = jnp.where(first, y1, dx0).astype(BF16)
-    end_move = remote(end_tx, end_rx, misc_send.at[0], misc_recv.at[0], here.twin)
-    end_move.start()
-
+    again_wd = pltpu.make_async_copy(wd_in.at[1], wd, load_sem.at[1, NAMES.index("wd")])
+    again_hid = pltpu.make_async_copy(hid_in.at[1], hid, load_sem.at[1, NAMES.index("hid")])
+    again_wd.start()
+    again_hid.start()
     gain_x_move = remote(gain_loc, gain_x, misc_send.at[1], misc_recv.at[1], here.x_peer)
     gain_x_move.start()
-    steps((2, 0, 2), (3, 0, 0))()
+    steps((3, 0, 1))()
     gain_x_move.wait()
     gain_loc[...] += gain_x[...]
     gain_y_move = remote(gain_loc, gain_y, misc_send.at[2], misc_recv.at[2], here.y_peer)
     gain_y_move.start()
-    steps((3, 0, 1))()
+    steps((2, 0, 3))()
     gain_y_move.wait()
     cols = pl.ds(pl.multiple_of(shard * part, part), part)
     own_gains = pl.ds(pl.multiple_of((core * LINE + place) * 8, 8), 8)
@@ -993,11 +1017,23 @@
     for i in range(1, LINE * CORES):
         gain_sum += gain_line[8 * i:8 * i + 8, :]
     gain_out[...] = gain_sum
+
+    again_wd.wait()
+    again_hid.wait()
+    reduce(3, hid, wd, slice(None), (None, steps((3, 0, 0))))
+    res_load(3).wait()
+
+    first = core == 0
+    dx0 = dx0.astype(BF16).astype(F32)
+    y1 = (res[...] + total[...]).astype(BF16).astype(F32)
+    end_tx[...] = jnp.where(first, y1, dx0).astype(BF16)
+    end_move = remote(end_tx, end_rx, misc_send.at[0], misc_recv.at[0], here.twin)
+    end_move.start()
+    steps((3, 0, 3))()
     end_move.wait()
     crossed = end_rx[...].astype(F32)
     ends_out[:SLOT] = jnp.where(first, dx0, crossed).astype(BF16)
     ends_out[SLOT:] = jnp.where(first, crossed, y1).astype(BF16)
-    steps((2, 0, 3), (3, 0, 2), (3, 0, 3))()
     for key in list(pending):
         claim(key)
     for rep in range(replicas):
@@ -1014,7 +1050,7 @@
                                {"section": 1 - core, "dp": base + where}).wait_recv()
 
 
-def backward_call(replicas, cot, y, gain, lens, tables, res, wa, wg, wd, xn, hn, qkv, ctx, gu, hid):
+def backward_call(replicas, cot, gain, lens, tables, res, dm, wa, wg, wd, xn, hn, qkv, ctx, gu, hid):
     width = cot.shape[1]
     rows = LINE * CORES * SLOT
     part = width // SHARDS
@@ -1035,7 +1071,7 @@
             shape((2, 2, part // 2, SLAB), BF16),
             shape((2, 2, part, SLAB), BF16),
         ],
-        in_specs=[vmem] * 5 + [hbm] * 10,
+        in_specs=[vmem] * 4 + [hbm] * 11,
         out_specs=[hbm, vmem, vmem, hbm, hbm],
         scratch_shapes=[
             vm((width, A_COLS), BF16), vm((width, 2 * FF_SLAB), BF16), vm((width, FF_SLAB), BF16),
@@ -1048,7 +1084,7 @@
             move, move, move, move, move,
             vm((8, width), F32), vm((8, width), F32), vm((8, width), F32), vm((8 * LINE * CORES, part), F32),
             vm((SLOT, width), BF16), vm((SLOT, width), BF16),
-            dma((2, 8)), dma((2, 2)), dma((4,)), dma((2, 4, 2)), dma((2, 4, 2)), dma((2, 4, 2)), dma((2, 4, 2)),
+            dma((2, 9)), dma((2, 2)), dma((4,)), dma((2, 4, 2)), dma((2, 4, 2)), dma((2, 4, 2)), dma((2, 4, 2)),
             dma((2, 4, replicas, LINE)), dma((replicas, KV_HEADS, 4)), dma((2,)), dma((3,)), dma((3,)),
         ] + [line] * 16,
         compiler_params=pltpu.CompilerParams(
@@ -1056,7 +1092,7 @@
         ),
         name="backward_two_layers",
         cost_estimate=pl.CostEstimate(flops=32_000_000_000, bytes_accessed=600_000_000, transcendentals=0),
-    )(cot, y, gain, lens, tables, res, wa, wg, wd, xn, hn, qkv, ctx, gu, hid)
+    )(cot, gain, lens, tables, res, dm, wa, wg, wd, xn, hn, qkv, ctx, gu, hid)
 
 
 def place_body(fin, in_out, out_out, held, wide_in, wide_out, load_sem, save_sem):
@@ -1154,11 +1190,11 @@
     own_length = jnp.where(core == 0, seq_len[0], seq_len[1])
     lens_block = jnp.full((8, 128), own_length.astype(F32))
     rope = rope_blocks()
-    (wa, wg, wd, xn, hn, qkv, ctx, gu, hid, res, y1, cot, gains, lens) = forward_call(
+    (wa, wg, wd, xn, hn, qkv, ctx, gu, hid, res, dm, cot, gains, lens) = forward_call(
         ends_in[0], lens_block, norm_gain[0], rope, in_weight[0], out_weight[0]
     )
     fin, ends_out, gain_sum, _, _ = backward_call(
-        replicas, cot, y1, gains, lens, rope, res, wa, wg, wd, xn, hn, qkv, ctx, gu, hid
+        replicas, cot, gains, lens, rope, res, dm, wa, wg, wd, xn, hn, qkv, ctx, gu, hid
     )
     own_gain = lax.dynamic_slice_in_dim(gain_sum, 2 * core, 2, 0)
     if replicas > 1:

time: 674 us -> 646 us (0.958)
  Pallas kernels: 652 us -> 622 us
    pallas_call x1, Pallas kernels: 286 us -> 268 us  [forward_call(): pl.pallas_call(forward_body, out_shape=[shape((2, width, A_COLS), BF16),...]
    pallas_call x1, Pallas kernels: 360 us -> 348 us  [backward_call(): pl.pallas_call(functools.partial(backward_body, replicas), out_shape=[sha...]
where the time goes in v5:
time: 646 us; the launch traced here: 633 us
  Pallas kernels  622 us (96%)
  local copies, waits for them, and re-layouts  7.39 us (1%)
    pallas_call x1, Pallas kernels, backward_call(): pl.pallas_call(functools.partial(backward_body, replicas), out_shape=[sha...  348 us
    pallas_call x1, Pallas kernels, forward_call(): pl.pallas_call(forward_body, out_shape=[shape((2, width, A_COLS), BF16),...  268 us

profile of v5, /device:TPU:20, one launch (start us, length us, event | category | flops | bytes accessed | tf_op | source)
XLA Modules:
  0.0 633.0 jit_solution(16597240920228967953)
XLA Ops:
  0.7 0.1 pad.9.clone
  0.7 0.1 pad.6.clone
  0.8 1.3 fusion.5
  3.4 0.6 broadcast_in_dim.23.lens_in
  4.0 0.1 fusion.3
  4.2 0.1 pad_maximum_fusion.1
  4.4 0.7 pad_maximum_fusion.tables
  5.1 268.4 %forward_two_layers.1 = (bf16[2,2048,640]{2,1,0:T(8,128)(2,1)}, bf16[2,2048,2048]{2,1,0:T(8,128)(2,1)}, bf16[2,2048,1024]{2,1,0:T(8,128)(2,1)}, bf16[2,512,2048]...) custom-call(bf16[128,2048]{1,0:T(8,128)(2,1)} %bitcast.24, ...), custom_call_target="tpu_custom_call" | custom-call | flops 16000000000 | bytes 600000000 | tf_op jit(solution)/shard_map/forward_two_layers/pallas_call | solution.py:584
  273.5 347.7 %backward_two_layers.1 = (bf16[8,128,3712]{2,1,0:T(8,128)(2,1)}, bf16[128,2048]{1,0:T(8,128)(2,1)}, f32[8,512]{1,0:T(8,128)}, bf16[2,2,256,3712]{3,2,1,0:T(8,128)(2,1)}, bf16[2,2,512,3712]{3,2,1,0:T(8,128)(2,1)}) custom-call(bf16[64,2048]{1,0:T(8,128)(2,1)} %get-tuple-element.23.cot_in, f32[2,2,2048]{2,1,0:T(2,128)} %get-tuple-element.24.gain, ...), custom_call_target="tpu_custom_call" | custom-call | flops 32000000000 | bytes 600000000 | tf_op jit(solution)/shard_map/backward_two_layers/pallas_call | solution.py:1065
  621.2 1.3 dynamic-slice_bitcast_fusion
  622.5 0.0 copy-start
  622.5 3.2 copy-done
  625.7 0.0 copy-start.1
  625.7 6.1 place_columns.1
  631.8 0.0 copy-done.1
  631.8 0.8 copy.10
  (7 shorter events, 0.0 us)
Async XLA Ops:
  622.5 3.2 copy-start
  625.7 6.1 copy-start.1

commit v6 on v5

--- a/solution.py
+++ b/solution.py
@@ -144,13 +144,12 @@
                 down(where, sub).wait_send()
 
 
-def line_reduce(here, out, ours, theirs, bufs, sems, terms, meanwhile=()):
+def line_reduce_steps(here, out, ours, theirs, bufs, sems, terms):
     sib_buf, rx_up, rx_dn, tx_up, tx_dn = bufs
     sib_send, sib_recv, up_send, up_recv, dn_send, dn_recv = sems
     rows, width = out.shape
     size = width // SUBS
     place, core = here.place, here.core
-    meanwhile = list(meanwhile) + [None] * (LINE + 1)
 
     def cols(sub):
         return slice(sub * size, (sub + 1) * size)
@@ -230,8 +229,7 @@
         begin(sub)
         turn_on(LINE - 1, sub)
     for step in range(LINE - 2, -1, -1):
-        if meanwhile[LINE - 2 - step] is not None:
-            meanwhile[LINE - 2 - step]()
+        yield
         if step > 0:
             for sub in range(SUBS):
                 turn_on(step, sub)
@@ -261,6 +259,15 @@
             @pl.when(where < place)
             def _():
                 down(where, sub).wait_send()
+
+
+def line_reduce(here, out, ours, theirs, bufs, sems, terms, meanwhile=()):
+    jobs = list(meanwhile)
+    for _ in line_reduce_steps(here, out, ours, theirs, bufs, sems, terms):
+        if jobs:
+            job = jobs.pop(0)
+            if job is not None:
+                job()
 
 
 def dot(a, b):
@@ -653,13 +660,13 @@
     replicas,
     cot_in, gain, lens, tables, res_in, dm_in, wa_in, wg_in, wd_in, xn_in, hn_in, qkv_in, ctx_in, gu_in, hid_in,
     fin, ends_out, gain_out, far_rx, near_rx,
-    wa, wg, wd, xn, hn, qkv, ctx, gu, hid, dm, da, dgu, dqkv, theirs, ours, total, res,
+    wa, wg, wd, xn, hn, qkv, ctx, gu, hid, dm, da, dgu, dqkv, theirs, ours, total, res, y_total,
     sib_buf, rx_up, rx_dn, tx_up, tx_dn, tx_far, tx_x, tx_y, tx_fin, stage, gain_loc, gain_x, gain_y, gain_line,
     end_tx, end_rx,
     load_sem, gu_sem, res_sem, far_send, far_recv, near_send, near_recv, fin_send, fin_recv, stage_sem, misc_send, misc_recv,
     *line_sems,
 ):
-    gather_sems, gain_sems, reduce_sems = line_sems[:5], line_sems[5:10], line_sems[10:]
+    gather_sems, gain_sems, reduce_sems, y_sems = line_sems[:5], line_sems[5:10], line_sems[10:16], line_sems[16:]
     here = Here()
     core, shard, place = here.core, here.shard, here.place
     width = cot_in.shape[1]
@@ -700,10 +707,12 @@
             for i in range(2)
         ]
 
+    for name in ("dm", "hid", "wd"):
+        load(name, 1).start()
     for tile in range(2):
         for copy in gu_loads(1, tile):
             copy.start()
-    for name in NAMES:
+    for name in ("hn", "wg", "wa", "qkv", "ctx"):
         load(name, 1).start()
 
     ready = set()
@@ -891,17 +900,26 @@
     def own_block(ref, layer):
         return ref.at[layer, pl.ds(pl.multiple_of((core * LINE + place) * SLOT, SLOT), SLOT), :]
 
-    def reduce(slot, src, weights, cols, meanwhile):
-        res_load(slot).start()
-
+    def terms_of(src, weights, cols):
         def terms(whose, dst, sub):
             rows = pl.ds(pl.multiple_of(whose * half_rows, half_rows), half_rows)
             size = width // SUBS
             for lo in range(sub * size, (sub + 1) * size, 512):
                 at = slice(lo, lo + 512)
                 dst[:, at] = dot_last(src[rows, :], weights[at, cols]).astype(dst.dtype)
-
-        line_reduce(here, total, ours, theirs, reduce_bufs, reduce_sems, terms, meanwhile)
+        return terms
+
+    def reduce(slot, src, weights, cols, meanwhile):
+        res_load(slot).start()
+        line_reduce(here, total, ours, theirs, reduce_bufs, reduce_sems, terms_of(src, weights, cols), meanwhile)
+
+    lower, upper = pl.ds(0, half_rows), pl.ds(half_rows, half_rows)
+    y_bufs = (dm.at[0, lower], dm.at[0, upper], da.at[0, lower], da.at[0, upper], dgu.at[0, lower])
+    y_theirs, y_ours = dgu.at[0, upper], xn.at[lower]
+    y_steps = line_reduce_steps(here, y_total, y_ours, y_theirs, y_bufs, y_sems, terms_of(hid, wd, slice(None)))
+
+    def y_step():
+        next(y_steps, None)
 
     def res_load(slot):
         return pltpu.make_async_copy(res_in.at[slot], res, res_sem.at[slot])
@@ -940,13 +958,12 @@
             if ahead[0] >= 0:
                 for copy in gu_loads(*ahead):
                     copy.start()
-        if layer == 1:
-            load("wd", 0).start()
         step_one(layer, 0)
         need("wg", layer)
         reduce(2 * layer + 1, dgu.at[layer], wg, slice(None), jobs[1])
         if layer == 1:
             load("wg", 0).start()
+            load("wd", 0).start()
         grad_mid = grad_out + norm_back(gain[layer, 1:2], 2 * layer + 1)
         own_block(da, layer)[...] = grad_mid.astype(BF16)
         line_gather(here, da.at[layer], gather_sems, jobs[2])
@@ -983,12 +1000,11 @@
 
     dx1 = layer_back(1, cot_in[...].astype(F32), (
         (),
-        (steps((1, 1, 1)), steps((2, 1, 2))),
-        (None, steps((2, 1, 1))),
+        (lambda: (steps((1, 1, 1))(), y_step()), steps((2, 1, 2)), y_step),
+        (y_step, steps((2, 1, 1)), lambda: (y_step(), load("xn", 1).start())),
         (steps((1, 1, 3), (2, 1, 0)), steps((3, 1, 2))),
     ))
     load("hid", 0).start()
-
     dx0 = layer_back(0, dx1.astype(BF16).astype(F32), (
         (steps((3, 1, 1)), None, steps((3, 1, 0), (2, 1, 3))),
         (steps((3, 1, 3), (1, 0, 1)), steps((2, 0, 2))),
@@ -996,10 +1012,8 @@
         (steps((1, 0, 3), (2, 0, 0)), steps((3, 0, 2))),
     ))
 
-    again_wd = pltpu.make_async_copy(wd_in.at[1], wd, load_sem.at[1, NAMES.index("wd")])
-    again_hid = pltpu.make_async_copy(hid_in.at[1], hid, load_sem.at[1, NAMES.index("hid")])
-    again_wd.start()
-    again_hid.start()
+    res_load(3).start()
+
     gain_x_move = remote(gain_loc, gain_x, misc_send.at[1], misc_recv.at[1], here.x_peer)
     gain_x_move.start()
     steps((3, 0, 1))()
@@ -1018,22 +1032,20 @@
         gain_sum += gain_line[8 * i:8 * i + 8, :]
     gain_out[...] = gain_sum
 
-    again_wd.wait()
-    again_hid.wait()
-    reduce(3, hid, wd, slice(None), (None, steps((3, 0, 0))))
     res_load(3).wait()
 
     first = core == 0
     dx0 = dx0.astype(BF16).astype(F32)
-    y1 = (res[...] + total[...]).astype(BF16).astype(F32)
+    y1 = (res[...] + y_total[...]).astype(BF16).astype(F32)
     end_tx[...] = jnp.where(first, y1, dx0).astype(BF16)
     end_move = remote(end_tx, end_rx, misc_send.at[0], misc_recv.at[0], here.twin)
     end_move.start()
-    steps((3, 0, 3))()
+    steps((3, 0, 0))()
     end_move.wait()
     crossed = end_rx[...].astype(F32)
     ends_out[:SLOT] = jnp.where(first, dx0, crossed).astype(BF16)
     ends_out[SLOT:] = jnp.where(first, crossed, y1).astype(BF16)
+    steps((3, 0, 3))()
     for key in list(pending):
         claim(key)
     for rep in range(replicas):
@@ -1079,16 +1091,16 @@
             vm((2, rows, 512), F32), vm((rows, FF_SLAB), BF16),
             vm((2, rows, width), BF16), vm((2, rows, width), BF16),
             vm((2, rows, 2 * FF_SLAB), BF16), vm((2, rows, AO_AT), BF16),
-            block, vm((LINE * SLOT, width), F32), vm((SLOT, width), F32), vm((SLOT, width), F32),
+            block, vm((LINE * SLOT, width), F32), vm((SLOT, width), F32), vm((SLOT, width), F32), vm((SLOT, width), F32),
             block, block, block, block, block,
             move, move, move, move, move,
             vm((8, width), F32), vm((8, width), F32), vm((8, width), F32), vm((8 * LINE * CORES, part), F32),
             vm((SLOT, width), BF16), vm((SLOT, width), BF16),
             dma((2, 9)), dma((2, 2)), dma((4,)), dma((2, 4, 2)), dma((2, 4, 2)), dma((2, 4, 2)), dma((2, 4, 2)),
             dma((2, 4, replicas, LINE)), dma((replicas, KV_HEADS, 4)), dma((2,)), dma((3,)), dma((3,)),
-        ] + [line] * 16,
+        ] + [line] * 22,
         compiler_params=pltpu.CompilerParams(
-            collective_id=1, has_side_effects=True, vmem_limit_bytes=61 * 2**20
+            collective_id=1, has_side_effects=True, vmem_limit_bytes=62 * 2**20
         ),
         name="backward_two_layers",
         cost_estimate=pl.CostEstimate(flops=32_000_000_000, bytes_accessed=600_000_000, transcendentals=0),
@@ -1164,7 +1176,7 @@
             pltpu.SemaphoreType.DMA((2,)),
             pltpu.SemaphoreType.DMA((2, 7)),
         ],
-        compiler_params=pltpu.CompilerParams(vmem_limit_bytes=32 * 2**20),
+        compiler_params=pltpu.CompilerParams(vmem_limit_bytes=60 * 2**20),
         name="place_columns",
     )(fin)
 

time: 646 us -> 642 us (level); the launches traced: 633 us -> 640 us
  Pallas kernels: 622 us -> 632 us
    pallas_call x1, Pallas kernels: 348 us -> 355 us  [backward_call(): pl.pallas_call(functools.partial(backward_body, replicas), out_shape=[sha...]
where the time goes in v6:
time: 642 us; the launch traced here: 640 us
  Pallas kernels  632 us (98%)
    pallas_call x1, Pallas kernels, backward_call(): pl.pallas_call(functools.partial(backward_body, replicas), out_shape=[sha...  355 us
    pallas_call x1, Pallas kernels, forward_call(): pl.pallas_call(forward_body, out_shape=[shape((2, width, A_COLS), BF16),...  268 us

profile of v6, /device:TPU:20, one launch (start us, length us, event | category | flops | bytes accessed | tf_op | source)
XLA Modules:
  0.0 639.8 jit_solution(3343367123902903755)
XLA Ops:
  0.7 0.1 pad.9.clone
  0.7 0.1 pad.6.clone
  0.8 1.3 fusion.5
  3.4 0.6 broadcast_in_dim.23.lens_in
  4.0 0.1 fusion.3
  4.2 0.1 pad_maximum_fusion.1
  4.4 0.7 pad_maximum_fusion.tables
  5.1 268.4 %forward_two_layers.1 = (bf16[2,2048,640]{2,1,0:T(8,128)(2,1)}, bf16[2,2048,2048]{2,1,0:T(8,128)(2,1)}, bf16[2,2048,1024]{2,1,0:T(8,128)(2,1)}, bf16[2,512,2048]...) custom-call(bf16[128,2048]{1,0:T(8,128)(2,1)} %bitcast.24, ...), custom_call_target="tpu_custom_call" | custom-call | flops 16000000000 | bytes 600000000 | tf_op jit(solution)/shard_map/forward_two_layers/pallas_call | solution.py:591
  273.5 355.2 %backward_two_layers.1 = (bf16[8,128,3712]{2,1,0:T(8,128)(2,1)}, bf16[128,2048]{1,0:T(8,128)(2,1)}, f32[8,512]{1,0:T(8,128)}, bf16[2,2,256,3712]{3,2,1,0:T(8,128)(2,1)}, bf16[2,2,512,3712]{3,2,1,0:T(8,128)(2,1)}) custom-call(bf16[64,2048]{1,0:T(8,128)(2,1)} %get-tuple-element.23.cot_in, f32[2,2,2048]{2,1,0:T(2,128)} %get-tuple-element.24.gain, ...), custom_call_target="tpu_custom_call" | custom-call | flops 32000000000 | bytes 600000000 | tf_op jit(solution)/shard_map/backward_two_layers/pallas_call | solution.py:1077
  628.7 0.0 copy-start
  628.7 1.4 dynamic-slice_bitcast_fusion
  630.1 8.7 %place_columns.1 = (f32[128,19456]{1,0:T(8,128)}, f32[128,10240]{1,0:T(8,128)}) custom-call(bf16[8,128,3712]{2,1,0:T(8,128)(2,1)} %get-tuple-element.38.fin), custom_call_target="tpu_custom_call" | custom-call | tf_op jit(solution)/shard_map/place_columns/pallas_call | solution.py:1167
  638.8 0.0 copy-done
  638.8 0.8 copy.10
  (7 shorter events, 0.0 us)
Async XLA Ops:
  628.7 10.1 %copy-start = (bf16[128,2048]{1,0:T(8,128)(2,1)S(1)}, bf16[128,2048]{1,0:T(8,128)(2,1)}, u32[]{:S(2)}) copy-start(bf16[128,2048]{1,0:T(8,128)(2,1)} %get-tuple-element.37) | copy-start | bytes 1572868

commit v7 on v6

--- a/solution.py
+++ b/solution.py
@@ -1026,26 +1026,23 @@
     cols = pl.ds(pl.multiple_of(shard * part, part), part)
     own_gains = pl.ds(pl.multiple_of((core * LINE + place) * 8, 8), 8)
     gain_line[own_gains, :] = gain_loc[:, cols] + gain_y[:, cols]
-    line_gather(here, gain_line, gain_sems, (), 1)
-    gain_sum = gain_line[0:8, :]
-    for i in range(1, LINE * CORES):
-        gain_sum += gain_line[8 * i:8 * i + 8, :]
-    gain_out[...] = gain_sum
-
     res_load(3).wait()
-
     first = core == 0
     dx0 = dx0.astype(BF16).astype(F32)
     y1 = (res[...] + y_total[...]).astype(BF16).astype(F32)
     end_tx[...] = jnp.where(first, y1, dx0).astype(BF16)
     end_move = remote(end_tx, end_rx, misc_send.at[0], misc_recv.at[0], here.twin)
     end_move.start()
-    steps((3, 0, 0))()
+
+    line_gather(here, gain_line, gain_sems, (steps((3, 0, 0)), None, steps((3, 0, 3))), 1)
+    gain_sum = gain_line[0:8, :]
+    for i in range(1, LINE * CORES):
+        gain_sum += gain_line[8 * i:8 * i + 8, :]
+    gain_out[...] = gain_sum
     end_move.wait()
     crossed = end_rx[...].astype(F32)
     ends_out[:SLOT] = jnp.where(first, dx0, crossed).astype(BF16)
     ends_out[SLOT:] = jnp.where(first, crossed, y1).astype(BF16)
-    steps((3, 0, 3))()
     for key in list(pending):
         claim(key)
     for rep in range(replicas):

time: 642 us -> 640 us (level)
  no operation moved by 1% of the time
where the time goes in v7:
time: 640 us; the launch traced here: 638 us
  Pallas kernels  630 us (98%)
    pallas_call x1, Pallas kernels, backward_call(): pl.pallas_call(functools.partial(backward_body, replicas), out_shape=[sha...  353 us
    pallas_call x1, Pallas kernels, forward_call(): pl.pallas_call(forward_body, out_shape=[shape((2, width, A_COLS), BF16),...  268 us

profile of v7, /device:TPU:20, one launch (start us, length us, event | category | flops | bytes accessed | tf_op | source)
XLA Modules:
  0.0 637.8 jit_solution(1747124957412506932)
XLA Ops:
  0.7 0.1 pad.9.clone
  0.7 0.1 pad.6.clone
  0.8 1.3 fusion.5
  3.4 0.6 broadcast_in_dim.23.lens_in
  4.0 0.1 fusion.3
  4.2 0.1 pad_maximum_fusion.1
  4.4 0.7 pad_maximum_fusion.tables
  5.1 268.4 %forward_two_layers.1 = (bf16[2,2048,640]{2,1,0:T(8,128)(2,1)}, bf16[2,2048,2048]{2,1,0:T(8,128)(2,1)}, bf16[2,2048,1024]{2,1,0:T(8,128)(2,1)}, bf16[2,512,2048]...) custom-call(bf16[128,2048]{1,0:T(8,128)(2,1)} %bitcast.24, ...), custom_call_target="tpu_custom_call" | custom-call | flops 16000000000 | bytes 600000000 | tf_op jit(solution)/shard_map/forward_two_layers/pallas_call | solution.py:591
  273.5 353.2 %backward_two_layers.1 = (bf16[8,128,3712]{2,1,0:T(8,128)(2,1)}, bf16[128,2048]{1,0:T(8,128)(2,1)}, f32[8,512]{1,0:T(8,128)}, bf16[2,2,256,3712]{3,2,1,0:T(8,128)(2,1)}, bf16[2,2,512,3712]{3,2,1,0:T(8,128)(2,1)}) custom-call(bf16[64,2048]{1,0:T(8,128)(2,1)} %get-tuple-element.23.cot_in, f32[2,2,2048]{2,1,0:T(2,128)} %get-tuple-element.24.gain, ...), custom_call_target="tpu_custom_call" | custom-call | flops 32000000000 | bytes 600000000 | tf_op jit(solution)/shard_map/backward_two_layers/pallas_call | solution.py:1074
  626.7 0.0 copy-start
  626.7 1.4 dynamic-slice_bitcast_fusion
  628.1 8.7 %place_columns.1 = (f32[128,19456]{1,0:T(8,128)}, f32[128,10240]{1,0:T(8,128)}) custom-call(bf16[8,128,3712]{2,1,0:T(8,128)(2,1)} %get-tuple-element.38.fin), custom_call_target="tpu_custom_call" | custom-call | tf_op jit(solution)/shard_map/place_columns/pallas_call | solution.py:1164
  636.8 0.0 copy-done
  636.8 0.8 copy.10
  (7 shorter events, 0.0 us)
Async XLA Ops:
  626.7 10.1 %copy-start = (bf16[128,2048]{1,0:T(8,128)(2,1)S(1)}, bf16[128,2048]{1,0:T(8,128)(2,1)}, u32[]{:S(2)}) copy-start(bf16[128,2048]{1,0:T(8,128)(2,1)} %get-tuple-element.37) | copy-start | bytes 1572868
